TPU v7x, 256 devices: a whole 4x4x8 slice. The times are simulated.
256 devices in a mesh: aux: 16 (over z, core), grp: 16 (over x, y).
Axes of the slice: x: 4, y: 4, z: 8, core: 2. Of those that a mesh axis runs over, the one named last changes fastest.
Arguments:
- integrals: bfloat16 [1024, 512, 256], P('aux', 'grp'), may hold values from -2.5 to 2.5
- metric: bfloat16 [1024, 1024], replicated, may hold values from -0.1875 to 0.1875
- fock: bfloat16 [512, 512], replicated, may hold values from -2 to 0.5, as said below
- virt_energy: float32 [256], replicated, may hold values from 0.3 to 3
- send_orb: int32 [256, 16], P(('aux', 'grp')), may hold values from 0 to 1, as said below
- pair_orb: int32 [4096, 2], P(('aux', 'grp')), may hold values from 0 to 511, as said below
- send_pair: int32 [256, 16], P(('aux', 'grp')), may hold values from 0 to 15, as said below
- cpl_slot: int32 [4096, 4], P(('aux', 'grp')), may hold values from 0 to 15, as said below
- cpl_orb: int32 [4096, 4, 2], P(('aux', 'grp')), may hold values from 0 to 511
Outputs:
- amplitudes: float32 [4096, 256, 256], P(('aux', 'grp'))
Inputs may be any that keep to these rules, and one draw needn't show every extreme that they name: send_orb is below 2. `pair_orb`: the orbitals of the pairs owned by device (col, g) lie in column col: an orbital o of them has (o % 32) // 2 == col and o % 2 == send_orb[col * 16 + o // 32, g]. No pair is listed twice on a device. send_pair indexes the sending device's own pairs. `cpl_slot`: the entries of one pair are distinct. fock is symmetric with diagonal entries between -2 and -0.5.
All inputs are finite; a program needn't handle non-finite values.
Results may differ from a plain program's by a relative error of at most 0.0027.
Values may be sent and summed in bfloat16 or wider, within the bound.
No kernel may reach another device: no remote copies, remote signals or barrier semaphores. Data moves between devices by JAX's collectives and lax.ppermute only.
A program may use at most 128 MiB of HBM per device.

v0:
```python
import jax
import jax.numpy as jnp
from jax import lax
from jax.sharding import PartitionSpec as P

ITERS = 2


def on_device(
    integrals, metric, fock, virt_energy, send_orb, pair_orb, send_pair, cpl_slot, cpl_orb
):
    group_orbs = integrals.shape[1]
    n_grp = lax.axis_size("grp")
    block = lax.all_to_all(integrals, "aux", split_axis=1, concat_axis=0, tiled=True)
    rows, orbs, items = block.shape
    fit_flat = block.reshape(rows, orbs * items)
    fitted_part = jnp.dot(metric, fit_flat, preferred_element_type=jnp.float32)
    fitted = fitted_part.reshape(rows, orbs, items).astype(jnp.bfloat16)
    orb_dev = fitted.shape[1]
    orb_i = pair_orb[:, 0]
    orb_j = pair_orb[:, 1]
    pool = lax.all_gather(fitted, "grp", axis=1, tiled=True)
    idx_i = orb_i // group_orbs * orb_dev + orb_i % orb_dev
    idx_j = orb_j // group_orbs * orb_dev + orb_j % orb_dev
    left = jnp.take(pool, idx_i, axis=1)
    right = jnp.take(pool, idx_j, axis=1)
    kmat = jnp.einsum("qpa,qpb->pab", left, right, preferred_element_type=jnp.float32)
    diag_sum = fock[orb_i, orb_i].astype(jnp.float32) + fock[orb_j, orb_j].astype(jnp.float32)
    denom = (virt_energy[:, None] + virt_energy[None, :])[None, :, :] - diag_sum[:, None, None]
    k_orb = cpl_orb[:, :, 0]
    l_orb = cpl_orb[:, :, 1]
    first = (l_orb == orb_j[:, None]) & (k_orb != orb_i[:, None])
    second = (k_orb == orb_i[:, None]) & (l_orb != orb_j[:, None])
    f_ik = fock[orb_i[:, None], k_orb].astype(jnp.float32)
    f_jl = fock[orb_j[:, None], l_orb].astype(jnp.float32)
    weight = jnp.where(first, f_ik, 0.0) + jnp.where(second, f_jl, 0.0)
    onehot = cpl_slot[:, :, None] == jnp.arange(n_grp, dtype=jnp.int32)[None, None, :]
    mixing = jnp.sum(jnp.where(onehot, weight[:, :, None], 0.0), axis=1)
    amps = -(kmat / denom)
    for step in range(ITERS):
        rounded = amps.astype(jnp.bfloat16)
        sending = jnp.take(rounded, send_pair[0], axis=0)
        incoming = lax.all_to_all(sending, "grp", split_axis=0, concat_axis=0, tiled=True)
        flat = incoming.reshape(n_grp, -1).astype(jnp.float32)
        term = jnp.dot(mixing, flat, precision=lax.Precision.HIGHEST).reshape(amps.shape)
        resid = kmat + denom * amps - term
        amps = amps - resid / denom
    return amps


def solution(mesh):
    in_specs = (
        P("aux", "grp", None),
        P(),
        P(),
        P(),
        P(("aux", "grp"), None),
        P(("aux", "grp"), None),
        P(("aux", "grp"), None),
        P(("aux", "grp"), None),
        P(("aux", "grp"), None, None),
    )
    out_specs = P(("aux", "grp"), None, None)
    return jax.shard_map(
        on_device, mesh=mesh, in_specs=in_specs, out_specs=out_specs, check_vma=False
    )
```

profile of v0, /device:TPU:2, one launch (start us, length us, event | category | flops | bytes accessed | tf_op | source)
XLA Modules:
  0.0 300.9 jit_solution(8403146177767070503)
XLA Ops:
  6.5 2.0 copy.43
  8.5 35.6 %all_to_all.25 = bf16[64,32,256]{2,0,1:T(8,128)(2,1)S(1)} all-to-all(bf16[64,32,256]{2,0,1:T(8,128)(2,1)S(1)} %copy.43), channel_id=1, replica_groups=mesh['aux'=16,'grp'=16] {'aux'}, dimensions={1} | all-to-all | bytes 2097152 | tf_op jit(solution)/shard_map/all_to_all | solution.py:14
  44.1 1.1 copy.44
  45.2 1.2 copy.59
  46.4 2.3 copy.45
  48.7 3.5 %fusion.24 = bf16[1024,2,256]{2,0,1:T(8,128)(2,1)} fusion(bf16[2,256,1024]{2,1,0:T(8,128)(2,1)} %bitcast.83, bf16[1024,1024]{1,0:T(8,128)(2,1)S(1)} %copy-done), kind=kOutput, calls=%fused_computation.39 | convolution fusion | flops 1074266112 | bytes 4194304 | tf_op jit(solution)/shard_map/dot_general | solution.py:17
  53.0 0.7 gather_fusion.1
  53.9 113.4 %all-gather.2.cloned.1.call-done = bf16[1024,32,256]{2,0,1:T(8,128)(2,1)} async-done(((bf16[1024,2,256]{2,0,1:T(8,128)(2,1)}), bf16[1024,32,256]{2,0,1:T(8,128)(2,1)}) %all-gather.2.cloned.1.call-update) | async-done | bytes 16777232 | tf_op jit(solution)/shard_map/all_gather | solution.py:22
  167.3 10.5 %gather_fusion.4 = bf16[16,1024,256]{2,1,0:T(8,128)(2,1)} fusion(bf16[1024,32,256]{2,0,1:T(8,128)(2,1)} %all-gather.2.cloned.1.call-done, s32[1024]{0:T(1024)S(1)} %get-tuple-element.26), kind=kCustom, calls=%fused_computation.clone | custom fusion | bytes 16777280 | tf_op jit(solution)/shard_map/jit(_take)/gather | solution.py:25
  177.9 10.5 %gather_fusion.5 = bf16[16,1024,256]{2,1,0:T(8,128)(2,1)} fusion(bf16[1024,32,256]{2,0,1:T(8,128)(2,1)} %all-gather.2.cloned.1.call-done, s32[1024]{0:T(1024)S(1)} %get-tuple-element.25), kind=kCustom, calls=%fused_computation.2.clone | custom fusion | bytes 16777280 | tf_op jit(solution)/shard_map/jit(_take)/gather | solution.py:26
  188.4 12.0 %fusion.15 = (bf16[16,256,256]{2,1,0:T(8,128)(2,1)}, f32[16,256,256]{2,1,0:T(8,128)}) fusion(f32[16]{0:T(128)S(1)} %convert_add_fusion, f32[256,256]{1,0:T(8,128)S(1)} %broadcast_add_fusion, bf16[16,1024,256]{2,1,0:T(8,128)(2,1)} %gather_fusion.5, pred[16]{0:T(512)(128)(4,1)S(1)} %get-tuple-element.19, bf16[16,1024,256]{2,1,0:T(8,128)(2,1)} %gather_fusion.4, ...), kind=kOutput, calls=%fused_computation.28 | convolution fusion | flops 2160066560 | bytes 23330912 | tf_op jit(solution)/shard_map/qpa,qpb->pab/dot_general | solution.py:27
  200.4 2.3 gather_fusion.6
  202.7 1.6 broadcast_select_fusion.1
  204.3 5.8 %all-to-all-start.1 = ((bf16[16,256,256]{2,1,0:T(8,128)(2,1)}), bf16[16,256,256]{2,1,0:T(8,128)(2,1)S(1)}, u32[]{:S(2)}, u32[]{:S(2)}) async-start(bf16[16,256,256]{2,1,0:T(8,128)(2,1)} %broadcast_select_fusion.1), calls=%async_computation.1 | async-start | bytes 4194304 | tf_op jit(solution)/shard_map/all_to_all | solution.py:43
  210.4 0.9 gather_fusion.2
  211.5 0.9 gather_fusion.3
  212.8 24.4 %all-to-all-done.1 = bf16[16,256,256]{2,1,0:T(8,128)(2,1)S(1)} async-done(((bf16[16,256,256]{2,1,0:T(8,128)(2,1)}), bf16[16,256,256]{2,1,0:T(8,128)(2,1)S(1)}, u32[]{:S(2)}, u32[]{:S(2)}) %all-to-all-start.1) | async-done | bytes 2097184 | tf_op jit(solution)/shard_map/all_to_all | solution.py:43
  237.2 2.5 fusion.19
  239.7 1.9 copy-done.3
  241.6 5.9 %fusion.40 = bf16[16,256,256]{2,1,0:T(8,128)(2,1)} fusion(f32[16,256,256]{2,0,1:T(8,128)S(1)} %fusion.19, f32[16,256,256]{2,1,0:T(8,128)S(1)} %copy-done.5, f32[16]{0:T(128)S(1)} %convert_add_fusion, f32[256,256]{1,0:T(8,128)S(1)} %broadcast_add_fusion), kind=kLoop, calls=%fused_computation.89 | loop fusion | flops 9437184 | bytes 10747968 | tf_op jit(solution)/shard_map/convert_element_type | solution.py:41
  247.6 2.3 gather_fusion.7
  250.1 30.8 %all_to_all.26 = bf16[16,256,256]{2,1,0:T(8,128)(2,1)S(1)} all-to-all(bf16[16,256,256]{2,1,0:T(8,128)(2,1)S(1)} %broadcast_select_fusion), channel_id=1, replica_groups=mesh['aux'=16,'grp'=16] {'grp'}, dimensions={0} | all-to-all | bytes 4194304 | tf_op jit(solution)/shard_map/all_to_all | solution.py:43
  281.0 2.5 fusion.16
  283.5 10.6 %fusion.13 = f32[16,256,256]{2,1,0:T(8,128)} fusion(f32[16,256,256]{2,1,0:T(8,128)S(1)} %copy-done.6, f32[16,256,256]{2,0,1:T(8,128)S(1)} %fusion.16, f32[16]{0:T(128)S(1)} %convert_add_fusion, f32[256,256]{1,0:T(8,128)S(1)} %broadcast_add_fusion, f32[16,256,256]{2,0,1:T(8,128)S(1)} %copy-done.4), kind=kLoop, calls=%fused_computation.26 | loop fusion | flops 13631488 | bytes 17039424 | tf_op jit(solution)/shard_map/sub | solution.py:47
  (46 shorter events, 2.0 us)
Async XLA Ops:
  6.5 42.2 %copy-start = (bf16[1024,1024]{1,0:T(8,128)(2,1)S(1)}, bf16[1024,1024]{1,0:T(8,128)(2,1)}, u32[]{:S(2)}) copy-start(bf16[1024,1024]{1,0:T(8,128)(2,1)} %param.14) | copy-start | bytes 6291460
  6.5 160.8 %all-gather.2.cloned.1.call-start = ((), (), s32[]{:S(2)}) async-start(), calls=%async_computation.3 | async-start | bytes 17825792 | tf_op jit(solution)/shard_map/all_gather | solution.py:22
  48.7 3.6 %copy-start.9 = (s32[16,2]{0,1:T(2,128)S(1)}, s32[16,2]{0,1:T(2,128)}, u32[]{:S(2)}) copy-start(s32[16,2]{0,1:T(2,128)} %param.17) | copy-start | bytes 388
  48.7 3.6 %copy-start.2 = (bf16[512,512]{1,0:T(8,128)(2,1)S(1)}, bf16[512,512]{1,0:T(8,128)(2,1)}, u32[]{:S(2)}) copy-start(bf16[512,512]{1,0:T(8,128)(2,1)} %param.15) | copy-start | bytes 1572868
  48.7 5.0 %copy-start.11 = (s32[1,16]{1,0:T(1,128)S(1)}, s32[1,16]{1,0:T(1,128)}, u32[]{:S(2)}) copy-start(s32[1,16]{1,0:T(1,128)} %param.18) | copy-start | bytes 196
  48.7 5.1 %copy-start.7 = (f32[256]{0:T(256)S(1)}, f32[256]{0:T(256)}, u32[]{:S(2)}) copy-start(f32[256]{0:T(256)} %param.16) | copy-start | bytes 3076
  202.7 7.4 %copy-start.8 = (s32[16,4,2]{0,2,1:T(2,128)S(1)}, s32[16,4,2]{0,2,1:T(2,128)}, u32[]{:S(2)}) copy-start(s32[16,4,2]{0,2,1:T(2,128)} %param.20) | copy-start | bytes 1540
  204.3 32.9 %all-to-all-start.1 = ((bf16[16,256,256]{2,1,0:T(8,128)(2,1)}), bf16[16,256,256]{2,1,0:T(8,128)(2,1)S(1)}, u32[]{:S(2)}, u32[]{:S(2)}) async-start(bf16[16,256,256]{2,1,0:T(8,128)(2,1)} %broadcast_select_fusion.1), calls=%async_computation.1 | async-start | bytes 4194304 | tf_op jit(solution)/shard_map/all_to_all | solution.py:43
  210.4 2.3 copy-start.10
  237.2 4.4 %copy-start.5 = (f32[16,256,256]{2,1,0:T(8,128)S(1)}, f32[16,256,256]{2,1,0:T(8,128)}, u32[]{:S(2)}) copy-start(f32[16,256,256]{2,1,0:T(8,128)} %get-tuple-element.22) | copy-start | bytes 12582916
  239.7 1.9 copy-start.3
  250.1 33.3 %copy-start.6 = (f32[16,256,256]{2,1,0:T(8,128)S(1)}, f32[16,256,256]{2,1,0:T(8,128)}, u32[]{:S(2)}) copy-start(f32[16,256,256]{2,1,0:T(8,128)} %get-tuple-element.22) | copy-start | bytes 12582916
  281.0 2.5 copy-start.4
  283.5 10.6 %copy-start.1 = (bf16[1024,1024]{1,0:T(8,128)(2,1)S(1)}, bf16[1024,1024]{1,0:T(8,128)(2,1)}, u32[]{:S(2)}) copy-start(bf16[1024,1024]{1,0:T(8,128)(2,1)} %param.14) | copy-start | bytes 6291460
Sparse Core Ops, SparseCore 0:
  52.4 114.8 all-gather.1
where the time goes:
time: 303 us; the launch traced here: 301 us
  waiting for transfers between devices  138 us (46%)
  blocking collectives  66.5 us (22%)
  local copies, waits for them, and re-layouts  37.9 us (13%)
  matrix products  20.5 us (7%)
  other arithmetic  18.8 us (6%)
  between operations  13.6 us (4%)
  starting transfers between devices  5.77 us (2%)
    all_gather x1, waiting for transfers between devices, on_device(): pool = lax.all_gather(fitted, 'grp', axis=1, tiled=True)  113 us
    all_to_all x1, blocking collectives, on_device(): lax.all_to_all(integrals, 'aux', split_axis=1, concat_axis=0, tiled=True)  35.6 us
    all_to_all x1, blocking collectives, on_device(): lax.all_to_all(sending, 'grp', split_axis=0, concat_axis=0, tiled=True)  30.8 us
    all_to_all x1, waiting for transfers between devices, on_device(): lax.all_to_all(sending, 'grp', split_axis=0, concat_axis=0, tiled=True)  24.4 us
    dot_general x1, matrix products, on_device(): jnp.einsum('qpa,qpb->pab', left, right, preferred_element_type=jnp.float32)  12 us
    sub x1, other arithmetic, on_device(): amps = amps - resid / denom  10.6 us
    gather x1, local copies, waits for them, and re-layouts, on_device(): left = jnp.take(pool, idx_i, axis=1)  10.5 us
    gather x1, local copies, waits for them, and re-layouts, on_device(): right = jnp.take(pool, idx_j, axis=1)  10.5 us
  transfers between devices with their start and end apart: 2, of which 2 were waited for; matrix products, arithmetic and copies ran while one was open for 1% of the time, Pallas kernels for 0%

commit v1 on v0

v1 whole, which is shorter than its diff:
```python
import jax
import jax.numpy as jnp
from jax import lax
from jax.experimental import pallas as pl
from jax.experimental.pallas import tpu as pltpu
from jax.sharding import PartitionSpec as P

NT = (((1,), (1,)), ((), ()))


def recip(x):
    r = pl.reciprocal(x, approx=True)
    return r * (2.0 - x * r)


def pair_kernel(idx, slot, wts, dsum, pool, vrow, vcol, out, vsum, acc, amp):
    t = pl.program_id(0)

    @pl.when(t == 0)
    def _():
        vsum[...] = vrow[...] + vcol[...]

    def kmat(n):
        return lax.dot_general(
            pool[idx[n, 0]], pool[idx[n, 1]], NT, preferred_element_type=jnp.float32
        )

    @pl.when(t < 16)
    def _():
        acc[...] = -kmat(16 + t)

        def entry(e, carry):
            n = 4 * t + e

            @pl.when(wts[64 + n] != 0.0)
            def _():
                start = -(kmat(32 + n) * recip(vsum[...] - dsum[32 + n]))
                rounded = start.astype(jnp.bfloat16).astype(jnp.float32)
                acc[...] += wts[64 + n] * rounded

            return carry

        lax.fori_loop(0, 4, entry, 0)
        amp[t] = (acc[...] * recip(vsum[...] - dsum[16 + t])).astype(jnp.bfloat16)

    @pl.when(t >= 16)
    def _():
        p = t - 16
        total = -kmat(p)
        for e in range(4):
            total += wts[4 * p + e] * amp[slot[4 * p + e]].astype(jnp.float32)
        out[0] = total * recip(vsum[...] - dsum[p])


def local_orbital(orbital):
    return orbital // 32 * 2 + orbital % 2


def lookup(table, rows, cols):
    ids = jnp.arange(32, dtype=jnp.int32)
    pick = (rows[:, None, None] == ids[None, :, None]) & (
        cols[:, None, None] == ids[None, None, :]
    )
    return jnp.sum(jnp.where(pick, table[None], 0.0), axis=(1, 2))


def coupling(table, orb, cpl):
    i, j = orb[:, 0, None], orb[:, 1, None]
    k, l = cpl[:, :, 0], cpl[:, :, 1]
    first = (l == j) & (k != i)
    second = (k == i) & (l != j)
    rows = jnp.where(first, i, j) + jnp.zeros_like(k)
    cols = jnp.where(first, k, l)
    value = lookup(table, rows.reshape(-1), cols.reshape(-1)).reshape(k.shape)
    return jnp.where(first | second, value, 0.0).reshape(-1)


def on_device(
    integrals, metric, fock, virt_energy, send_orb, pair_orb, send_pair, cpl_slot, cpl_orb
):
    col = lax.axis_index("aux")
    grp = lax.axis_index("grp")
    orb = local_orbital(pair_orb)
    cpl = local_orbital(cpl_orb)
    meta = jnp.concatenate([orb.reshape(16, 2), cpl.reshape(16, 8)], axis=1)
    meta = jnp.concatenate([meta.reshape(1, 160), send_pair], axis=1)
    metas = lax.all_gather(meta, "grp", axis=0, tiled=True)
    chosen = jnp.sum(
        jnp.where(jnp.arange(16)[None, :] == grp, metas[:, 160:], 0), axis=1
    )
    pick = chosen[:, None, None] == jnp.arange(16, dtype=jnp.int32)[None, :, None]
    sent = jnp.sum(jnp.where(pick, metas[:, :160].reshape(16, 16, 10), 0), axis=1)
    orb_q, cpl_q = sent[:, :2], sent[:, 2:].reshape(16, 4, 2)

    local = jnp.arange(32, dtype=jnp.int32)
    whole = local // 2 * 32 + col * 2 + local % 2
    select = (whole[:, None] == jnp.arange(512)[None, :]).astype(jnp.bfloat16)
    fock_rows = jnp.dot(select, fock, preferred_element_type=jnp.float32)
    fock_col = lax.dot_general(
        fock_rows.astype(jnp.bfloat16), select, NT, preferred_element_type=jnp.float32
    )
    diag = jnp.sum(jnp.where(local[:, None] == local[None, :], fock_col, 0.0), axis=1)

    idx = jnp.concatenate([orb, orb_q, cpl_q.reshape(64, 2)], axis=0)
    at = idx[:, :, None] == local[None, None, :]
    dsum = jnp.sum(jnp.where(at, diag[None, None, :], 0.0), axis=2)
    dsum = dsum[:, 0] + dsum[:, 1]
    wts = jnp.concatenate([coupling(fock_col, orb, cpl), coupling(fock_col, orb_q, cpl_q)])

    rows = integrals.reshape(64, 16, 512).transpose(1, 0, 2)
    block = lax.all_to_all(rows, "aux", split_axis=0, concat_axis=0, tiled=True)
    fitted = lax.dot_general(
        block.reshape(1024, 512),
        metric,
        (((0,), (1,)), ((), ())),
        preferred_element_type=jnp.float32,
    ).astype(jnp.bfloat16)
    pool = lax.all_gather(fitted, "grp", axis=0, tiled=True).reshape(32, 256, 1024)

    smem = pl.BlockSpec(memory_space=pltpu.SMEM)
    vmem = pl.BlockSpec(memory_space=pltpu.VMEM)
    return pl.pallas_call(
        pair_kernel,
        grid=(32,),
        in_specs=[smem] * 4 + [vmem] * 3,
        out_specs=pl.BlockSpec((1, 256, 256), lambda t: (jnp.maximum(t - 16, 0), 0, 0)),
        out_shape=jax.ShapeDtypeStruct((16, 256, 256), jnp.float32),
        scratch_shapes=[
            pltpu.VMEM((256, 256), jnp.float32),
            pltpu.VMEM((256, 256), jnp.float32),
            pltpu.VMEM((16, 256, 256), jnp.bfloat16),
        ],
        compiler_params=pltpu.CompilerParams(vmem_limit_bytes=48 * 2**20),
    )(idx, cpl_slot.reshape(64), wts, dsum, pool, virt_energy[None, :], virt_energy[:, None])


def solution(mesh):
    in_specs = (
        P("aux", "grp", None),
        P(),
        P(),
        P(),
        P(("aux", "grp"), None),
        P(("aux", "grp"), None),
        P(("aux", "grp"), None),
        P(("aux", "grp"), None),
        P(("aux", "grp"), None, None),
    )
    out_specs = P(("aux", "grp"), None, None)
    return jax.shard_map(
        on_device, mesh=mesh, in_specs=in_specs, out_specs=out_specs, check_vma=False
    )
```

time: 303 us -> 212 us (0.70)
  the two profiles are of different devices: /device:TPU:2 before, /device:TPU:1 now
where the time goes in v1:
time: 212 us; the launch traced here: 211 us
  waiting for transfers between devices  89.9 us (42%)
  blocking collectives  57.3 us (27%)
  Pallas kernels  41.5 us (20%)
  between operations  13.6 us (6%)
  local copies, waits for them, and re-layouts  5.02 us (2%)
  matrix products  2.66 us (1%)
    all_gather x1, waiting for transfers between devices, on_device(): lax.all_gather(fitted, 'grp', axis=0, tiled=True).reshape(32, 256, 1024)  89.8 us
    pallas_call x1, Pallas kernels, on_device(): pl.pallas_call(pair_kernel, grid=(32,), in_specs=[smem] * 4 + [vmem] * 3,...  41.5 us
    all_to_all x1, blocking collectives, on_device(): block = lax.all_to_all(rows, 'aux', split_axis=0, concat_axis=0, tiled=True)  38.3 us
    all_gather x1, blocking collectives, on_device(): metas = lax.all_gather(meta, 'grp', axis=0, tiled=True)  18.9 us
  transfers between devices with their start and end apart: 1, of which 1 were waited for; matrix products, arithmetic and copies ran while one was open for 2% of the time, Pallas kernels for 0%

profile of v1, /device:TPU:1, one launch (start us, length us, event | category | flops | bytes accessed | tf_op | source)
XLA Modules:
  0.0 210.9 jit_solution(894267857908383715)
XLA Ops:
  6.5 1.6 reshape.312
  8.1 0.6 copy.91
  8.7 38.3 %all_to_all.5 = bf16[16,64,512]{2,1,0:T(8,128)(2,1)S(1)} all-to-all(bf16[16,64,512]{2,1,0:T(8,128)(2,1)S(1)} %copy.91), channel_id=1, replica_groups=mesh['aux'=16,'grp'=16] {'aux'}, dimensions={0} | all-to-all | bytes 2097152 | tf_op jit(solution)/shard_map/all_to_all | solution.py:111
  47.1 2.3 %convolution_convert_fusion = bf16[512,1024]{1,0:T(8,128)(2,1)} fusion(bf16[1024,512]{1,0:T(8,128)(2,1)S(1)} %bitcast.31, bf16[1024,1024]{1,0:T(8,128)(2,1)S(1)} %copy-done), kind=kOutput, calls=%fused_computation | convolution fusion | flops 1074266112 | bytes 4194304 | tf_op jit(solution)/shard_map/dot_general | solution.py:112
  49.9 18.9 %all-gather = s32[16,1,176]{2,1,0:T(1,128)S(1)} all-gather(s32[1,1,176]{2,1,0:T(1,128)S(1)} %add_bitcast_fusion), channel_id=1, replica_groups=mesh['aux'=16,'grp'=16] {'grp'}, dimensions={0}, use_global_device_ids=true | all-gather | bytes 11968 | tf_op jit(solution)/shard_map/all_gather | solution.py:87
  68.8 0.1 reshape.309
  68.9 0.2 fusion.6
  69.2 0.1 select_reduce_fusion.2
  69.6 0.1 squeeze.14
  69.8 0.1 squeeze.15
  69.9 0.2 slice_reduce_fusion.3
  70.2 0.1 eq.207
  70.3 0.1 ne.148
  70.5 0.1 reshape.310.slot
  70.6 0.4 select_reduce_fusion.4
  71.1 0.2 slice_reduce_fusion.1
  71.3 0.1 eq.221
  71.7 0.1 squeeze.17
  71.9 0.1 ne.157
  72.1 0.1 copy.92.vcol
  72.3 0.3 select_reduce_fusion.1
  72.6 0.1 select_reduce_fusion.3
  72.7 89.8 %all-gather.3.cloned.1.call-done = bf16[8192,1024]{1,0:T(8,128)(2,1)} async-done(((bf16[512,1024]{1,0:T(8,128)(2,1)}), bf16[8192,1024]{1,0:T(8,128)(2,1)}) %all-gather.3.cloned.1.call-update) | async-done | bytes 16777232 | tf_op jit(solution)/shard_map/all_gather | solution.py:118
  162.6 41.5 %shard_map.82 = f32[16,256,256]{2,1,0:T(8,128)} custom-call(s32[96,2]{1,0:T(8,128)S(1)} %pad_add_fusion.idx, s32[64]{0:T(128)S(1)} %reshape.310.slot, f32[128]{0:T(128)S(1)} %pad_maximum_fusion.wts, f32[96]{0:T(128)S(1)} %add_bitcast_fusion.1.dsum, bf16[32,256,1024]{2,1,0:T(8,128)(2,1)} %bitcast.29, f32[1,256]{1,0:T(1,128)S(1)} %bitcast.28, ...), custom_call_target="tpu_custom_call" | custom-call | tf_op jit(solution)/shard_map/pallas_call | solution.py:122
  (54 shorter events, 1.9 us)
Async XLA Ops:
  6.5 40.5 %copy-start = (bf16[1024,1024]{1,0:T(8,128)(2,1)S(1)}, bf16[1024,1024]{1,0:T(8,128)(2,1)}, u32[]{:S(2)}) copy-start(bf16[1024,1024]{1,0:T(8,128)(2,1)} %param.10) | copy-start | bytes 6291460
  6.5 156.0 %all-gather.3.cloned.1.call-start = ((), (), s32[]{:S(2)}) async-start(), calls=%async_computation.1 | async-start | bytes 17825792 | tf_op jit(solution)/shard_map/all_gather | solution.py:118
  47.0 2.4 %copy-start.4 = (s32[16,2]{0,1:T(2,128)S(1)}, s32[16,2]{0,1:T(2,128)}, u32[]{:S(2)}) copy-start(s32[16,2]{0,1:T(2,128)} %param.13) | copy-start | bytes 388
  47.0 2.6 %copy-start.2 = (s32[16,4,2]{0,2,1:T(2,128)S(1)}, s32[16,4,2]{0,2,1:T(2,128)}, u32[]{:S(2)}) copy-start(s32[16,4,2]{0,2,1:T(2,128)} %param.16) | copy-start | bytes 1540
  47.0 2.8 %copy-start.5 = (s32[1,16]{1,0:T(1,128)S(1)}, s32[1,16]{1,0:T(1,128)}, u32[]{:S(2)}) copy-start(s32[1,16]{1,0:T(1,128)} %param.14) | copy-start | bytes 196
  47.0 23.4 %copy-start.3 = (s32[16,4]{0,1:T(4,128)S(1)}, s32[16,4]{0,1:T(4,128)}, u32[]{:S(2)}) copy-start(s32[16,4]{0,1:T(4,128)} %param.15) | copy-start | bytes 772
  47.1 23.6 %copy-start.6 = (bf16[512,512]{1,0:T(8,128)(2,1)S(1)}, bf16[512,512]{1,0:T(8,128)(2,1)}, u32[]{:S(2)}) copy-start(bf16[512,512]{1,0:T(8,128)(2,1)} %param.11) | copy-start | bytes 1572868
  49.4 22.7 %copy-start.1 = (f32[256]{0:T(256)S(1)}, f32[256]{0:T(256)}, u32[]{:S(2)}) copy-start(f32[256]{0:T(256)} %param.12) | copy-start | bytes 3076
Sparse Core Ops, SparseCore 0:
  49.5 113.0 all-gather.2

commit v2 on v1

v2 whole, which is shorter than its diff:
```python
import jax
import jax.numpy as jnp
from jax import lax
from jax.experimental import pallas as pl
from jax.experimental.pallas import tpu as pltpu
from jax.sharding import PartitionSpec as P

NT = (((1,), (1,)), ((), ()))
MIB = 2**20
MASKS = ((4, 12, 1, 3), (12, 4, 3, 1), (1, 3, 4, 12), (3, 1, 12, 4))


def recip(x):
    r = pl.reciprocal(x, approx=True)
    return r * (2.0 - x * r)


def listed(wts, order):
    def entry(n, count):
        hit = wts[64 + n] != 0.0

        @pl.when(hit)
        def _():
            order[count] = n

        return count + hit.astype(jnp.int32)

    count = lax.fori_loop(0, 64, entry, 0)
    for k in range(4):

        @pl.when(count + k < 64)
        def _(k=k):
            order[count + k] = -1

    return (count + 3) // 4


def load(pieces, pool, sems):
    copies = []
    for q in range(4):
        for part in range(2):
            copies.append(
                pltpu.make_async_copy(
                    pieces[2 * q + part], pool.at[q, pl.ds(16 * part, 16)], sems.at[2 * q + part]
                )
            )
    for copy in copies:
        copy.start()
    for copy in copies:
        copy.wait()


def product(idx, pool, n):
    left = jnp.concatenate([pool[q, idx[q, n]] for q in range(4)], axis=1)
    right = jnp.concatenate([pool[q, idx[q, 96 + n]] for q in range(4)], axis=1)
    return lax.dot_general(left, right, NT, preferred_element_type=jnp.float32)


def first_kernel(idx, wts, *refs):
    pieces, sums, pool, acc, order, sems, out_sems = refs[:8], *refs[8:]
    fours = listed(wts, order)
    load(pieces, pool, sems)

    def out_copy(g):
        rows = pl.ds(4 * g, 4)
        return pltpu.make_async_copy(acc.at[rows], sums.at[rows], out_sems.at[g])

    def plain(g, carry):
        for u in range(4):
            acc[4 * g + u] = product(idx, pool, 4 * g + u)
        out_copy(g).start()
        return carry

    def coupled(g, carry):
        for u in range(4):
            acc[32 + 4 * g + u] = product(idx, pool, 32 + jnp.maximum(order[4 * g + u], 0))
        out_copy(8 + g).start()
        return carry

    def finish(g, carry):
        out_copy(g).wait()
        return carry

    lax.fori_loop(0, 8, plain, 0)
    lax.fori_loop(0, fours, coupled, 0)
    lax.fori_loop(0, 8 + fours, finish, 0)


def last_kernel(idx, wts, slot, dsum, vrow, vcol, *refs):
    pieces, sums, out, pool, acc, mixed, amp, vsum, order, sems, in_sems = refs[:8], *refs[8:]
    fours = listed(wts, order)

    def in_copy(g):
        rows = pl.ds(4 * g, 4)
        return pltpu.make_async_copy(sums.at[rows], acc.at[rows], in_sems.at[g])

    def out_copy(g):
        rows = pl.ds(4 * g, 4)
        return pltpu.make_async_copy(acc.at[rows], out.at[rows], in_sems.at[g])

    def begin(g, carry):
        in_copy(g).start()
        return carry

    def clear(s, carry):
        mixed[s] = jnp.zeros((256, 256), jnp.float32)
        return carry

    lax.fori_loop(8, 8 + fours, begin, 0)
    lax.fori_loop(0, 8, begin, 0)
    vsum[...] = vrow[...] + vcol[...]
    lax.fori_loop(0, 16, clear, 0)
    load(pieces, pool, sems)

    def coupled(g, carry):
        in_copy(8 + g).wait()
        for u in range(4):
            entry = order[4 * g + u]
            n = jnp.maximum(entry, 0)
            weight = jnp.where(entry >= 0, wts[64 + n], 0.0)
            kmat = acc[32 + 4 * g + u] + product(idx, pool, 32 + n)
            start = -(kmat * recip(vsum[...] - dsum[32 + n]))
            rounded = start.astype(jnp.bfloat16).astype(jnp.float32)
            mixed[n // 4] += weight * rounded
        return carry

    def received(g, carry):
        in_copy(4 + g).wait()
        for u in range(4):
            s = 4 * g + u
            kmat = acc[16 + s] + product(idx, pool, 16 + s)
            value = (mixed[s] - kmat) * recip(vsum[...] - dsum[16 + s])
            amp[s] = value.astype(jnp.bfloat16)
        return carry

    def own(g, carry):
        in_copy(g).wait()
        for u in range(4):
            p = 4 * g + u
            total = -(acc[p] + product(idx, pool, p))
            for e in range(4):
                total += wts[4 * p + e] * amp[slot[4 * p + e]].astype(jnp.float32)
            acc[p] = total * recip(vsum[...] - dsum[p])
        out_copy(g).start()
        return carry

    def finish(g, carry):
        out_copy(g).wait()
        return carry

    lax.fori_loop(0, fours, coupled, 0)
    lax.fori_loop(0, 4, received, 0)
    lax.fori_loop(0, 4, own, 0)
    lax.fori_loop(0, 4, finish, 0)


SMEM = pl.BlockSpec(memory_space=pltpu.SMEM)
VMEM = pl.BlockSpec(memory_space=pltpu.VMEM)
HBM = pl.BlockSpec(memory_space=pl.ANY)


def first_sums(idx, wts, pieces):
    return pl.pallas_call(
        first_kernel,
        in_specs=[SMEM] * 2 + [HBM] * 8,
        out_specs=HBM,
        out_shape=jax.ShapeDtypeStruct((96, 256, 256), jnp.float32),
        scratch_shapes=[
            pltpu.VMEM((4, 32, 256, 128), jnp.bfloat16),
            pltpu.VMEM((96, 256, 256), jnp.float32),
            pltpu.SMEM((68,), jnp.int32),
            pltpu.SemaphoreType.DMA((8,)),
            pltpu.SemaphoreType.DMA((24,)),
        ],
        compiler_params=pltpu.CompilerParams(vmem_limit_bytes=44 * MIB),
        cost_estimate=pl.CostEstimate(
            flops=96 * 2 * 256 * 256 * 512, bytes_accessed=32 * MIB, transcendentals=0
        ),
    )(idx, wts, *pieces)


def amplitudes(idx, wts, slot, dsum, virt, pieces, sums):
    return pl.pallas_call(
        last_kernel,
        in_specs=[SMEM] * 4 + [VMEM] * 2 + [HBM] * 9,
        out_specs=HBM,
        out_shape=jax.ShapeDtypeStruct((16, 256, 256), jnp.float32),
        scratch_shapes=[
            pltpu.VMEM((4, 32, 256, 128), jnp.bfloat16),
            pltpu.VMEM((96, 256, 256), jnp.float32),
            pltpu.VMEM((16, 256, 256), jnp.float32),
            pltpu.VMEM((16, 256, 256), jnp.bfloat16),
            pltpu.VMEM((256, 256), jnp.float32),
            pltpu.SMEM((68,), jnp.int32),
            pltpu.SemaphoreType.DMA((8,)),
            pltpu.SemaphoreType.DMA((24,)),
        ],
        compiler_params=pltpu.CompilerParams(vmem_limit_bytes=52 * MIB),
        cost_estimate=pl.CostEstimate(
            flops=96 * 2 * 256 * 256 * 512, bytes_accessed=36 * MIB, transcendentals=0
        ),
    )(idx, wts, slot, dsum, virt[None, :], virt[:, None], *pieces, sums)


def lookup(table, rows, cols):
    ids = jnp.arange(32, dtype=jnp.int32)
    pick = (rows[:, None, None] == ids[None, :, None]) & (
        cols[:, None, None] == ids[None, None, :]
    )
    return jnp.sum(jnp.where(pick, table[None], 0.0), axis=(1, 2))


def coupling(table, orb, cpl):
    i, j = orb[:, 0, None], orb[:, 1, None]
    k, l = cpl[:, :, 0], cpl[:, :, 1]
    first = (l == j) & (k != i)
    second = (k == i) & (l != j)
    rows = jnp.where(first, i, j) + jnp.zeros_like(k)
    cols = jnp.where(first, k, l)
    value = lookup(table, rows.reshape(-1), cols.reshape(-1)).reshape(k.shape)
    return jnp.where(first | second, value, 0.0).reshape(-1)


def arrival(masks):
    order = [0]
    for mask in masks:
        order = order + [o ^ mask for o in order]
    return order


def tables(metas, fock, orb, cpl):
    col = lax.axis_index("aux")
    grp = lax.axis_index("grp")
    chosen = jnp.sum(
        jnp.where(jnp.arange(16)[None, :] == grp, metas[:, 160:], 0), axis=1
    )
    pick = chosen[:, None, None] == jnp.arange(16, dtype=jnp.int32)[None, :, None]
    sent = jnp.sum(jnp.where(pick, metas[:, :160].reshape(16, 16, 10), 0), axis=1)
    orb_q, cpl_q = sent[:, :2], sent[:, 2:].reshape(16, 4, 2)

    local = jnp.arange(32, dtype=jnp.int32)
    whole = local // 2 * 32 + col * 2 + local % 2
    select = (whole[:, None] == jnp.arange(512)[None, :]).astype(jnp.bfloat16)
    fock_rows = jnp.dot(select, fock, preferred_element_type=jnp.float32)
    fock_col = lax.dot_general(
        fock_rows.astype(jnp.bfloat16), select, NT, preferred_element_type=jnp.float32
    )
    diag = jnp.sum(jnp.where(local[:, None] == local[None, :], fock_col, 0.0), axis=1)

    orbs = jnp.concatenate([orb, orb_q, cpl_q.reshape(64, 2)], axis=0)
    at = orbs[:, :, None] == local[None, None, :]
    dsum = jnp.sum(jnp.where(at, diag[None, None, :], 0.0), axis=2)
    dsum = dsum[:, 0] + dsum[:, 1]
    wts = jnp.concatenate([coupling(fock_col, orb, cpl), coupling(fock_col, orb_q, cpl_q)])

    flat = orbs.T.reshape(1, 192)
    offset = (flat // 2) ^ grp
    place = jnp.array([arrival(m) for m in MASKS], jnp.int32)
    found = offset[:, :, None] == place[:, None, :]
    spot = jnp.sum(jnp.where(found, jnp.arange(16, dtype=jnp.int32), 0), axis=2)
    return spot * 2 + flat % 2, wts, dsum


def swap(block, mask):
    return lax.ppermute(block, "grp", [(g, g ^ mask) for g in range(16)])


def on_device(
    integrals, metric, fock, virt_energy, send_orb, pair_orb, send_pair, cpl_slot, cpl_orb
):
    orb = pair_orb // 32 * 2 + pair_orb % 2
    cpl = cpl_orb // 32 * 2 + cpl_orb % 2
    meta = jnp.concatenate([orb, cpl.reshape(16, 8)], axis=1).reshape(1, 160)
    meta = jnp.concatenate([meta, send_pair], axis=1)
    metas = lax.all_gather(meta, "grp", axis=0, tiled=True)

    rows = integrals.reshape(64, 16, 512).transpose(1, 0, 2)
    rows, metas = lax.optimization_barrier((rows, metas))
    idx, wts, dsum = tables(metas, fock, orb, cpl)
    block = lax.all_to_all(rows, "aux", split_axis=0, concat_axis=0, tiled=True)
    fitted = lax.dot_general(
        block.reshape(1024, 512),
        metric,
        (((0,), (1,)), ((), ())),
        preferred_element_type=jnp.float32,
    ).astype(jnp.bfloat16)
    held = [
        jnp.stack([fitted[:, 256 * q + 128 * h : 256 * q + 128 * h + 128] for h in range(2)])[:, None]
        for q in range(4)
    ]
    for step in range(3):
        got = [swap(held[q], MASKS[q][step]) for q in range(4)]
        held = [jnp.concatenate([a, b], axis=1) for a, b in zip(held, got)]
        held = list(lax.optimization_barrier(tuple(held)))
    halves = []
    for h in range(2):
        sent = [block[h] for block in held]
        got = [swap(sent[q], MASKS[q][3]) for q in range(4)]
        halves.append([x.reshape(16, 256, 128) for pair in zip(sent, got) for x in pair])
    sums = first_sums(idx, wts, halves[0])
    return amplitudes(idx, wts, cpl_slot.reshape(64), dsum, virt_energy, halves[1], sums)


def solution(mesh):
    in_specs = (
        P("aux", "grp", None),
        P(),
        P(),
        P(),
        P(("aux", "grp"), None),
        P(("aux", "grp"), None),
        P(("aux", "grp"), None),
        P(("aux", "grp"), None),
        P(("aux", "grp"), None, None),
    )
    out_specs = P(("aux", "grp"), None, None)
    return jax.shard_map(
        on_device, mesh=mesh, in_specs=in_specs, out_specs=out_specs, check_vma=False
    )
```

time: 212 us -> 220 us (1.038)
  the two profiles are of different devices: /device:TPU:1 before, /device:TPU:2 now
where the time goes in v2:
time: 220 us; the launch traced here: 218 us
  waiting for transfers between devices  79.2 us (36%)
  Pallas kernels  42.1 us (19%)
  starting transfers between devices  37.3 us (17%)
  blocking collectives  23.3 us (11%)
  local copies, waits for them, and re-layouts  20.8 us (9%)
  other arithmetic  12.3 us (6%)
  matrix products  2.71 us (1%)
    ppermute x20, waiting for transfers between devices, swap(): return lax.ppermute(block, 'grp', [(g, g ^ mask) for g in range(16)])  55 us
    ppermute x20, starting transfers between devices, swap(): return lax.ppermute(block, 'grp', [(g, g ^ mask) for g in range(16)])  28.8 us
    pallas_call x1, Pallas kernels, amplitudes(): pl.pallas_call(last_kernel, in_specs=[SMEM] * 4 + [VMEM] * 2 + [HBM] * 9,...  27.1 us
    all_to_all x1, waiting for transfers between devices, on_device(): block = lax.all_to_all(rows, 'aux', split_axis=0, concat_axis=0, tiled=True)  24.2 us
    all_gather x1, blocking collectives, on_device(): metas = lax.all_gather(meta, 'grp', axis=0, tiled=True)  23.3 us
    pallas_call x1, Pallas kernels, first_sums(): pl.pallas_call(first_kernel, in_specs=[SMEM] * 2 + [HBM] * 8, out_specs=H...  14.9 us
    squeeze x4, local copies, waits for them, and re-layouts, on_device(): sent = [block[h] for block in held]  11.2 us
    concatenate x12, other arithmetic, on_device(): held = [jnp.concatenate([a, b], axis=1) for a, b in zip(held, got)]  8.94 us
  transfers between devices with their start and end apart: 21, of which 16 were waited for; matrix products, arithmetic and copies ran while one was open for 9% of the time, Pallas kernels for 7%

profile of v2, /device:TPU:2, one launch (start us, length us, event | category | flops | bytes accessed | tf_op | source)
XLA Modules:
  0.0 218.2 jit_solution(11561219784702524146)
XLA Ops:
  2.5 23.3 %all-gather = s32[16,1,176]{2,1,0:T(1,128)S(1)} all-gather(s32[1,1,176]{2,1,0:T(1,128)S(1)} %add_bitcast_fusion), channel_id=1, replica_groups=mesh['aux'=16,'grp'=16] {'grp'}, dimensions={0}, use_global_device_ids=true | all-gather | bytes 11968 | tf_op jit(solution)/shard_map/all_gather | solution.py:275
  28.7 8.6 %all-to-all-start = ((bf16[16,64,512]{2,1,0:T(8,128)(2,1)}), bf16[16,64,512]{2,1,0:T(8,128)(2,1)S(1)}, u32[]{:S(2)}, u32[]{:S(2)}) async-start(bf16[16,64,512]{2,1,0:T(8,128)(2,1)} %copy.77), calls=%async_computation | async-start | bytes 2097152 | tf_op jit(solution)/shard_map/all_to_all | solution.py:280
  39.8 24.2 %all-to-all-done = bf16[16,64,512]{2,1,0:T(8,128)(2,1)S(1)} async-done(((bf16[16,64,512]{2,1,0:T(8,128)(2,1)}), bf16[16,64,512]{2,1,0:T(8,128)(2,1)S(1)}, u32[]{:S(2)}, u32[]{:S(2)}) %all-to-all-start) | async-done | bytes 1048608 | tf_op jit(solution)/shard_map/all_to_all | solution.py:280
  68.5 2.1 collective-permute-start
  70.6 4.7 %collective-permute-done.3 = bf16[2,1,512,128]{3,2,0,1:T(8,128)(2,1)S(1)} collective-permute-done((bf16[2,1,512,128]{3,2,0,1:T(8,128)(2,1)S(1)}, bf16[2,1,512,128]{3,2,0,1:T(8,128)(2,1)S(1)}, u32[]{:S(2)}, u32[]{:S(2)}) %collective-permute-start.3) | collective-permute-done | bytes 262176 | tf_op jit(solution)/shard_map/ppermute | solution.py:265
  78.5 2.0 collective-permute-start.7
  82.9 2.1 collective-permute-start.5
  85.6 7.0 %collective-permute-done.7 = bf16[2,2,512,128]{3,2,0,1:T(8,128)(2,1)S(1)} collective-permute-done((bf16[2,2,512,128]{3,2,0,1:T(8,128)(2,1)S(1)}, bf16[2,2,512,128]{3,2,0,1:T(8,128)(2,1)S(1)}, u32[]{:S(2)}, u32[]{:S(2)}) %collective-permute-start.7) | collective-permute-done | bytes 524320 | tf_op jit(solution)/shard_map/ppermute | solution.py:265
  92.7 3.2 %collective-permute-done.6 = bf16[2,2,512,128]{3,2,0,1:T(8,128)(2,1)S(1)} collective-permute-done((bf16[2,2,512,128]{3,2,0,1:T(8,128)(2,1)S(1)}, bf16[2,2,512,128]{3,2,0,1:T(8,128)(2,1)S(1)}, u32[]{:S(2)}, u32[]{:S(2)}) %collective-permute-start.6) | collective-permute-done | bytes 524320 | tf_op jit(solution)/shard_map/ppermute | solution.py:265
  98.1 2.1 pad_maximum_fusion.4
  101.0 2.2 %collective-permute-start.10 = (bf16[2,4,512,128]{3,2,0,1:T(8,128)(2,1)S(1)}, bf16[2,4,512,128]{3,2,0,1:T(8,128)(2,1)}, u32[]{:S(2)}, u32[]{:S(2)}) collective-permute-start(bf16[2,4,512,128]{3,2,0,1:T(8,128)(2,1)S(1)} %pad_maximum_fusion.6), channel_id=1, source_target_pairs={{0,4},{1,5},{2,6},{3,7},{4,0},{5,1},{6,2},{7,3},{8,12},{9,13},{10,... | collective-permute-start | bytes 3145736 | tf_op jit(solution)/shard_map/ppermute | solution.py:265
  106.2 17.6 %collective-permute-done.11 = bf16[2,4,512,128]{3,2,0,1:T(8,128)(2,1)} collective-permute-done((bf16[2,4,512,128]{3,2,0,1:T(8,128)(2,1)S(1)}, bf16[2,4,512,128]{3,2,0,1:T(8,128)(2,1)}, u32[]{:S(2)}, u32[]{:S(2)}) %collective-permute-start.11) | collective-permute-done | bytes 1048608 | tf_op jit(solution)/shard_map/ppermute | solution.py:265
  123.7 2.7 %pad_maximum_fusion.3 = bf16[2,8,512,128]{3,2,0,1:T(8,128)(2,1)} fusion(bf16[2,4,512,128]{3,2,0,1:T(8,128)(2,1)} %collective-permute-done.11, bf16[2,4,512,128]{3,2,0,1:T(8,128)(2,1)S(1)} %pad_maximum_fusion.7), kind=kLoop, calls=%fused_computation.3 | loop fusion | flops 1048576 | bytes 4194304 | tf_op jit(solution)/shard_map/concatenate | solution.py:293
  129.3 2.3 %slice_bitcast_fusion.13 = (bf16[8,512,128]{2,1,0:T(8,128)(2,1)}, bf16[8,512,128]{2,1,0:T(8,128)(2,1)}, bf16[1,8,512,128]{3,2,0,1:T(8,128)(2,1)S(1)}, bf16[1,8,512,128]{3,2,0,1:T(8,128)(2,1)S(1)}) fusion(bf16[2,8,512,128]{3,2,0,1:T(8,128)(2,1)S(1)} %pad_maximum_fusion), kind=kLoop, calls=%fused_computation.97 | loop fusion | bytes 6291456 | tf_op jit(solution)/shard_map/squeeze | solution.py:297
  133.2 2.1 slice_bitcast_fusion.12
  135.3 2.5 %slice_bitcast_fusion.11 = (bf16[8,512,128]{2,1,0:T(8,128)(2,1)}, bf16[8,512,128]{2,1,0:T(8,128)(2,1)}, bf16[1,8,512,128]{3,2,0,1:T(8,128)(2,1)}, bf16[1,8,512,128]{3,2,0,1:T(8,128)(2,1)}) fusion(bf16[2,8,512,128]{3,2,0,1:T(8,128)(2,1)S(1)} %pad_maximum_fusion.2), kind=kLoop, calls=%fused_computation.95 | loop fusion | bytes 6291456 | tf_op jit(solution)/shard_map/squeeze | solution.py:297
  139.1 4.2 %slice_bitcast_fusion.10 = (bf16[8,512,128]{2,1,0:T(8,128)(2,1)}, bf16[8,512,128]{2,1,0:T(8,128)(2,1)}, bf16[1,8,512,128]{3,2,0,1:T(8,128)(2,1)}, bf16[1,8,512,128]{3,2,0,1:T(8,128)(2,1)}) fusion(bf16[2,8,512,128]{3,2,0,1:T(8,128)(2,1)} %pad_maximum_fusion.3), kind=kLoop, calls=%fused_computation.94 | loop fusion | bytes 6291456 | tf_op jit(solution)/shard_map/squeeze | solution.py:297
  143.3 3.6 %collective-permute-start.19 = (bf16[8,512,128]{2,1,0:T(8,128)(2,1)}, bf16[8,512,128]{2,1,0:T(8,128)(2,1)}, u32[]{:S(2)}, u32[]{:S(2)}) collective-permute-start(bf16[8,512,128]{2,1,0:T(8,128)(2,1)} %get-tuple-element.37), channel_id=1, source_target_pairs={{0,4},{1,5},{2,6},{3,7},{4,0},{5,1},{6,2},{7,3},{8,12},{9,13},{10,... | collective-permute-start | bytes 3145736 | tf_op jit(solution)/shard_map/ppermute | solution.py:265
  149.4 9.9 %collective-permute-done.16 = bf16[8,512,128]{2,1,0:T(8,128)(2,1)} collective-permute-done((bf16[8,512,128]{2,1,0:T(8,128)(2,1)}, bf16[8,512,128]{2,1,0:T(8,128)(2,1)}, u32[]{:S(2)}, u32[]{:S(2)}) %collective-permute-start.16) | collective-permute-done | bytes 1048608 | tf_op jit(solution)/shard_map/ppermute | solution.py:265
  161.3 2.4 %collective-permute-done.18 = bf16[8,512,128]{2,1,0:T(8,128)(2,1)} collective-permute-done((bf16[8,512,128]{2,1,0:T(8,128)(2,1)}, bf16[8,512,128]{2,1,0:T(8,128)(2,1)}, u32[]{:S(2)}, u32[]{:S(2)}) %collective-permute-start.18) | collective-permute-done | bytes 1048608 | tf_op jit(solution)/shard_map/ppermute | solution.py:265
  163.7 4.2 %collective-permute-start.15 = (bf16[8,512,128]{2,1,0:T(8,128)(2,1)}, bf16[8,512,128]{2,1,0:T(8,128)(2,1)S(1)}, u32[]{:S(2)}, u32[]{:S(2)}) collective-permute-start(bf16[8,512,128]{2,1,0:T(8,128)(2,1)} %get-tuple-element.38), channel_id=1, source_target_pairs={{0,4},{1,5},{2,6},{3,7},{4,0},{5,1},{6,2},{7,3},{8,12},{9,13},{10,... | collective-permute-start | bytes 3145736 | tf_op jit(solution)/shard_map/ppermute | solution.py:265
  167.9 3.3 %collective-permute-done.19 = bf16[8,512,128]{2,1,0:T(8,128)(2,1)} collective-permute-done((bf16[8,512,128]{2,1,0:T(8,128)(2,1)}, bf16[8,512,128]{2,1,0:T(8,128)(2,1)}, u32[]{:S(2)}, u32[]{:S(2)}) %collective-permute-start.19) | collective-permute-done | bytes 1048608 | tf_op jit(solution)/shard_map/ppermute | solution.py:265
  173.7 14.9 %shard_map.91.refs_8_ = f32[96,256,256]{2,1,0:T(8,128)} custom-call(s32[4,192]{1,0:T(4,128)S(1)} %multiply_add_fusion.idx, f32[128]{0:T(128)S(1)} %pad_maximum_fusion.12.wts, bf16[16,256,128]{2,1,0:T(8,128)(2,1)S(1)} %bitcast.89, bf16[16,256,128]{2,1,0:T(8,128)(2,1)} %bitcast.37.refs_1_, bf16[16,256,128]{2,1,0:T(8,128)(2,1)S(1)} %bitcast.90, ...), custom_call_target="tpu_custom_call" | custom-call | flops 6442450944 | bytes 33554432 | tf_op jit(solution)/shard_map/pallas_call | solution.py:163
  190.9 27.1 %shard_map.92 = f32[16,256,256]{2,1,0:T(8,128)} custom-call(s32[4,192]{1,0:T(4,128)S(1)} %multiply_add_fusion.idx, f32[128]{0:T(128)S(1)} %pad_maximum_fusion.12.wts, s32[64]{0:T(128)S(1)} %reshape.434.slot, f32[96]{0:T(128)S(1)} %add_bitcast_fusion.1.dsum, f32[1,256]{1,0:T(1,128)S(1)} %bitcast.94, f32[256,1]{1,0:T(8,128)S(1)} %copy.78.vcol, ...), custom_call_target="tpu_custom_call" | custom-call | flops 6442450944 | bytes 37748736 | tf_op jit(solution)/shard_map/pallas_call | solution.py:183
  (130 shorter events, 39.3 us)
Async XLA Ops:
  0.0 64.0 %copy-start = (bf16[1024,1024]{1,0:T(8,128)(2,1)S(1)}, bf16[1024,1024]{1,0:T(8,128)(2,1)}, u32[]{:S(2)}) copy-start(bf16[1024,1024]{1,0:T(8,128)(2,1)} %param.11) | copy-start | bytes 6291460
  28.7 35.2 %all-to-all-start = ((bf16[16,64,512]{2,1,0:T(8,128)(2,1)}), bf16[16,64,512]{2,1,0:T(8,128)(2,1)S(1)}, u32[]{:S(2)}, u32[]{:S(2)}) async-start(bf16[16,64,512]{2,1,0:T(8,128)(2,1)} %copy.77), calls=%async_computation | async-start | bytes 2097152 | tf_op jit(solution)/shard_map/all_to_all | solution.py:280
  65.5 9.8 %collective-permute-start.3 = (bf16[2,1,512,128]{3,2,0,1:T(8,128)(2,1)S(1)}, bf16[2,1,512,128]{3,2,0,1:T(8,128)(2,1)S(1)}, u32[]{:S(2)}, u32[]{:S(2)}) collective-permute-start(bf16[2,1,512,128]{3,2,0,1:T(8,128)(2,1)S(1)} %maximum_bitcast_fusion.3), channel_id=1, source_target_pairs={{0,3},{1,2},{2,1},{3,0},{4,7},{5,6},{6,5},{7,4},{8,11},{9,10},{10,... | collective-permute-start | bytes 786440 | tf_op jit(solution)/shard_map/ppermute | solution.py:265
  66.5 8.9 %collective-permute-start.2 = (bf16[2,1,512,128]{3,2,0,1:T(8,128)(2,1)S(1)}, bf16[2,1,512,128]{3,2,0,1:T(8,128)(2,1)S(1)}, u32[]{:S(2)}, u32[]{:S(2)}) collective-permute-start(bf16[2,1,512,128]{3,2,0,1:T(8,128)(2,1)S(1)} %maximum_bitcast_fusion.2), channel_id=1, source_target_pairs={{0,1},{1,0},{2,3},{3,2},{4,5},{5,4},{6,7},{7,6},{8,9},{9,8},{10,11... | collective-permute-start | bytes 786440 | tf_op jit(solution)/shard_map/ppermute | solution.py:265
  67.2 9.1 %collective-permute-start.1 = (bf16[2,1,512,128]{3,2,0,1:T(8,128)(2,1)S(1)}, bf16[2,1,512,128]{3,2,0,1:T(8,128)(2,1)S(1)}, u32[]{:S(2)}, u32[]{:S(2)}) collective-permute-start(bf16[2,1,512,128]{3,2,0,1:T(8,128)(2,1)S(1)} %maximum_bitcast_fusion.1), channel_id=1, source_target_pairs={{0,12},{1,13},{2,14},{3,15},{4,8},{5,9},{6,10},{7,11},{8,4},{9,5},... | collective-permute-start | bytes 786440 | tf_op jit(solution)/shard_map/ppermute | solution.py:265
  68.5 9.1 %collective-permute-start = (bf16[2,1,512,128]{3,2,0,1:T(8,128)(2,1)S(1)}, bf16[2,1,512,128]{3,2,0,1:T(8,128)(2,1)S(1)}, u32[]{:S(2)}, u32[]{:S(2)}) collective-permute-start(bf16[2,1,512,128]{3,2,0,1:T(8,128)(2,1)S(1)} %maximum_bitcast_fusion), channel_id=1, source_target_pairs={{0,4},{1,5},{2,6},{3,7},{4,0},{5,1},{6,2},{7,3},{8,12},{9,13},{10,... | collective-permute-start | bytes 786440 | tf_op jit(solution)/shard_map/ppermute | solution.py:265
  76.3 19.6 %copy-start.6 = (bf16[2,2,512,128]{3,2,0,1:T(8,128)(2,1)}, bf16[2,2,512,128]{3,2,0,1:T(8,128)(2,1)S(1)}, u32[]{:S(2)}) copy-start(bf16[2,2,512,128]{3,2,0,1:T(8,128)(2,1)S(1)} %pad_maximum_fusion.9) | copy-start | bytes 1572868
  78.5 14.1 %collective-permute-start.7 = (bf16[2,2,512,128]{3,2,0,1:T(8,128)(2,1)S(1)}, bf16[2,2,512,128]{3,2,0,1:T(8,128)(2,1)S(1)}, u32[]{:S(2)}, u32[]{:S(2)}) collective-permute-start(bf16[2,2,512,128]{3,2,0,1:T(8,128)(2,1)S(1)} %pad_maximum_fusion.11), channel_id=1, source_target_pairs={{0,1},{1,0},{2,3},{3,2},{4,5},{5,4},{6,7},{7,6},{8,9},{9,8},{10,11... | collective-permute-start | bytes 1572872 | tf_op jit(solution)/shard_map/ppermute | solution.py:265
  81.0 14.8 %collective-permute-start.6 = (bf16[2,2,512,128]{3,2,0,1:T(8,128)(2,1)S(1)}, bf16[2,2,512,128]{3,2,0,1:T(8,128)(2,1)S(1)}, u32[]{:S(2)}, u32[]{:S(2)}) collective-permute-start(bf16[2,2,512,128]{3,2,0,1:T(8,128)(2,1)S(1)} %pad_maximum_fusion.10), channel_id=1, source_target_pairs={{0,3},{1,2},{2,1},{3,0},{4,7},{5,6},{6,5},{7,4},{8,11},{9,10},{10,... | collective-permute-start | bytes 1572872 | tf_op jit(solution)/shard_map/ppermute | solution.py:265
  82.9 13.6 %collective-permute-start.5 = (bf16[2,2,512,128]{3,2,0,1:T(8,128)(2,1)S(1)}, bf16[2,2,512,128]{3,2,0,1:T(8,128)(2,1)S(1)}, u32[]{:S(2)}, u32[]{:S(2)}) collective-permute-start(bf16[2,2,512,128]{3,2,0,1:T(8,128)(2,1)S(1)} %pad_maximum_fusion.9), channel_id=1, source_target_pairs={{0,4},{1,5},{2,6},{3,7},{4,0},{5,1},{6,2},{7,3},{8,12},{9,13},{10,... | collective-permute-start | bytes 1572872 | tf_op jit(solution)/shard_map/ppermute | solution.py:265
  85.0 13.2 %collective-permute-start.4 = (bf16[2,2,512,128]{3,2,0,1:T(8,128)(2,1)}, bf16[2,2,512,128]{3,2,0,1:T(8,128)(2,1)S(1)}, u32[]{:S(2)}, u32[]{:S(2)}) collective-permute-start(bf16[2,2,512,128]{3,2,0,1:T(8,128)(2,1)} %pad_maximum_fusion.8), channel_id=1, source_target_pairs={{0,12},{1,13},{2,14},{3,15},{4,8},{5,9},{6,10},{7,11},{8,4},{9,5},... | collective-permute-start | bytes 1572872 | tf_op jit(solution)/shard_map/ppermute | solution.py:265
  100.3 23.5 %collective-permute-start.11 = (bf16[2,4,512,128]{3,2,0,1:T(8,128)(2,1)S(1)}, bf16[2,4,512,128]{3,2,0,1:T(8,128)(2,1)}, u32[]{:S(2)}, u32[]{:S(2)}) collective-permute-start(bf16[2,4,512,128]{3,2,0,1:T(8,128)(2,1)S(1)} %pad_maximum_fusion.7), channel_id=1, source_target_pairs={{0,12},{1,13},{2,14},{3,15},{4,8},{5,9},{6,10},{7,11},{8,4},{9,5},... | collective-permute-start | bytes 3145736 | tf_op jit(solution)/shard_map/ppermute | solution.py:265
  101.0 25.5 %collective-permute-start.10 = (bf16[2,4,512,128]{3,2,0,1:T(8,128)(2,1)S(1)}, bf16[2,4,512,128]{3,2,0,1:T(8,128)(2,1)}, u32[]{:S(2)}, u32[]{:S(2)}) collective-permute-start(bf16[2,4,512,128]{3,2,0,1:T(8,128)(2,1)S(1)} %pad_maximum_fusion.6), channel_id=1, source_target_pairs={{0,4},{1,5},{2,6},{3,7},{4,0},{5,1},{6,2},{7,3},{8,12},{9,13},{10,... | collective-permute-start | bytes 3145736 | tf_op jit(solution)/shard_map/ppermute | solution.py:265
  104.0 24.5 %collective-permute-start.9 = (bf16[2,4,512,128]{3,2,0,1:T(8,128)(2,1)S(1)}, bf16[2,4,512,128]{3,2,0,1:T(8,128)(2,1)S(1)}, u32[]{:S(2)}, u32[]{:S(2)}) collective-permute-start(bf16[2,4,512,128]{3,2,0,1:T(8,128)(2,1)S(1)} %pad_maximum_fusion.5), channel_id=1, source_target_pairs={{0,3},{1,2},{2,1},{3,0},{4,7},{5,6},{6,5},{7,4},{8,11},{9,10},{10,... | collective-permute-start | bytes 3145736 | tf_op jit(solution)/shard_map/ppermute | solution.py:265
  105.9 22.9 %collective-permute-start.8 = (bf16[2,4,512,128]{3,2,0,1:T(8,128)(2,1)}, bf16[2,4,512,128]{3,2,0,1:T(8,128)(2,1)S(1)}, u32[]{:S(2)}, u32[]{:S(2)}) collective-permute-start(bf16[2,4,512,128]{3,2,0,1:T(8,128)(2,1)} %pad_maximum_fusion.4), channel_id=1, source_target_pairs={{0,1},{1,0},{2,3},{3,2},{4,5},{5,4},{6,7},{7,6},{8,9},{9,8},{10,11... | collective-permute-start | bytes 3145736 | tf_op jit(solution)/shard_map/ppermute | solution.py:265
  131.6 27.6 %collective-permute-start.16 = (bf16[8,512,128]{2,1,0:T(8,128)(2,1)}, bf16[8,512,128]{2,1,0:T(8,128)(2,1)}, u32[]{:S(2)}, u32[]{:S(2)}) collective-permute-start(bf16[8,512,128]{2,1,0:T(8,128)(2,1)} %get-tuple-element.49), channel_id=1, source_target_pairs={{0,3},{1,2},{2,1},{3,0},{4,7},{5,6},{6,5},{7,4},{8,11},{9,10},{10,... | collective-permute-start | bytes 3145736 | tf_op jit(solution)/shard_map/ppermute | solution.py:265
  135.3 25.7 %collective-permute-start.17 = (bf16[8,512,128]{2,1,0:T(8,128)(2,1)}, bf16[8,512,128]{2,1,0:T(8,128)(2,1)}, u32[]{:S(2)}, u32[]{:S(2)}) collective-permute-start(bf16[8,512,128]{2,1,0:T(8,128)(2,1)} %get-tuple-element.45), channel_id=1, source_target_pairs={{0,1},{1,0},{2,3},{3,2},{4,5},{5,4},{6,7},{7,6},{8,9},{9,8},{10,11... | collective-permute-start | bytes 3145736 | tf_op jit(solution)/shard_map/ppermute | solution.py:265
  137.9 25.9 %collective-permute-start.18 = (bf16[8,512,128]{2,1,0:T(8,128)(2,1)}, bf16[8,512,128]{2,1,0:T(8,128)(2,1)}, u32[]{:S(2)}, u32[]{:S(2)}) collective-permute-start(bf16[8,512,128]{2,1,0:T(8,128)(2,1)} %get-tuple-element.41), channel_id=1, source_target_pairs={{0,12},{1,13},{2,14},{3,15},{4,8},{5,9},{6,10},{7,11},{8,4},{9,5},... | collective-permute-start | bytes 3145736 | tf_op jit(solution)/shard_map/ppermute | solution.py:265
  143.3 28.0 %collective-permute-start.19 = (bf16[8,512,128]{2,1,0:T(8,128)(2,1)}, bf16[8,512,128]{2,1,0:T(8,128)(2,1)}, u32[]{:S(2)}, u32[]{:S(2)}) collective-permute-start(bf16[8,512,128]{2,1,0:T(8,128)(2,1)} %get-tuple-element.37), channel_id=1, source_target_pairs={{0,4},{1,5},{2,6},{3,7},{4,0},{5,1},{6,2},{7,3},{8,12},{9,13},{10,... | collective-permute-start | bytes 3145736 | tf_op jit(solution)/shard_map/ppermute | solution.py:265
  147.7 40.9 %collective-permute-start.12 = (bf16[8,512,128]{2,1,0:T(8,128)(2,1)}, bf16[8,512,128]{2,1,0:T(8,128)(2,1)S(1)}, u32[]{:S(2)}, u32[]{:S(2)}) collective-permute-start(bf16[8,512,128]{2,1,0:T(8,128)(2,1)} %get-tuple-element.50), channel_id=1, source_target_pairs={{0,3},{1,2},{2,1},{3,0},{4,7},{5,6},{6,5},{7,4},{8,11},{9,10},{10,... | collective-permute-start | bytes 3145736 | tf_op jit(solution)/shard_map/ppermute | solution.py:265
  159.2 29.4 %collective-permute-start.13 = (bf16[8,512,128]{2,1,0:T(8,128)(2,1)}, bf16[8,512,128]{2,1,0:T(8,128)(2,1)S(1)}, u32[]{:S(2)}, u32[]{:S(2)}) collective-permute-start(bf16[8,512,128]{2,1,0:T(8,128)(2,1)} %get-tuple-element.46), channel_id=1, source_target_pairs={{0,1},{1,0},{2,3},{3,2},{4,5},{5,4},{6,7},{7,6},{8,9},{9,8},{10,11... | collective-permute-start | bytes 3145736 | tf_op jit(solution)/shard_map/ppermute | solution.py:265
  161.1 27.6 %collective-permute-start.14 = (bf16[8,512,128]{2,1,0:T(8,128)(2,1)}, bf16[8,512,128]{2,1,0:T(8,128)(2,1)S(1)}, u32[]{:S(2)}, u32[]{:S(2)}) collective-permute-start(bf16[8,512,128]{2,1,0:T(8,128)(2,1)} %get-tuple-element.42), channel_id=1, source_target_pairs={{0,12},{1,13},{2,14},{3,15},{4,8},{5,9},{6,10},{7,11},{8,4},{9,5},... | collective-permute-start | bytes 3145736 | tf_op jit(solution)/shard_map/ppermute | solution.py:265
  163.7 26.2 %collective-permute-start.15 = (bf16[8,512,128]{2,1,0:T(8,128)(2,1)}, bf16[8,512,128]{2,1,0:T(8,128)(2,1)S(1)}, u32[]{:S(2)}, u32[]{:S(2)}) collective-permute-start(bf16[8,512,128]{2,1,0:T(8,128)(2,1)} %get-tuple-element.38), channel_id=1, source_target_pairs={{0,4},{1,5},{2,6},{3,7},{4,0},{5,1},{6,2},{7,3},{8,12},{9,13},{10,... | collective-permute-start | bytes 3145736 | tf_op jit(solution)/shard_map/ppermute | solution.py:265
  190.9 27.2 %copy-start.1 = (bf16[1024,1024]{1,0:T(8,128)(2,1)S(1)}, bf16[1024,1024]{1,0:T(8,128)(2,1)}, u32[]{:S(2)}) copy-start(bf16[1024,1024]{1,0:T(8,128)(2,1)} %param.11) | copy-start | bytes 6291460
  (10 other events, 33.7 us)

commit v3 on v2

v3 whole, which is shorter than its diff:
```python
import jax
import jax.numpy as jnp
from jax import lax
from jax.experimental import pallas as pl
from jax.experimental.pallas import tpu as pltpu
from jax.sharding import PartitionSpec as P

NT = (((1,), (1,)), ((), ()))
MIB = 2**20
MASKS = ((4, 12, 1, 3), (1, 3, 4, 12), (12, 4, 3, 1), (3, 1, 12, 4))


def recip(x):
    r = pl.reciprocal(x, approx=True)
    return r * (2.0 - x * r)


def listed(wts, order):
    def entry(n, count):
        hit = wts[64 + n] != 0.0

        @pl.when(hit)
        def _():
            order[count] = n

        return count + hit.astype(jnp.int32)

    count = lax.fori_loop(0, 64, entry, 0)
    for k in range(4):
        order[count + k] = -1
    return (count + 3) // 4


def pair_kernel(idx, wts, slot, dsum, vrow, vcol, *refs):
    pieces, out, pool, mixed, amp, vsum, order, sems, out_sems = refs[:16], *refs[16:]
    copies = [
        pltpu.make_async_copy(
            pieces[4 * q + part], pool.at[q, pl.ds(8 * part, 8)], sems.at[4 * q + part]
        )
        for q in range(4)
        for part in range(4)
    ]
    for copy in copies:
        copy.start()
    fours = listed(wts, order)
    vsum[...] = vrow[...] + vcol[...]

    def clear(s, carry):
        mixed[s] = jnp.zeros((256, 256), jnp.float32)
        return carry

    lax.fori_loop(0, 16, clear, 0)
    for copy in copies:
        copy.wait()

    def product(n):
        left = jnp.concatenate([pool[q, idx[q, n]] for q in range(4)], axis=1)
        right = jnp.concatenate([pool[q, idx[q, 96 + n]] for q in range(4)], axis=1)
        return lax.dot_general(left, right, NT, preferred_element_type=jnp.float32)

    def coupled(g, carry):
        for u in range(4):
            entry = order[4 * g + u]
            n = jnp.maximum(entry, 0)
            weight = jnp.where(entry >= 0, wts[64 + n], 0.0)
            start = -(product(32 + n) * recip(vsum[...] - dsum[32 + n]))
            rounded = start.astype(jnp.bfloat16).astype(jnp.float32)
            mixed[n // 4] += weight * rounded
        return carry

    def received(g, carry):
        for u in range(4):
            s = 4 * g + u
            value = (mixed[s] - product(16 + s)) * recip(vsum[...] - dsum[16 + s])
            amp[s] = value.astype(jnp.bfloat16)
        return carry

    def out_copy(g):
        rows = pl.ds(4 * g, 4)
        return pltpu.make_async_copy(mixed.at[rows], out.at[rows], out_sems.at[g])

    def own(g, carry):
        for u in range(4):
            p = 4 * g + u
            total = -product(p)
            for e in range(4):
                total += wts[4 * p + e] * amp[slot[4 * p + e]].astype(jnp.float32)
            mixed[p] = total * recip(vsum[...] - dsum[p])
        out_copy(g).start()
        return carry

    def finish(g, carry):
        out_copy(g).wait()
        return carry

    lax.fori_loop(0, fours, coupled, 0)
    lax.fori_loop(0, 4, received, 0)
    lax.fori_loop(0, 4, own, 0)
    lax.fori_loop(0, 4, finish, 0)


SMEM = pl.BlockSpec(memory_space=pltpu.SMEM)
VMEM = pl.BlockSpec(memory_space=pltpu.VMEM)
HBM = pl.BlockSpec(memory_space=pl.ANY)


def amplitudes(idx, wts, slot, dsum, virt, pieces):
    return pl.pallas_call(
        pair_kernel,
        in_specs=[SMEM] * 4 + [VMEM] * 2 + [HBM] * 16,
        out_specs=HBM,
        out_shape=jax.ShapeDtypeStruct((16, 256, 256), jnp.float32),
        scratch_shapes=[
            pltpu.VMEM((4, 32, 256, 256), jnp.bfloat16),
            pltpu.VMEM((16, 256, 256), jnp.float32),
            pltpu.VMEM((16, 256, 256), jnp.bfloat16),
            pltpu.VMEM((256, 256), jnp.float32),
            pltpu.SMEM((68,), jnp.int32),
            pltpu.SemaphoreType.DMA((16,)),
            pltpu.SemaphoreType.DMA((4,)),
        ],
        compiler_params=pltpu.CompilerParams(vmem_limit_bytes=58 * MIB),
        cost_estimate=pl.CostEstimate(
            flops=96 * 2 * 256 * 256 * 1024, bytes_accessed=20 * MIB, transcendentals=0
        ),
    )(idx, wts, slot, dsum, virt[None, :], virt[:, None], *pieces)


def lookup(table, rows, cols):
    ids = jnp.arange(32, dtype=jnp.int32)
    pick = (rows[:, None, None] == ids[None, :, None]) & (
        cols[:, None, None] == ids[None, None, :]
    )
    return jnp.sum(jnp.where(pick, table[None], 0.0), axis=(1, 2))


def coupling(table, orb, cpl):
    i, j = orb[:, 0, None], orb[:, 1, None]
    k, l = cpl[:, :, 0], cpl[:, :, 1]
    first = (l == j) & (k != i)
    second = (k == i) & (l != j)
    rows = jnp.where(first, i, j) + jnp.zeros_like(k)
    cols = jnp.where(first, k, l)
    value = lookup(table, rows.reshape(-1), cols.reshape(-1)).reshape(k.shape)
    return jnp.where(first | second, value, 0.0).reshape(-1)


def arrival(masks):
    order = [0]
    for mask in masks:
        order = order + [o ^ mask for o in order]
    return order


def found_in(values, order):
    ids = jnp.arange(16, dtype=jnp.int32)
    hit = values[..., None] == jnp.array(order, jnp.int32)
    return jnp.sum(jnp.where(hit, ids, 0), axis=-1)


def tables(metas, fock, orb, cpl, cpl_slot):
    col = lax.axis_index("aux")
    grp = lax.axis_index("grp")
    chosen = jnp.sum(
        jnp.where(jnp.arange(16)[None, :] == grp, metas[:, 160:], 0), axis=1
    )
    pick = chosen[:, None, None] == jnp.arange(16, dtype=jnp.int32)[None, :, None]
    sent = jnp.sum(jnp.where(pick, metas[:, :160].reshape(16, 16, 10), 0), axis=1)
    orb_q, cpl_q = sent[:, :2], sent[:, 2:].reshape(16, 4, 2)

    local = jnp.arange(32, dtype=jnp.int32)
    whole = local // 2 * 32 + col * 2 + local % 2
    select = (whole[:, None] == jnp.arange(512)[None, :]).astype(jnp.bfloat16)
    fock_rows = jnp.dot(select, fock, preferred_element_type=jnp.float32)
    fock_col = lax.dot_general(
        fock_rows.astype(jnp.bfloat16), select, NT, preferred_element_type=jnp.float32
    )
    diag = jnp.sum(jnp.where(local[:, None] == local[None, :], fock_col, 0.0), axis=1)

    orbs = jnp.concatenate([orb, orb_q, cpl_q.reshape(64, 2)], axis=0)
    at = orbs[:, :, None] == local[None, None, :]
    dsum = jnp.sum(jnp.where(at, diag[None, None, :], 0.0), axis=2)
    dsum = dsum[:, 0] + dsum[:, 1]
    wts = jnp.concatenate([coupling(fock_col, orb, cpl), coupling(fock_col, orb_q, cpl_q)])

    flat = orbs.T.reshape(192)
    offset = (flat // 2) ^ grp
    spot = jnp.stack([found_in(offset, arrival(masks)) for masks in MASKS])
    slot = found_in(cpl_slot.reshape(64) ^ grp, arrival(MASKS[0]))
    return spot * 2 + flat % 2, wts, slot, dsum


def swap(block, mask):
    return lax.ppermute(block, "grp", [(g, g ^ mask) for g in range(16)])


def on_device(
    integrals, metric, fock, virt_energy, send_orb, pair_orb, send_pair, cpl_slot, cpl_orb
):
    orb = pair_orb // 32 * 2 + pair_orb % 2
    cpl = cpl_orb // 32 * 2 + cpl_orb % 2
    metas = jnp.concatenate([orb, cpl.reshape(16, 8)], axis=1).reshape(1, 160)
    metas = jnp.concatenate([metas, send_pair], axis=1)
    for mask in MASKS[0]:
        metas = jnp.concatenate([metas, swap(metas, mask)], axis=0)

    rows = integrals.reshape(64, 16, 512).transpose(1, 0, 2)
    block = lax.all_to_all(rows, "aux", split_axis=0, concat_axis=0, tiled=True)
    block, metas = lax.optimization_barrier((block, metas))
    idx, wts, slot, dsum = tables(metas, fock, orb, cpl, cpl_slot)
    fitted = lax.dot_general(
        block.reshape(1024, 512),
        metric,
        (((0,), (1,)), ((), ())),
        preferred_element_type=jnp.float32,
    ).astype(jnp.bfloat16)
    held = [fitted[None, :, 256 * q : 256 * q + 256] for q in range(4)]
    for step in range(2):
        got = [swap(held[q], MASKS[q][step]) for q in range(4)]
        held = [jnp.concatenate([a, b], axis=0) for a, b in zip(held, got)]
        held = list(lax.optimization_barrier(tuple(held)))
    third = [swap(held[q], MASKS[q][2]) for q in range(4)]
    early = [swap(held[q], MASKS[q][3]) for q in range(4)]
    late = [swap(third[q], MASKS[q][3]) for q in range(4)]
    pieces = [x.reshape(8, 256, 256) for four in zip(held, third, early, late) for x in four]
    return amplitudes(idx, wts, slot, dsum, virt_energy, pieces)


def solution(mesh):
    in_specs = (
        P("aux", "grp", None),
        P(),
        P(),
        P(),
        P(("aux", "grp"), None),
        P(("aux", "grp"), None),
        P(("aux", "grp"), None),
        P(("aux", "grp"), None),
        P(("aux", "grp"), None, None),
    )
    out_specs = P(("aux", "grp"), None, None)
    return jax.shard_map(
        on_device, mesh=mesh, in_specs=in_specs, out_specs=out_specs, check_vma=False
    )
```

time: 220 us -> 185 us (0.84)
  blocking collectives: 23.3 us -> 0 us
  Pallas kernels: 42.1 us -> 26.4 us
  local copies, waits for them, and re-layouts: 20.8 us -> 7.34 us
  starting transfers between devices: 37.3 us -> 47.1 us
  waiting for transfers between devices: 79.2 us -> 85.3 us
  other arithmetic: 12.3 us -> 16.3 us
    all_gather x1 -> x0, blocking collectives: 23.3 us -> none  [on_device(): metas = lax.all_gather(meta, 'grp', axis=0, tiled=True)]
    ppermute x20 -> x24, waiting for transfers between devices: 55 us -> 74.9 us  [swap(): return lax.ppermute(block, 'grp', [(g, g ^ mask) for g in range(16)])]
    pallas_call x2 -> x1, Pallas kernels: 42.1 us -> 26.4 us  [amplitudes(): pl.pallas_call(pair_kernel, in_specs=[SMEM] * 4 + [VMEM] * 2 + [HBM] * 16...]
    all_to_all x1, waiting for transfers between devices: 24.2 us -> 10.3 us  [on_device(): block = lax.all_to_all(rows, 'aux', split_axis=0, concat_axis=0, tiled=True)]
    squeeze x4 -> x0, local copies, waits for them, and re-layouts: 11.2 us -> none  [on_device(): sent = [block[h] for block in held]]
    ppermute x20 -> x24, starting transfers between devices: 28.8 us -> 38.6 us  [swap(): return lax.ppermute(block, 'grp', [(g, g ^ mask) for g in range(16)])]
    concatenate x13, other arithmetic: 8.95 us -> 13 us  [the longest x8 12.6 us: on_device(): held = [jnp.concatenate([a, b], axis=0) for a, b in zip(held, got)]]
    unnamed x28 -> x24, local copies, waits for them, and re-layouts: 3.83 us -> 0.06 us
  transfers between devices with their start and end apart: 21 -> 25, of which waited for: 16 -> 17; matrix products, arithmetic and copies ran while one was open for 9% -> 10% of each run, Pallas kernels for 7% -> 0%
where the time goes in v3:
time: 185 us
  waiting for transfers between devices  85.3 us (46%)
  starting transfers between devices  47.1 us (25%)
  Pallas kernels  26.4 us (14%)
  other arithmetic  16.3 us (9%)
  local copies, waits for them, and re-layouts  7.34 us (4%)
    ppermute x24, waiting for transfers between devices, swap(): return lax.ppermute(block, 'grp', [(g, g ^ mask) for g in range(16)])  74.9 us
    ppermute x24, starting transfers between devices, swap(): return lax.ppermute(block, 'grp', [(g, g ^ mask) for g in range(16)])  38.6 us
    pallas_call x1, Pallas kernels, amplitudes(): pl.pallas_call(pair_kernel, in_specs=[SMEM] * 4 + [VMEM] * 2 + [HBM] * 16...  26.4 us
    concatenate x8, other arithmetic, on_device(): held = [jnp.concatenate([a, b], axis=0) for a, b in zip(held, got)]  12.6 us
    all_to_all x1, waiting for transfers between devices, on_device(): block = lax.all_to_all(rows, 'aux', split_axis=0, concat_axis=0, tiled=True)  10.3 us
    all_to_all x1, starting transfers between devices, on_device(): block = lax.all_to_all(rows, 'aux', split_axis=0, concat_axis=0, tiled=True)  8.57 us
  transfers between devices with their start and end apart: 25, of which 17 were waited for; matrix products, arithmetic and copies ran while one was open for 10% of the time, Pallas kernels for 0%

profile of v3, /device:TPU:2, one launch (start us, length us, event | category | flops | bytes accessed | tf_op | source)
XLA Modules:
  0.0 184.6 jit_solution(17393212960049685888)
XLA Ops:
  3.2 8.6 %all-to-all-start = ((bf16[16,64,512]{2,1,0:T(8,128)(2,1)}), bf16[16,64,512]{2,1,0:T(8,128)(2,1)S(1)}, u32[]{:S(2)}, u32[]{:S(2)}) async-start(bf16[16,64,512]{2,1,0:T(8,128)(2,1)} %copy.70), calls=%async_computation | async-start | bytes 2097152 | tf_op jit(solution)/shard_map/all_to_all | solution.py:208
  12.6 3.0 %collective-permute-done = s32[1,176]{1,0:T(1,128)S(1)} collective-permute-done((s32[1,176]{1,0:T(1,128)S(1)}, s32[1,176]{1,0:T(1,128)S(1)}, u32[]{:S(2)}, u32[]{:S(2)}) %collective-permute-start) | collective-permute-done | bytes 736 | tf_op jit(solution)/shard_map/ppermute | solution.py:194
  17.3 2.1 %collective-permute-done.1 = s32[2,176]{1,0:T(2,128)S(1)} collective-permute-done((s32[2,176]{1,0:T(2,128)S(1)}, s32[2,176]{1,0:T(2,128)S(1)}, u32[]{:S(2)}, u32[]{:S(2)}) %collective-permute-start.1) | collective-permute-done | bytes 1440 | tf_op jit(solution)/shard_map/ppermute | solution.py:194
  21.0 2.0 %collective-permute-done.2 = s32[4,176]{1,0:T(4,128)S(1)} collective-permute-done((s32[4,176]{1,0:T(4,128)S(1)}, s32[4,176]{1,0:T(4,128)S(1)}, u32[]{:S(2)}, u32[]{:S(2)}) %collective-permute-start.2) | collective-permute-done | bytes 2848 | tf_op jit(solution)/shard_map/ppermute | solution.py:194
  23.1 3.0 %collective-permute-start.3 = (s32[8,176]{1,0:T(8,128)S(1)}, s32[8,176]{1,0:T(8,128)S(1)}, u32[]{:S(2)}, u32[]{:S(2)}) collective-permute-start(s32[8,176]{1,0:T(8,128)S(1)} %pad_add_fusion.2), channel_id=1, source_target_pairs={{0,3},{1,2},{2,1},{3,0},{4,7},{5,6},{6,5},{7,4},{8,11},{9,10},{10,... | collective-permute-start | bytes 16904 | tf_op jit(solution)/shard_map/ppermute | solution.py:194
  28.1 10.3 %all-to-all-done = bf16[16,64,512]{2,1,0:T(8,128)(2,1)S(1)} async-done(((bf16[16,64,512]{2,1,0:T(8,128)(2,1)}), bf16[16,64,512]{2,1,0:T(8,128)(2,1)S(1)}, u32[]{:S(2)}, u32[]{:S(2)}) %all-to-all-start) | async-done | bytes 1048608 | tf_op jit(solution)/shard_map/all_to_all | solution.py:208
  40.5 3.0 %collective-permute-start.7 = (bf16[1,512,256]{2,1,0:T(8,128)(2,1)S(1)}, bf16[1,512,256]{2,1,0:T(8,128)(2,1)}, u32[]{:S(2)}, u32[]{:S(2)}) collective-permute-start(bf16[1,512,256]{2,1,0:T(8,128)(2,1)S(1)} %get-tuple-element.33), channel_id=1, source_target_pairs={{0,3},{1,2},{2,1},{3,0},{4,7},{5,6},{6,5},{7,4},{8,11},{9,10},{10,... | collective-permute-start | bytes 786440 | tf_op jit(solution)/shard_map/ppermute | solution.py:194
  47.5 2.8 %collective-permute-done.7 = bf16[1,512,256]{2,1,0:T(8,128)(2,1)} collective-permute-done((bf16[1,512,256]{2,1,0:T(8,128)(2,1)S(1)}, bf16[1,512,256]{2,1,0:T(8,128)(2,1)}, u32[]{:S(2)}, u32[]{:S(2)}) %collective-permute-start.7) | collective-permute-done | bytes 262176 | tf_op jit(solution)/shard_map/ppermute | solution.py:194
  54.8 1.9 %pad_maximum_fusion.5 = bf16[2,512,256]{2,1,0:T(8,128)(2,1)} fusion(bf16[1,512,256]{2,1,0:T(8,128)(2,1)} %collective-permute-done.5, bf16[1,512,256]{2,1,0:T(8,128)(2,1)} %get-tuple-element.35), kind=kLoop, calls=%fused_computation.8 | loop fusion | flops 262144 | bytes 1048576 | tf_op jit(solution)/shard_map/concatenate | solution.py:220
  62.4 9.4 %collective-permute-done.8 = bf16[2,512,256]{2,1,0:T(8,128)(2,1)} collective-permute-done((bf16[2,512,256]{2,1,0:T(8,128)(2,1)}, bf16[2,512,256]{2,1,0:T(8,128)(2,1)}, u32[]{:S(2)}, u32[]{:S(2)}) %collective-permute-start.8) | collective-permute-done | bytes 524320 | tf_op jit(solution)/shard_map/ppermute | solution.py:194
  71.8 2.3 %pad_maximum_fusion = bf16[4,512,256]{2,1,0:T(8,128)(2,1)} fusion(bf16[2,512,256]{2,1,0:T(8,128)(2,1)} %collective-permute-done.8, bf16[2,512,256]{2,1,0:T(8,128)(2,1)} %pad_maximum_fusion.4), kind=kLoop, calls=%fused_computation.3 | loop fusion | flops 524288 | bytes 2097152 | tf_op jit(solution)/shard_map/concatenate | solution.py:220
  74.1 2.3 %pad_maximum_fusion.1 = bf16[4,512,256]{2,1,0:T(8,128)(2,1)} fusion(bf16[2,512,256]{2,1,0:T(8,128)(2,1)} %collective-permute-done.9, bf16[2,512,256]{2,1,0:T(8,128)(2,1)} %pad_maximum_fusion.5), kind=kLoop, calls=%fused_computation.4 | loop fusion | flops 524288 | bytes 2097152 | tf_op jit(solution)/shard_map/concatenate | solution.py:220
  76.4 2.1 %pad_maximum_fusion.2 = bf16[4,512,256]{2,1,0:T(8,128)(2,1)} fusion(bf16[2,512,256]{2,1,0:T(8,128)(2,1)} %collective-permute-done.10, bf16[2,512,256]{2,1,0:T(8,128)(2,1)S(1)} %pad_maximum_fusion.6), kind=kLoop, calls=%fused_computation.5 | loop fusion | flops 524288 | bytes 2097152 | tf_op jit(solution)/shard_map/concatenate | solution.py:220
  84.8 3.3 %collective-permute-start.15 = (bf16[4,512,256]{2,1,0:T(8,128)(2,1)}, bf16[4,512,256]{2,1,0:T(8,128)(2,1)}, u32[]{:S(2)}, u32[]{:S(2)}) collective-permute-start(bf16[4,512,256]{2,1,0:T(8,128)(2,1)} %pad_maximum_fusion.1), channel_id=1, source_target_pairs={{0,4},{1,5},{2,6},{3,7},{4,0},{5,1},{6,2},{7,3},{8,12},{9,13},{10,... | collective-permute-start | bytes 3145736 | tf_op jit(solution)/shard_map/ppermute | solution.py:194
  88.1 2.0 %collective-permute-start.19 = (bf16[4,512,256]{2,1,0:T(8,128)(2,1)}, bf16[4,512,256]{2,1,0:T(8,128)(2,1)}, u32[]{:S(2)}, u32[]{:S(2)}) collective-permute-start(bf16[4,512,256]{2,1,0:T(8,128)(2,1)} %pad_maximum_fusion.2), channel_id=1, source_target_pairs={{0,1},{1,0},{2,3},{3,2},{4,5},{5,4},{6,7},{7,6},{8,9},{9,8},{10,11... | collective-permute-start | bytes 3145736 | tf_op jit(solution)/shard_map/ppermute | solution.py:194
  90.2 15.4 %collective-permute-done.13 = bf16[4,512,256]{2,1,0:T(8,128)(2,1)} collective-permute-done((bf16[4,512,256]{2,1,0:T(8,128)(2,1)}, bf16[4,512,256]{2,1,0:T(8,128)(2,1)}, u32[]{:S(2)}, u32[]{:S(2)}) %collective-permute-start.13) | collective-permute-done | bytes 1048608 | tf_op jit(solution)/shard_map/ppermute | solution.py:194
  109.9 3.5 %collective-permute-start.22 = (bf16[4,512,256]{2,1,0:T(8,128)(2,1)}, bf16[4,512,256]{2,1,0:T(8,128)(2,1)}, u32[]{:S(2)}, u32[]{:S(2)}) collective-permute-start(bf16[4,512,256]{2,1,0:T(8,128)(2,1)} %pad_maximum_fusion.3), channel_id=1, source_target_pairs={{0,4},{1,5},{2,6},{3,7},{4,0},{5,1},{6,2},{7,3},{8,12},{9,13},{10,... | collective-permute-start | bytes 3145736 | tf_op jit(solution)/shard_map/ppermute | solution.py:194
  113.4 2.3 %collective-permute-start.14 = (bf16[4,512,256]{2,1,0:T(8,128)(2,1)}, bf16[4,512,256]{2,1,0:T(8,128)(2,1)}, u32[]{:S(2)}, u32[]{:S(2)}) collective-permute-start(bf16[4,512,256]{2,1,0:T(8,128)(2,1)} %collective-permute-done.12), channel_id=1, source_target_pairs={{0,3},{1,2},{2,1},{3,0},{4,7},{5,6},{6,5},{7,4},{8,11},{9,10},{10,... | collective-permute-start | bytes 3145736 | tf_op jit(solution)/shard_map/ppermute | solution.py:194
  115.6 12.3 %collective-permute-done.19 = bf16[4,512,256]{2,1,0:T(8,128)(2,1)} collective-permute-done((bf16[4,512,256]{2,1,0:T(8,128)(2,1)}, bf16[4,512,256]{2,1,0:T(8,128)(2,1)}, u32[]{:S(2)}, u32[]{:S(2)}) %collective-permute-start.19) | collective-permute-done | bytes 1048608 | tf_op jit(solution)/shard_map/ppermute | solution.py:194
  129.5 3.7 %collective-permute-done.18 = bf16[4,512,256]{2,1,0:T(8,128)(2,1)} collective-permute-done((bf16[4,512,256]{2,1,0:T(8,128)(2,1)}, bf16[4,512,256]{2,1,0:T(8,128)(2,1)}, u32[]{:S(2)}, u32[]{:S(2)}) %collective-permute-start.18) | collective-permute-done | bytes 1048608 | tf_op jit(solution)/shard_map/ppermute | solution.py:194
  133.2 3.0 %collective-permute-start.23 = (bf16[4,512,256]{2,1,0:T(8,128)(2,1)}, bf16[4,512,256]{2,1,0:T(8,128)(2,1)}, u32[]{:S(2)}, u32[]{:S(2)}) collective-permute-start(bf16[4,512,256]{2,1,0:T(8,128)(2,1)} %collective-permute-done.21), channel_id=1, source_target_pairs={{0,4},{1,5},{2,6},{3,7},{4,0},{5,1},{6,2},{7,3},{8,12},{9,13},{10,... | collective-permute-start | bytes 3145736 | tf_op jit(solution)/shard_map/ppermute | solution.py:194
  138.4 14.5 %collective-permute-done.14 = bf16[4,512,256]{2,1,0:T(8,128)(2,1)} collective-permute-done((bf16[4,512,256]{2,1,0:T(8,128)(2,1)}, bf16[4,512,256]{2,1,0:T(8,128)(2,1)}, u32[]{:S(2)}, u32[]{:S(2)}) %collective-permute-start.14) | collective-permute-done | bytes 1048608 | tf_op jit(solution)/shard_map/ppermute | solution.py:194
  153.3 4.7 %collective-permute-done.23 = bf16[4,512,256]{2,1,0:T(8,128)(2,1)} collective-permute-done((bf16[4,512,256]{2,1,0:T(8,128)(2,1)}, bf16[4,512,256]{2,1,0:T(8,128)(2,1)}, u32[]{:S(2)}, u32[]{:S(2)}) %collective-permute-start.23) | collective-permute-done | bytes 1048608 | tf_op jit(solution)/shard_map/ppermute | solution.py:194
  158.0 26.4 %shard_map.127 = f32[16,256,256]{2,1,0:T(8,128)} custom-call(s32[4,192]{1,0:T(4,128)} %fusion.4.idx, f32[128]{0:T(128)} %pad_maximum_fusion.8.wts, s32[64]{0:T(128)} %select_reduce_fusion.9.slot, f32[96]{0:T(128)} %add_bitcast_fusion.dsum, f32[1,256]{1,0:T(1,128)} %bitcast.68, f32[256,1]{1,0:T(8,128)} %copy.82.vcol, bf16[8,256,256]{2,1,0:T(8,128)(2,1)} %bitcast.18.refs_0_, ...), custom_call_target="tpu_custom_call" | custom-call | flops 12884901888 | bytes 20971520 | tf_op jit(solution)/shard_map/pallas_call | solution.py:108
  (127 shorter events, 40.1 us)
Async XLA Ops:
  3.2 35.2 %all-to-all-start = ((bf16[16,64,512]{2,1,0:T(8,128)(2,1)}), bf16[16,64,512]{2,1,0:T(8,128)(2,1)S(1)}, u32[]{:S(2)}, u32[]{:S(2)}) async-start(bf16[16,64,512]{2,1,0:T(8,128)(2,1)} %copy.70), calls=%async_computation | async-start | bytes 2097152 | tf_op jit(solution)/shard_map/all_to_all | solution.py:208
  15.7 3.6 %collective-permute-start.1 = (s32[2,176]{1,0:T(2,128)S(1)}, s32[2,176]{1,0:T(2,128)S(1)}, u32[]{:S(2)}, u32[]{:S(2)}) collective-permute-start(s32[2,176]{1,0:T(2,128)S(1)} %pad_add_fusion.4), channel_id=1, source_target_pairs={{0,12},{1,13},{2,14},{3,15},{4,8},{5,9},{6,10},{7,11},{8,4},{9,5},... | collective-permute-start | bytes 4232 | tf_op jit(solution)/shard_map/ppermute | solution.py:194
  19.4 3.6 %collective-permute-start.2 = (s32[4,176]{1,0:T(4,128)S(1)}, s32[4,176]{1,0:T(4,128)S(1)}, u32[]{:S(2)}, u32[]{:S(2)}) collective-permute-start(s32[4,176]{1,0:T(4,128)S(1)} %pad_add_fusion.3), channel_id=1, source_target_pairs={{0,1},{1,0},{2,3},{3,2},{4,5},{5,4},{6,7},{7,6},{8,9},{9,8},{10,11... | collective-permute-start | bytes 8456 | tf_op jit(solution)/shard_map/ppermute | solution.py:194
  23.1 4.9 %collective-permute-start.3 = (s32[8,176]{1,0:T(8,128)S(1)}, s32[8,176]{1,0:T(8,128)S(1)}, u32[]{:S(2)}, u32[]{:S(2)}) collective-permute-start(s32[8,176]{1,0:T(8,128)S(1)} %pad_add_fusion.2), channel_id=1, source_target_pairs={{0,3},{1,2},{2,1},{3,0},{4,7},{5,6},{6,5},{7,4},{8,11},{9,10},{10,... | collective-permute-start | bytes 16904 | tf_op jit(solution)/shard_map/ppermute | solution.py:194
  40.5 9.8 %collective-permute-start.7 = (bf16[1,512,256]{2,1,0:T(8,128)(2,1)S(1)}, bf16[1,512,256]{2,1,0:T(8,128)(2,1)}, u32[]{:S(2)}, u32[]{:S(2)}) collective-permute-start(bf16[1,512,256]{2,1,0:T(8,128)(2,1)S(1)} %get-tuple-element.33), channel_id=1, source_target_pairs={{0,3},{1,2},{2,1},{3,0},{4,7},{5,6},{6,5},{7,4},{8,11},{9,10},{10,... | collective-permute-start | bytes 786440 | tf_op jit(solution)/shard_map/ppermute | solution.py:194
  43.9 9.0 %collective-permute-start.6 = (bf16[1,512,256]{2,1,0:T(8,128)(2,1)S(1)}, bf16[1,512,256]{2,1,0:T(8,128)(2,1)}, u32[]{:S(2)}, u32[]{:S(2)}) collective-permute-start(bf16[1,512,256]{2,1,0:T(8,128)(2,1)S(1)} %get-tuple-element.34), channel_id=1, source_target_pairs={{0,12},{1,13},{2,14},{3,15},{4,8},{5,9},{6,10},{7,11},{8,4},{9,5},... | collective-permute-start | bytes 786440 | tf_op jit(solution)/shard_map/ppermute | solution.py:194
  45.5 9.3 %collective-permute-start.5 = (bf16[1,512,256]{2,1,0:T(8,128)(2,1)}, bf16[1,512,256]{2,1,0:T(8,128)(2,1)}, u32[]{:S(2)}, u32[]{:S(2)}) collective-permute-start(bf16[1,512,256]{2,1,0:T(8,128)(2,1)} %get-tuple-element.35), channel_id=1, source_target_pairs={{0,1},{1,0},{2,3},{3,2},{4,5},{5,4},{6,7},{7,6},{8,9},{9,8},{10,11... | collective-permute-start | bytes 786440 | tf_op jit(solution)/shard_map/ppermute | solution.py:194
  45.6 11.1 %collective-permute-start.4 = (bf16[1,512,256]{2,1,0:T(8,128)(2,1)S(1)}, bf16[1,512,256]{2,1,0:T(8,128)(2,1)S(1)}, u32[]{:S(2)}, u32[]{:S(2)}) collective-permute-start(bf16[1,512,256]{2,1,0:T(8,128)(2,1)S(1)} %get-tuple-element.36), channel_id=1, source_target_pairs={{0,4},{1,5},{2,6},{3,7},{4,0},{5,1},{6,2},{7,3},{8,12},{9,13},{10,... | collective-permute-start | bytes 786440 | tf_op jit(solution)/shard_map/ppermute | solution.py:194
  57.5 14.3 %collective-permute-start.8 = (bf16[2,512,256]{2,1,0:T(8,128)(2,1)}, bf16[2,512,256]{2,1,0:T(8,128)(2,1)}, u32[]{:S(2)}, u32[]{:S(2)}) collective-permute-start(bf16[2,512,256]{2,1,0:T(8,128)(2,1)} %pad_maximum_fusion.4), channel_id=1, source_target_pairs={{0,12},{1,13},{2,14},{3,15},{4,8},{5,9},{6,10},{7,11},{8,4},{9,5},... | collective-permute-start | bytes 1572872 | tf_op jit(solution)/shard_map/ppermute | solution.py:194
  58.2 15.8 %collective-permute-start.9 = (bf16[2,512,256]{2,1,0:T(8,128)(2,1)}, bf16[2,512,256]{2,1,0:T(8,128)(2,1)}, u32[]{:S(2)}, u32[]{:S(2)}) collective-permute-start(bf16[2,512,256]{2,1,0:T(8,128)(2,1)} %pad_maximum_fusion.5), channel_id=1, source_target_pairs={{0,3},{1,2},{2,1},{3,0},{4,7},{5,6},{6,5},{7,4},{8,11},{9,10},{10,... | collective-permute-start | bytes 1572872 | tf_op jit(solution)/shard_map/ppermute | solution.py:194
  59.7 16.7 %collective-permute-start.10 = (bf16[2,512,256]{2,1,0:T(8,128)(2,1)S(1)}, bf16[2,512,256]{2,1,0:T(8,128)(2,1)}, u32[]{:S(2)}, u32[]{:S(2)}) collective-permute-start(bf16[2,512,256]{2,1,0:T(8,128)(2,1)S(1)} %pad_maximum_fusion.6), channel_id=1, source_target_pairs={{0,4},{1,5},{2,6},{3,7},{4,0},{5,1},{6,2},{7,3},{8,12},{9,13},{10,... | collective-permute-start | bytes 1572872 | tf_op jit(solution)/shard_map/ppermute | solution.py:194
  62.2 16.4 %collective-permute-start.11 = (bf16[2,512,256]{2,1,0:T(8,128)(2,1)S(1)}, bf16[2,512,256]{2,1,0:T(8,128)(2,1)S(1)}, u32[]{:S(2)}, u32[]{:S(2)}) collective-permute-start(bf16[2,512,256]{2,1,0:T(8,128)(2,1)S(1)} %pad_maximum_fusion.7), channel_id=1, source_target_pairs={{0,1},{1,0},{2,3},{3,2},{4,5},{5,4},{6,7},{7,6},{8,9},{9,8},{10,11... | collective-permute-start | bytes 1572872 | tf_op jit(solution)/shard_map/ppermute | solution.py:194
  79.7 25.9 %collective-permute-start.13 = (bf16[4,512,256]{2,1,0:T(8,128)(2,1)}, bf16[4,512,256]{2,1,0:T(8,128)(2,1)}, u32[]{:S(2)}, u32[]{:S(2)}) collective-permute-start(bf16[4,512,256]{2,1,0:T(8,128)(2,1)} %pad_maximum_fusion), channel_id=1, source_target_pairs={{0,3},{1,2},{2,1},{3,0},{4,7},{5,6},{6,5},{7,4},{8,11},{9,10},{10,... | collective-permute-start | bytes 3145736 | tf_op jit(solution)/shard_map/ppermute | solution.py:194
  80.9 26.4 %collective-permute-start.12 = (bf16[4,512,256]{2,1,0:T(8,128)(2,1)}, bf16[4,512,256]{2,1,0:T(8,128)(2,1)}, u32[]{:S(2)}, u32[]{:S(2)}) collective-permute-start(bf16[4,512,256]{2,1,0:T(8,128)(2,1)} %pad_maximum_fusion), channel_id=1, source_target_pairs={{0,1},{1,0},{2,3},{3,2},{4,5},{5,4},{6,7},{7,6},{8,9},{9,8},{10,11... | collective-permute-start | bytes 3145736 | tf_op jit(solution)/shard_map/ppermute | solution.py:194
  83.3 26.6 %collective-permute-start.16 = (bf16[4,512,256]{2,1,0:T(8,128)(2,1)}, bf16[4,512,256]{2,1,0:T(8,128)(2,1)}, u32[]{:S(2)}, u32[]{:S(2)}) collective-permute-start(bf16[4,512,256]{2,1,0:T(8,128)(2,1)} %pad_maximum_fusion.1), channel_id=1, source_target_pairs={{0,12},{1,13},{2,14},{3,15},{4,8},{5,9},{6,10},{7,11},{8,4},{9,5},... | collective-permute-start | bytes 3145736 | tf_op jit(solution)/shard_map/ppermute | solution.py:194
  84.8 28.6 %collective-permute-start.15 = (bf16[4,512,256]{2,1,0:T(8,128)(2,1)}, bf16[4,512,256]{2,1,0:T(8,128)(2,1)}, u32[]{:S(2)}, u32[]{:S(2)}) collective-permute-start(bf16[4,512,256]{2,1,0:T(8,128)(2,1)} %pad_maximum_fusion.1), channel_id=1, source_target_pairs={{0,4},{1,5},{2,6},{3,7},{4,0},{5,1},{6,2},{7,3},{8,12},{9,13},{10,... | collective-permute-start | bytes 3145736 | tf_op jit(solution)/shard_map/ppermute | solution.py:194
  88.1 39.8 %collective-permute-start.19 = (bf16[4,512,256]{2,1,0:T(8,128)(2,1)}, bf16[4,512,256]{2,1,0:T(8,128)(2,1)}, u32[]{:S(2)}, u32[]{:S(2)}) collective-permute-start(bf16[4,512,256]{2,1,0:T(8,128)(2,1)} %pad_maximum_fusion.2), channel_id=1, source_target_pairs={{0,1},{1,0},{2,3},{3,2},{4,5},{5,4},{6,7},{7,6},{8,9},{9,8},{10,11... | collective-permute-start | bytes 3145736 | tf_op jit(solution)/shard_map/ppermute | solution.py:194
  105.6 27.6 %collective-permute-start.18 = (bf16[4,512,256]{2,1,0:T(8,128)(2,1)}, bf16[4,512,256]{2,1,0:T(8,128)(2,1)}, u32[]{:S(2)}, u32[]{:S(2)}) collective-permute-start(bf16[4,512,256]{2,1,0:T(8,128)(2,1)} %pad_maximum_fusion.2), channel_id=1, source_target_pairs={{0,3},{1,2},{2,1},{3,0},{4,7},{5,6},{6,5},{7,4},{8,11},{9,10},{10,... | collective-permute-start | bytes 3145736 | tf_op jit(solution)/shard_map/ppermute | solution.py:194
  107.3 25.9 %collective-permute-start.21 = (bf16[4,512,256]{2,1,0:T(8,128)(2,1)}, bf16[4,512,256]{2,1,0:T(8,128)(2,1)}, u32[]{:S(2)}, u32[]{:S(2)}) collective-permute-start(bf16[4,512,256]{2,1,0:T(8,128)(2,1)} %pad_maximum_fusion.3), channel_id=1, source_target_pairs={{0,12},{1,13},{2,14},{3,15},{4,8},{5,9},{6,10},{7,11},{8,4},{9,5},... | collective-permute-start | bytes 3145736 | tf_op jit(solution)/shard_map/ppermute | solution.py:194
  109.9 28.6 %collective-permute-start.22 = (bf16[4,512,256]{2,1,0:T(8,128)(2,1)}, bf16[4,512,256]{2,1,0:T(8,128)(2,1)}, u32[]{:S(2)}, u32[]{:S(2)}) collective-permute-start(bf16[4,512,256]{2,1,0:T(8,128)(2,1)} %pad_maximum_fusion.3), channel_id=1, source_target_pairs={{0,4},{1,5},{2,6},{3,7},{4,0},{5,1},{6,2},{7,3},{8,12},{9,13},{10,... | collective-permute-start | bytes 3145736 | tf_op jit(solution)/shard_map/ppermute | solution.py:194
  113.4 39.6 %collective-permute-start.14 = (bf16[4,512,256]{2,1,0:T(8,128)(2,1)}, bf16[4,512,256]{2,1,0:T(8,128)(2,1)}, u32[]{:S(2)}, u32[]{:S(2)}) collective-permute-start(bf16[4,512,256]{2,1,0:T(8,128)(2,1)} %collective-permute-done.12), channel_id=1, source_target_pairs={{0,3},{1,2},{2,1},{3,0},{4,7},{5,6},{6,5},{7,4},{8,11},{9,10},{10,... | collective-permute-start | bytes 3145736 | tf_op jit(solution)/shard_map/ppermute | solution.py:194
  128.0 25.2 %collective-permute-start.17 = (bf16[4,512,256]{2,1,0:T(8,128)(2,1)}, bf16[4,512,256]{2,1,0:T(8,128)(2,1)}, u32[]{:S(2)}, u32[]{:S(2)}) collective-permute-start(bf16[4,512,256]{2,1,0:T(8,128)(2,1)} %collective-permute-done.15), channel_id=1, source_target_pairs={{0,12},{1,13},{2,14},{3,15},{4,8},{5,9},{6,10},{7,11},{8,4},{9,5},... | collective-permute-start | bytes 3145736 | tf_op jit(solution)/shard_map/ppermute | solution.py:194
  133.2 20.1 %collective-permute-start.20 = (bf16[4,512,256]{2,1,0:T(8,128)(2,1)}, bf16[4,512,256]{2,1,0:T(8,128)(2,1)}, u32[]{:S(2)}, u32[]{:S(2)}) collective-permute-start(bf16[4,512,256]{2,1,0:T(8,128)(2,1)} %collective-permute-done.18), channel_id=1, source_target_pairs={{0,1},{1,0},{2,3},{3,2},{4,5},{5,4},{6,7},{7,6},{8,9},{9,8},{10,11... | collective-permute-start | bytes 3145736 | tf_op jit(solution)/shard_map/ppermute | solution.py:194
  133.2 24.8 %collective-permute-start.23 = (bf16[4,512,256]{2,1,0:T(8,128)(2,1)}, bf16[4,512,256]{2,1,0:T(8,128)(2,1)}, u32[]{:S(2)}, u32[]{:S(2)}) collective-permute-start(bf16[4,512,256]{2,1,0:T(8,128)(2,1)} %collective-permute-done.21), channel_id=1, source_target_pairs={{0,4},{1,5},{2,6},{3,7},{4,0},{5,1},{6,2},{7,3},{8,12},{9,13},{10,... | collective-permute-start | bytes 3145736 | tf_op jit(solution)/shard_map/ppermute | solution.py:194
  (13 other events, 292.9 us)

commit v4 on v3

--- a/solution.py
+++ b/solution.py
@@ -7,6 +7,7 @@
 
 NT = (((1,), (1,)), ((), ()))
 MIB = 2**20
+UNROLL = 4
 MASKS = ((4, 12, 1, 3), (1, 3, 4, 12), (12, 4, 3, 1), (3, 1, 12, 4))
 
 
@@ -26,9 +27,9 @@
         return count + hit.astype(jnp.int32)
 
     count = lax.fori_loop(0, 64, entry, 0)
-    for k in range(4):
+    for k in range(UNROLL):
         order[count + k] = -1
-    return (count + 3) // 4
+    return (count + UNROLL - 1) // UNROLL
 
 
 def pair_kernel(idx, wts, slot, dsum, vrow, vcol, *refs):
@@ -42,7 +43,7 @@
     ]
     for copy in copies:
         copy.start()
-    fours = listed(wts, order)
+    trips = listed(wts, order)
     vsum[...] = vrow[...] + vcol[...]
 
     def clear(s, carry):
@@ -59,8 +60,8 @@
         return lax.dot_general(left, right, NT, preferred_element_type=jnp.float32)
 
     def coupled(g, carry):
-        for u in range(4):
-            entry = order[4 * g + u]
+        for u in range(UNROLL):
+            entry = order[UNROLL * g + u]
             n = jnp.maximum(entry, 0)
             weight = jnp.where(entry >= 0, wts[64 + n], 0.0)
             start = -(product(32 + n) * recip(vsum[...] - dsum[32 + n]))
@@ -69,19 +70,19 @@
         return carry
 
     def received(g, carry):
-        for u in range(4):
-            s = 4 * g + u
+        for u in range(UNROLL):
+            s = UNROLL * g + u
             value = (mixed[s] - product(16 + s)) * recip(vsum[...] - dsum[16 + s])
             amp[s] = value.astype(jnp.bfloat16)
         return carry
 
     def out_copy(g):
-        rows = pl.ds(4 * g, 4)
+        rows = pl.ds(UNROLL * g, UNROLL)
         return pltpu.make_async_copy(mixed.at[rows], out.at[rows], out_sems.at[g])
 
     def own(g, carry):
-        for u in range(4):
-            p = 4 * g + u
+        for u in range(UNROLL):
+            p = UNROLL * g + u
             total = -product(p)
             for e in range(4):
                 total += wts[4 * p + e] * amp[slot[4 * p + e]].astype(jnp.float32)
@@ -93,10 +94,10 @@
         out_copy(g).wait()
         return carry
 
-    lax.fori_loop(0, fours, coupled, 0)
-    lax.fori_loop(0, 4, received, 0)
-    lax.fori_loop(0, 4, own, 0)
-    lax.fori_loop(0, 4, finish, 0)
+    lax.fori_loop(0, trips, coupled, 0)
+    lax.fori_loop(0, 16 // UNROLL, received, 0)
+    lax.fori_loop(0, 16 // UNROLL, own, 0)
+    lax.fori_loop(0, 16 // UNROLL, finish, 0)
 
 
 SMEM = pl.BlockSpec(memory_space=pltpu.SMEM)
@@ -115,7 +116,7 @@
             pltpu.VMEM((16, 256, 256), jnp.float32),
             pltpu.VMEM((16, 256, 256), jnp.bfloat16),
             pltpu.VMEM((256, 256), jnp.float32),
-            pltpu.SMEM((68,), jnp.int32),
+            pltpu.SMEM((72,), jnp.int32),
             pltpu.SemaphoreType.DMA((16,)),
             pltpu.SemaphoreType.DMA((4,)),
         ],
@@ -192,6 +193,49 @@
 
 def swap(block, mask):
     return lax.ppermute(block, "grp", [(g, g ^ mask) for g in range(16)])
+
+
+def join_kernel(*refs):
+    held, got, joined = refs[:4], refs[4:8], refs[8:12]
+    whole, in_sems, out_sems = refs[12:16], refs[16], refs[17]
+    count = held[0].shape[0]
+
+    def in_copies(q):
+        return [
+            pltpu.make_async_copy(
+                source[q], whole[q].at[pl.ds(part * count, count)], in_sems.at[2 * q + part]
+            )
+            for part, source in enumerate((held, got))
+        ]
+
+    copies = [in_copies(q) for q in range(4)]
+    outs = [pltpu.make_async_copy(whole[q], joined[q], out_sems.at[q]) for q in range(4)]
+    for pair in copies:
+        for copy in pair:
+            copy.start()
+    for pair, out in zip(copies, outs):
+        for copy in pair:
+            copy.wait()
+        out.start()
+    for out in outs:
+        out.wait()
+
+
+def join(held, got, grant):
+    count, rows, columns = held[0].shape
+    shape = (2 * count, rows, columns)
+    return pl.pallas_call(
+        join_kernel,
+        in_specs=[HBM] * 8,
+        out_specs=[HBM] * 4,
+        out_shape=[jax.ShapeDtypeStruct(shape, jnp.bfloat16)] * 4,
+        scratch_shapes=[pltpu.VMEM(shape, jnp.bfloat16)] * 4
+        + [pltpu.SemaphoreType.DMA((8,)), pltpu.SemaphoreType.DMA((4,))],
+        compiler_params=pltpu.CompilerParams(vmem_limit_bytes=grant * MIB),
+        cost_estimate=pl.CostEstimate(
+            flops=0, bytes_accessed=16 * count * rows * columns * 2, transcendentals=0
+        ),
+    )(*held, *got)
 
 
 def on_device(
@@ -217,8 +261,7 @@
     held = [fitted[None, :, 256 * q : 256 * q + 256] for q in range(4)]
     for step in range(2):
         got = [swap(held[q], MASKS[q][step]) for q in range(4)]
-        held = [jnp.concatenate([a, b], axis=0) for a, b in zip(held, got)]
-        held = list(lax.optimization_barrier(tuple(held)))
+        held = join(held, got, (16, 58)[step])
     third = [swap(held[q], MASKS[q][2]) for q in range(4)]
     early = [swap(held[q], MASKS[q][3]) for q in range(4)]
     late = [swap(third[q], MASKS[q][3]) for q in range(4)]

time: 185 us -> 180 us (0.973)
  other arithmetic: 16.3 us -> 3.74 us
  Pallas kernels: 26.4 us -> 33.1 us
    concatenate x8 -> x0, other arithmetic: 12.6 us -> none  [on_device(): held = [jnp.concatenate([a, b], axis=0) for a, b in zip(held, got)]]
    pallas_call x0 -> x2, Pallas kernels: none -> 5.8 us  [join(): pl.pallas_call(join_kernel, in_specs=[HBM] * 8, out_specs=[HBM] * 4, out_...]
  transfers between devices with their start and end apart: 25 -> 25, of which waited for: 17 -> 20; matrix products, arithmetic and copies ran while one was open for 10% -> 5% of each run, Pallas kernels for 0% -> 0%
where the time goes in v4:
time: 180 us; the launch traced here: 179 us
  waiting for transfers between devices  87.1 us (48%)
  starting transfers between devices  45.5 us (25%)
  Pallas kernels  33.1 us (18%)
  local copies, waits for them, and re-layouts  6.66 us (4%)
  other arithmetic  3.74 us (2%)
  matrix products  2.71 us (2%)
    ppermute x24, waiting for transfers between devices, swap(): return lax.ppermute(block, 'grp', [(g, g ^ mask) for g in range(16)])  76.8 us
    ppermute x24, starting transfers between devices, swap(): return lax.ppermute(block, 'grp', [(g, g ^ mask) for g in range(16)])  37 us
    pallas_call x1, Pallas kernels, amplitudes(): pl.pallas_call(pair_kernel, in_specs=[SMEM] * 4 + [VMEM] * 2 + [HBM] * 16...  27.3 us
    all_to_all x1, waiting for transfers between devices, on_device(): block = lax.all_to_all(rows, 'aux', split_axis=0, concat_axis=0, tiled=True)  10.3 us
    all_to_all x1, starting transfers between devices, on_device(): block = lax.all_to_all(rows, 'aux', split_axis=0, concat_axis=0, tiled=True)  8.57 us
    pallas_call x2, Pallas kernels, join(): pl.pallas_call(join_kernel, in_specs=[HBM] * 8, out_specs=[HBM] * 4, out_...  5.8 us
  transfers between devices with their start and end apart: 25, of which 20 were waited for; matrix products, arithmetic and copies ran while one was open for 5% of the time, Pallas kernels for 0%

profile of v4, /device:TPU:2, one launch (start us, length us, event | category | flops | bytes accessed | tf_op | source)
XLA Modules:
  0.0 179.3 jit_solution(4731285229744847492)
XLA Ops:
  3.2 8.6 %all-to-all-start = ((bf16[16,64,512]{2,1,0:T(8,128)(2,1)}), bf16[16,64,512]{2,1,0:T(8,128)(2,1)S(1)}, u32[]{:S(2)}, u32[]{:S(2)}) async-start(bf16[16,64,512]{2,1,0:T(8,128)(2,1)} %copy.70), calls=%async_computation | async-start | bytes 2097152 | tf_op jit(solution)/shard_map/all_to_all | solution.py:252
  12.6 3.0 %collective-permute-done = s32[1,176]{1,0:T(1,128)S(1)} collective-permute-done((s32[1,176]{1,0:T(1,128)S(1)}, s32[1,176]{1,0:T(1,128)S(1)}, u32[]{:S(2)}, u32[]{:S(2)}) %collective-permute-start) | collective-permute-done | bytes 736 | tf_op jit(solution)/shard_map/ppermute | solution.py:195
  17.3 2.1 %collective-permute-done.1 = s32[2,176]{1,0:T(2,128)S(1)} collective-permute-done((s32[2,176]{1,0:T(2,128)S(1)}, s32[2,176]{1,0:T(2,128)S(1)}, u32[]{:S(2)}, u32[]{:S(2)}) %collective-permute-start.1) | collective-permute-done | bytes 1440 | tf_op jit(solution)/shard_map/ppermute | solution.py:195
  21.0 2.0 %collective-permute-done.2 = s32[4,176]{1,0:T(4,128)S(1)} collective-permute-done((s32[4,176]{1,0:T(4,128)S(1)}, s32[4,176]{1,0:T(4,128)S(1)}, u32[]{:S(2)}, u32[]{:S(2)}) %collective-permute-start.2) | collective-permute-done | bytes 2848 | tf_op jit(solution)/shard_map/ppermute | solution.py:195
  23.1 3.0 %collective-permute-start.3 = (s32[8,176]{1,0:T(8,128)S(1)}, s32[8,176]{1,0:T(8,128)S(1)}, u32[]{:S(2)}, u32[]{:S(2)}) collective-permute-start(s32[8,176]{1,0:T(8,128)S(1)} %pad_add_fusion.2), channel_id=1, source_target_pairs={{0,3},{1,2},{2,1},{3,0},{4,7},{5,6},{6,5},{7,4},{8,11},{9,10},{10,... | collective-permute-start | bytes 16904 | tf_op jit(solution)/shard_map/ppermute | solution.py:195
  26.2 1.8 %collective-permute-done.3 = s32[8,176]{1,0:T(8,128)S(1)} collective-permute-done((s32[8,176]{1,0:T(8,128)S(1)}, s32[8,176]{1,0:T(8,128)S(1)}, u32[]{:S(2)}, u32[]{:S(2)}) %collective-permute-start.3) | collective-permute-done | bytes 5664 | tf_op jit(solution)/shard_map/ppermute | solution.py:195
  28.1 10.3 %all-to-all-done = bf16[16,64,512]{2,1,0:T(8,128)(2,1)S(1)} async-done(((bf16[16,64,512]{2,1,0:T(8,128)(2,1)}), bf16[16,64,512]{2,1,0:T(8,128)(2,1)S(1)}, u32[]{:S(2)}, u32[]{:S(2)}) %all-to-all-start) | async-done | bytes 1048608 | tf_op jit(solution)/shard_map/all_to_all | solution.py:252
  39.8 3.1 %collective-permute-start.7 = (bf16[1,512,256]{2,1,0:T(8,128)(2,1)S(1)}, bf16[1,512,256]{2,1,0:T(8,128)(2,1)S(1)}, u32[]{:S(2)}, u32[]{:S(2)}) collective-permute-start(bf16[1,512,256]{2,1,0:T(8,128)(2,1)S(1)} %get-tuple-element.33.refs_3_), channel_id=1, source_target_pairs={{0,3},{1,2},{2,1},{3,0},{4,7},{5,6},{6,5},{7,4},{8,11},{9,10},{10,... | collective-permute-start | bytes 786440 | tf_op jit(solution)/shard_map/ppermute | solution.py:195
  47.0 2.5 %collective-permute-done.7.refs_7_ = bf16[1,512,256]{2,1,0:T(8,128)(2,1)S(1)} collective-permute-done((bf16[1,512,256]{2,1,0:T(8,128)(2,1)S(1)}, bf16[1,512,256]{2,1,0:T(8,128)(2,1)S(1)}, u32[]{:S(2)}, u32[]{:S(2)}) %collective-permute-start.7) | collective-permute-done | bytes 262176 | tf_op jit(solution)/shard_map/ppermute | solution.py:195
  49.5 2.3 %collective-permute-done.6.refs_6_ = bf16[1,512,256]{2,1,0:T(8,128)(2,1)} collective-permute-done((bf16[1,512,256]{2,1,0:T(8,128)(2,1)S(1)}, bf16[1,512,256]{2,1,0:T(8,128)(2,1)}, u32[]{:S(2)}, u32[]{:S(2)}) %collective-permute-start.6) | collective-permute-done | bytes 262176 | tf_op jit(solution)/shard_map/ppermute | solution.py:195
  53.7 2.4 %shard_map.127 = (bf16[2,512,256]{2,1,0:T(8,128)(2,1)}, bf16[2,512,256]{2,1,0:T(8,128)(2,1)}, bf16[2,512,256]{2,1,0:T(8,128)(2,1)}, bf16[2,512,256]{2,1,0:T(8,128)(2,1)}) custom-call(bf16[1,512,256]{2,1,0:T(8,128)(2,1)S(1)} %get-tuple-element.36.refs_0_, bf16[1,512,256]{2,1,0:T(8,128)(2,1)S(1)} %get-tuple-element.35.refs_1_, ...), custom_call_target="tpu_custom_call" | custom-call | bytes 4194304 | tf_op jit(solution)/shard_map/pallas_call | solution.py:227
  61.9 8.5 %collective-permute-done.8.refs_4_ = bf16[2,512,256]{2,1,0:T(8,128)(2,1)S(1)} collective-permute-done((bf16[2,512,256]{2,1,0:T(8,128)(2,1)}, bf16[2,512,256]{2,1,0:T(8,128)(2,1)S(1)}, u32[]{:S(2)}, u32[]{:S(2)}) %collective-permute-start.8) | collective-permute-done | bytes 524320 | tf_op jit(solution)/shard_map/ppermute | solution.py:195
  72.8 3.4 %shard_map.128 = (bf16[4,512,256]{2,1,0:T(8,128)(2,1)}, bf16[4,512,256]{2,1,0:T(8,128)(2,1)}, bf16[4,512,256]{2,1,0:T(8,128)(2,1)}, bf16[4,512,256]{2,1,0:T(8,128)(2,1)}) custom-call(bf16[2,512,256]{2,1,0:T(8,128)(2,1)} %get-tuple-element.17.refs_0_, bf16[2,512,256]{2,1,0:T(8,128)(2,1)} %get-tuple-element.18.refs_1_, ...), custom_call_target="tpu_custom_call" | custom-call | bytes 8388608 | tf_op jit(solution)/shard_map/pallas_call | solution.py:227
  76.2 2.8 %collective-permute-start.13 = (bf16[4,512,256]{2,1,0:T(8,128)(2,1)}, bf16[4,512,256]{2,1,0:T(8,128)(2,1)}, u32[]{:S(2)}, u32[]{:S(2)}) collective-permute-start(bf16[4,512,256]{2,1,0:T(8,128)(2,1)} %get-tuple-element.21), channel_id=1, source_target_pairs={{0,3},{1,2},{2,1},{3,0},{4,7},{5,6},{6,5},{7,4},{8,11},{9,10},{10,... | collective-permute-start | bytes 3145736 | tf_op jit(solution)/shard_map/ppermute | solution.py:195
  81.7 2.2 %collective-permute-start.16 = (bf16[4,512,256]{2,1,0:T(8,128)(2,1)}, bf16[4,512,256]{2,1,0:T(8,128)(2,1)S(1)}, u32[]{:S(2)}, u32[]{:S(2)}) collective-permute-start(bf16[4,512,256]{2,1,0:T(8,128)(2,1)} %get-tuple-element.22), channel_id=1, source_target_pairs={{0,12},{1,13},{2,14},{3,15},{4,8},{5,9},{6,10},{7,11},{8,4},{9,5},... | collective-permute-start | bytes 3145736 | tf_op jit(solution)/shard_map/ppermute | solution.py:195
  86.3 15.5 %collective-permute-done.13 = bf16[4,512,256]{2,1,0:T(8,128)(2,1)} collective-permute-done((bf16[4,512,256]{2,1,0:T(8,128)(2,1)}, bf16[4,512,256]{2,1,0:T(8,128)(2,1)}, u32[]{:S(2)}, u32[]{:S(2)}) %collective-permute-start.13) | collective-permute-done | bytes 1048608 | tf_op jit(solution)/shard_map/ppermute | solution.py:195
  101.8 2.3 %collective-permute-start.18 = (bf16[4,512,256]{2,1,0:T(8,128)(2,1)}, bf16[4,512,256]{2,1,0:T(8,128)(2,1)}, u32[]{:S(2)}, u32[]{:S(2)}) collective-permute-start(bf16[4,512,256]{2,1,0:T(8,128)(2,1)} %get-tuple-element.23), channel_id=1, source_target_pairs={{0,3},{1,2},{2,1},{3,0},{4,7},{5,6},{6,5},{7,4},{8,11},{9,10},{10,... | collective-permute-start | bytes 3145736 | tf_op jit(solution)/shard_map/ppermute | solution.py:195
  109.5 2.2 %collective-permute-start.14 = (bf16[4,512,256]{2,1,0:T(8,128)(2,1)}, bf16[4,512,256]{2,1,0:T(8,128)(2,1)}, u32[]{:S(2)}, u32[]{:S(2)}) collective-permute-start(bf16[4,512,256]{2,1,0:T(8,128)(2,1)} %collective-permute-done.12), channel_id=1, source_target_pairs={{0,3},{1,2},{2,1},{3,0},{4,7},{5,6},{6,5},{7,4},{8,11},{9,10},{10,... | collective-permute-start | bytes 3145736 | tf_op jit(solution)/shard_map/ppermute | solution.py:195
  111.7 13.3 %collective-permute-done.19 = bf16[4,512,256]{2,1,0:T(8,128)(2,1)} collective-permute-done((bf16[4,512,256]{2,1,0:T(8,128)(2,1)}, bf16[4,512,256]{2,1,0:T(8,128)(2,1)}, u32[]{:S(2)}, u32[]{:S(2)}) %collective-permute-start.19) | collective-permute-done | bytes 1048608 | tf_op jit(solution)/shard_map/ppermute | solution.py:195
  126.8 2.6 %collective-permute-done.18 = bf16[4,512,256]{2,1,0:T(8,128)(2,1)} collective-permute-done((bf16[4,512,256]{2,1,0:T(8,128)(2,1)}, bf16[4,512,256]{2,1,0:T(8,128)(2,1)}, u32[]{:S(2)}, u32[]{:S(2)}) %collective-permute-start.18) | collective-permute-done | bytes 1048608 | tf_op jit(solution)/shard_map/ppermute | solution.py:195
  130.0 2.9 %collective-permute-start.23 = (bf16[4,512,256]{2,1,0:T(8,128)(2,1)}, bf16[4,512,256]{2,1,0:T(8,128)(2,1)}, u32[]{:S(2)}, u32[]{:S(2)}) collective-permute-start(bf16[4,512,256]{2,1,0:T(8,128)(2,1)} %collective-permute-done.21), channel_id=1, source_target_pairs={{0,4},{1,5},{2,6},{3,7},{4,0},{5,1},{6,2},{7,3},{8,12},{9,13},{10,... | collective-permute-start | bytes 3145736 | tf_op jit(solution)/shard_map/ppermute | solution.py:195
  135.2 13.6 %collective-permute-done.14 = bf16[4,512,256]{2,1,0:T(8,128)(2,1)} collective-permute-done((bf16[4,512,256]{2,1,0:T(8,128)(2,1)}, bf16[4,512,256]{2,1,0:T(8,128)(2,1)}, u32[]{:S(2)}, u32[]{:S(2)}) %collective-permute-start.14) | collective-permute-done | bytes 1048608 | tf_op jit(solution)/shard_map/ppermute | solution.py:195
  150.1 1.8 %collective-permute-done.23 = bf16[4,512,256]{2,1,0:T(8,128)(2,1)} collective-permute-done((bf16[4,512,256]{2,1,0:T(8,128)(2,1)}, bf16[4,512,256]{2,1,0:T(8,128)(2,1)}, u32[]{:S(2)}, u32[]{:S(2)}) %collective-permute-start.23) | collective-permute-done | bytes 1048608 | tf_op jit(solution)/shard_map/ppermute | solution.py:195
  151.9 27.3 %shard_map.129 = f32[16,256,256]{2,1,0:T(8,128)} custom-call(s32[4,192]{1,0:T(4,128)} %fusion.4.idx, f32[128]{0:T(128)} %pad_maximum_fusion.wts, s32[64]{0:T(128)} %select_reduce_fusion.9.slot, f32[96]{0:T(128)} %add_bitcast_fusion.dsum, f32[1,256]{1,0:T(1,128)} %bitcast.65, f32[256,1]{1,0:T(8,128)} %copy.82.vcol, bf16[8,256,256]{2,1,0:T(8,128)(2,1)} %bitcast.67, ...), custom_call_target="tpu_custom_call" | custom-call | flops 12884901888 | bytes 20971520 | tf_op jit(solution)/shard_map/pallas_call | solution.py:109
  (123 shorter events, 39.2 us)
Async XLA Ops:
  3.2 35.2 %all-to-all-start = ((bf16[16,64,512]{2,1,0:T(8,128)(2,1)}), bf16[16,64,512]{2,1,0:T(8,128)(2,1)S(1)}, u32[]{:S(2)}, u32[]{:S(2)}) async-start(bf16[16,64,512]{2,1,0:T(8,128)(2,1)} %copy.70), calls=%async_computation | async-start | bytes 2097152 | tf_op jit(solution)/shard_map/all_to_all | solution.py:252
  15.7 3.6 %collective-permute-start.1 = (s32[2,176]{1,0:T(2,128)S(1)}, s32[2,176]{1,0:T(2,128)S(1)}, u32[]{:S(2)}, u32[]{:S(2)}) collective-permute-start(s32[2,176]{1,0:T(2,128)S(1)} %pad_add_fusion.4), channel_id=1, source_target_pairs={{0,12},{1,13},{2,14},{3,15},{4,8},{5,9},{6,10},{7,11},{8,4},{9,5},... | collective-permute-start | bytes 4232 | tf_op jit(solution)/shard_map/ppermute | solution.py:195
  19.4 3.6 %collective-permute-start.2 = (s32[4,176]{1,0:T(4,128)S(1)}, s32[4,176]{1,0:T(4,128)S(1)}, u32[]{:S(2)}, u32[]{:S(2)}) collective-permute-start(s32[4,176]{1,0:T(4,128)S(1)} %pad_add_fusion.3), channel_id=1, source_target_pairs={{0,1},{1,0},{2,3},{3,2},{4,5},{5,4},{6,7},{7,6},{8,9},{9,8},{10,11... | collective-permute-start | bytes 8456 | tf_op jit(solution)/shard_map/ppermute | solution.py:195
  23.1 4.9 %collective-permute-start.3 = (s32[8,176]{1,0:T(8,128)S(1)}, s32[8,176]{1,0:T(8,128)S(1)}, u32[]{:S(2)}, u32[]{:S(2)}) collective-permute-start(s32[8,176]{1,0:T(8,128)S(1)} %pad_add_fusion.2), channel_id=1, source_target_pairs={{0,3},{1,2},{2,1},{3,0},{4,7},{5,6},{6,5},{7,4},{8,11},{9,10},{10,... | collective-permute-start | bytes 16904 | tf_op jit(solution)/shard_map/ppermute | solution.py:195
  39.8 9.7 %collective-permute-start.7 = (bf16[1,512,256]{2,1,0:T(8,128)(2,1)S(1)}, bf16[1,512,256]{2,1,0:T(8,128)(2,1)S(1)}, u32[]{:S(2)}, u32[]{:S(2)}) collective-permute-start(bf16[1,512,256]{2,1,0:T(8,128)(2,1)S(1)} %get-tuple-element.33.refs_3_), channel_id=1, source_target_pairs={{0,3},{1,2},{2,1},{3,0},{4,7},{5,6},{6,5},{7,4},{8,11},{9,10},{10,... | collective-permute-start | bytes 786440 | tf_op jit(solution)/shard_map/ppermute | solution.py:195
  42.9 8.9 %collective-permute-start.6 = (bf16[1,512,256]{2,1,0:T(8,128)(2,1)S(1)}, bf16[1,512,256]{2,1,0:T(8,128)(2,1)}, u32[]{:S(2)}, u32[]{:S(2)}) collective-permute-start(bf16[1,512,256]{2,1,0:T(8,128)(2,1)S(1)} %get-tuple-element.34.refs_2_), channel_id=1, source_target_pairs={{0,12},{1,13},{2,14},{3,15},{4,8},{5,9},{6,10},{7,11},{8,4},{9,5},... | collective-permute-start | bytes 786440 | tf_op jit(solution)/shard_map/ppermute | solution.py:195
  44.4 9.1 %collective-permute-start.5 = (bf16[1,512,256]{2,1,0:T(8,128)(2,1)S(1)}, bf16[1,512,256]{2,1,0:T(8,128)(2,1)}, u32[]{:S(2)}, u32[]{:S(2)}) collective-permute-start(bf16[1,512,256]{2,1,0:T(8,128)(2,1)S(1)} %get-tuple-element.35.refs_1_), channel_id=1, source_target_pairs={{0,1},{1,0},{2,3},{3,2},{4,5},{5,4},{6,7},{7,6},{8,9},{9,8},{10,11... | collective-permute-start | bytes 786440 | tf_op jit(solution)/shard_map/ppermute | solution.py:195
  44.5 9.2 %collective-permute-start.4 = (bf16[1,512,256]{2,1,0:T(8,128)(2,1)S(1)}, bf16[1,512,256]{2,1,0:T(8,128)(2,1)}, u32[]{:S(2)}, u32[]{:S(2)}) collective-permute-start(bf16[1,512,256]{2,1,0:T(8,128)(2,1)S(1)} %get-tuple-element.36.refs_0_), channel_id=1, source_target_pairs={{0,4},{1,5},{2,6},{3,7},{4,0},{5,1},{6,2},{7,3},{8,12},{9,13},{10,... | collective-permute-start | bytes 786440 | tf_op jit(solution)/shard_map/ppermute | solution.py:195
  56.2 14.2 %collective-permute-start.8 = (bf16[2,512,256]{2,1,0:T(8,128)(2,1)}, bf16[2,512,256]{2,1,0:T(8,128)(2,1)S(1)}, u32[]{:S(2)}, u32[]{:S(2)}) collective-permute-start(bf16[2,512,256]{2,1,0:T(8,128)(2,1)} %get-tuple-element.17.refs_0_), channel_id=1, source_target_pairs={{0,12},{1,13},{2,14},{3,15},{4,8},{5,9},{6,10},{7,11},{8,4},{9,5},... | collective-permute-start | bytes 1572872 | tf_op jit(solution)/shard_map/ppermute | solution.py:195
  56.8 15.1 %collective-permute-start.9 = (bf16[2,512,256]{2,1,0:T(8,128)(2,1)}, bf16[2,512,256]{2,1,0:T(8,128)(2,1)S(1)}, u32[]{:S(2)}, u32[]{:S(2)}) collective-permute-start(bf16[2,512,256]{2,1,0:T(8,128)(2,1)} %get-tuple-element.18.refs_1_), channel_id=1, source_target_pairs={{0,3},{1,2},{2,1},{3,0},{4,7},{5,6},{6,5},{7,4},{8,11},{9,10},{10,... | collective-permute-start | bytes 1572872 | tf_op jit(solution)/shard_map/ppermute | solution.py:195
  57.8 14.2 %collective-permute-start.10 = (bf16[2,512,256]{2,1,0:T(8,128)(2,1)}, bf16[2,512,256]{2,1,0:T(8,128)(2,1)}, u32[]{:S(2)}, u32[]{:S(2)}) collective-permute-start(bf16[2,512,256]{2,1,0:T(8,128)(2,1)} %get-tuple-element.19.refs_2_), channel_id=1, source_target_pairs={{0,4},{1,5},{2,6},{3,7},{4,0},{5,1},{6,2},{7,3},{8,12},{9,13},{10,... | collective-permute-start | bytes 1572872 | tf_op jit(solution)/shard_map/ppermute | solution.py:195
  59.5 13.3 %collective-permute-start.11 = (bf16[2,512,256]{2,1,0:T(8,128)(2,1)}, bf16[2,512,256]{2,1,0:T(8,128)(2,1)}, u32[]{:S(2)}, u32[]{:S(2)}) collective-permute-start(bf16[2,512,256]{2,1,0:T(8,128)(2,1)} %get-tuple-element.20.refs_3_), channel_id=1, source_target_pairs={{0,1},{1,0},{2,3},{3,2},{4,5},{5,4},{6,7},{7,6},{8,9},{9,8},{10,11... | collective-permute-start | bytes 1572872 | tf_op jit(solution)/shard_map/ppermute | solution.py:195
  76.2 25.6 %collective-permute-start.13 = (bf16[4,512,256]{2,1,0:T(8,128)(2,1)}, bf16[4,512,256]{2,1,0:T(8,128)(2,1)}, u32[]{:S(2)}, u32[]{:S(2)}) collective-permute-start(bf16[4,512,256]{2,1,0:T(8,128)(2,1)} %get-tuple-element.21), channel_id=1, source_target_pairs={{0,3},{1,2},{2,1},{3,0},{4,7},{5,6},{6,5},{7,4},{8,11},{9,10},{10,... | collective-permute-start | bytes 3145736 | tf_op jit(solution)/shard_map/ppermute | solution.py:195
  79.1 26.4 %collective-permute-start.12 = (bf16[4,512,256]{2,1,0:T(8,128)(2,1)}, bf16[4,512,256]{2,1,0:T(8,128)(2,1)}, u32[]{:S(2)}, u32[]{:S(2)}) collective-permute-start(bf16[4,512,256]{2,1,0:T(8,128)(2,1)} %get-tuple-element.21), channel_id=1, source_target_pairs={{0,1},{1,0},{2,3},{3,2},{4,5},{5,4},{6,7},{7,6},{8,9},{9,8},{10,11... | collective-permute-start | bytes 3145736 | tf_op jit(solution)/shard_map/ppermute | solution.py:195
  81.7 26.9 %collective-permute-start.16 = (bf16[4,512,256]{2,1,0:T(8,128)(2,1)}, bf16[4,512,256]{2,1,0:T(8,128)(2,1)S(1)}, u32[]{:S(2)}, u32[]{:S(2)}) collective-permute-start(bf16[4,512,256]{2,1,0:T(8,128)(2,1)} %get-tuple-element.22), channel_id=1, source_target_pairs={{0,12},{1,13},{2,14},{3,15},{4,8},{5,9},{6,10},{7,11},{8,4},{9,5},... | collective-permute-start | bytes 3145736 | tf_op jit(solution)/shard_map/ppermute | solution.py:195
  83.8 25.7 %collective-permute-start.15 = (bf16[4,512,256]{2,1,0:T(8,128)(2,1)}, bf16[4,512,256]{2,1,0:T(8,128)(2,1)}, u32[]{:S(2)}, u32[]{:S(2)}) collective-permute-start(bf16[4,512,256]{2,1,0:T(8,128)(2,1)} %get-tuple-element.22), channel_id=1, source_target_pairs={{0,4},{1,5},{2,6},{3,7},{4,0},{5,1},{6,2},{7,3},{8,12},{9,13},{10,... | collective-permute-start | bytes 3145736 | tf_op jit(solution)/shard_map/ppermute | solution.py:195
  84.7 40.3 %collective-permute-start.19 = (bf16[4,512,256]{2,1,0:T(8,128)(2,1)}, bf16[4,512,256]{2,1,0:T(8,128)(2,1)}, u32[]{:S(2)}, u32[]{:S(2)}) collective-permute-start(bf16[4,512,256]{2,1,0:T(8,128)(2,1)} %get-tuple-element.23), channel_id=1, source_target_pairs={{0,1},{1,0},{2,3},{3,2},{4,5},{5,4},{6,7},{7,6},{8,9},{9,8},{10,11... | collective-permute-start | bytes 3145736 | tf_op jit(solution)/shard_map/ppermute | solution.py:195
  101.8 27.6 %collective-permute-start.18 = (bf16[4,512,256]{2,1,0:T(8,128)(2,1)}, bf16[4,512,256]{2,1,0:T(8,128)(2,1)}, u32[]{:S(2)}, u32[]{:S(2)}) collective-permute-start(bf16[4,512,256]{2,1,0:T(8,128)(2,1)} %get-tuple-element.23), channel_id=1, source_target_pairs={{0,3},{1,2},{2,1},{3,0},{4,7},{5,6},{6,5},{7,4},{8,11},{9,10},{10,... | collective-permute-start | bytes 3145736 | tf_op jit(solution)/shard_map/ppermute | solution.py:195
  105.5 24.5 %collective-permute-start.21 = (bf16[4,512,256]{2,1,0:T(8,128)(2,1)}, bf16[4,512,256]{2,1,0:T(8,128)(2,1)}, u32[]{:S(2)}, u32[]{:S(2)}) collective-permute-start(bf16[4,512,256]{2,1,0:T(8,128)(2,1)} %get-tuple-element.24), channel_id=1, source_target_pairs={{0,12},{1,13},{2,14},{3,15},{4,8},{5,9},{6,10},{7,11},{8,4},{9,5},... | collective-permute-start | bytes 3145736 | tf_op jit(solution)/shard_map/ppermute | solution.py:195
  108.6 26.6 %collective-permute-start.22 = (bf16[4,512,256]{2,1,0:T(8,128)(2,1)}, bf16[4,512,256]{2,1,0:T(8,128)(2,1)}, u32[]{:S(2)}, u32[]{:S(2)}) collective-permute-start(bf16[4,512,256]{2,1,0:T(8,128)(2,1)} %get-tuple-element.24), channel_id=1, source_target_pairs={{0,4},{1,5},{2,6},{3,7},{4,0},{5,1},{6,2},{7,3},{8,12},{9,13},{10,... | collective-permute-start | bytes 3145736 | tf_op jit(solution)/shard_map/ppermute | solution.py:195
  109.5 39.2 %collective-permute-start.14 = (bf16[4,512,256]{2,1,0:T(8,128)(2,1)}, bf16[4,512,256]{2,1,0:T(8,128)(2,1)}, u32[]{:S(2)}, u32[]{:S(2)}) collective-permute-start(bf16[4,512,256]{2,1,0:T(8,128)(2,1)} %collective-permute-done.12), channel_id=1, source_target_pairs={{0,3},{1,2},{2,1},{3,0},{4,7},{5,6},{6,5},{7,4},{8,11},{9,10},{10,... | collective-permute-start | bytes 3145736 | tf_op jit(solution)/shard_map/ppermute | solution.py:195
  125.0 25.0 %collective-permute-start.17 = (bf16[4,512,256]{2,1,0:T(8,128)(2,1)}, bf16[4,512,256]{2,1,0:T(8,128)(2,1)}, u32[]{:S(2)}, u32[]{:S(2)}) collective-permute-start(bf16[4,512,256]{2,1,0:T(8,128)(2,1)} %collective-permute-done.15), channel_id=1, source_target_pairs={{0,12},{1,13},{2,14},{3,15},{4,8},{5,9},{6,10},{7,11},{8,4},{9,5},... | collective-permute-start | bytes 3145736 | tf_op jit(solution)/shard_map/ppermute | solution.py:195
  129.4 20.7 %collective-permute-start.20 = (bf16[4,512,256]{2,1,0:T(8,128)(2,1)}, bf16[4,512,256]{2,1,0:T(8,128)(2,1)}, u32[]{:S(2)}, u32[]{:S(2)}) collective-permute-start(bf16[4,512,256]{2,1,0:T(8,128)(2,1)} %collective-permute-done.18), channel_id=1, source_target_pairs={{0,1},{1,0},{2,3},{3,2},{4,5},{5,4},{6,7},{7,6},{8,9},{9,8},{10,11... | collective-permute-start | bytes 3145736 | tf_op jit(solution)/shard_map/ppermute | solution.py:195
  130.0 21.9 %collective-permute-start.23 = (bf16[4,512,256]{2,1,0:T(8,128)(2,1)}, bf16[4,512,256]{2,1,0:T(8,128)(2,1)}, u32[]{:S(2)}, u32[]{:S(2)}) collective-permute-start(bf16[4,512,256]{2,1,0:T(8,128)(2,1)} %collective-permute-done.21), channel_id=1, source_target_pairs={{0,4},{1,5},{2,6},{3,7},{4,0},{5,1},{6,2},{7,3},{8,12},{9,13},{10,... | collective-permute-start | bytes 3145736 | tf_op jit(solution)/shard_map/ppermute | solution.py:195
  (14 other events, 392.3 us)

commit v5 on v4

--- a/solution.py
+++ b/solution.py
@@ -7,7 +7,7 @@
 
 NT = (((1,), (1,)), ((), ()))
 MIB = 2**20
-UNROLL = 4
+UNROLL = 8
 MASKS = ((4, 12, 1, 3), (1, 3, 4, 12), (12, 4, 3, 1), (3, 1, 12, 4))
 
 
@@ -16,9 +16,12 @@
     return r * (2.0 - x * r)
 
 
-def listed(wts, order):
+def listed(idx, wts, order, soon):
     def entry(n, count):
-        hit = wts[64 + n] != 0.0
+        last = idx[0, 32 + n]
+        for q in range(4):
+            last = jnp.maximum(last, jnp.maximum(idx[q, 32 + n], idx[q, 128 + n]))
+        hit = (wts[64 + n] != 0.0) & ((last < 24) == soon)
 
         @pl.when(hit)
         def _():
@@ -32,47 +35,68 @@
     return (count + UNROLL - 1) // UNROLL
 
 
-def pair_kernel(idx, wts, slot, dsum, vrow, vcol, *refs):
-    pieces, out, pool, mixed, amp, vsum, order, sems, out_sems = refs[:16], *refs[16:]
-    copies = [
-        pltpu.make_async_copy(
-            pieces[4 * q + part], pool.at[q, pl.ds(8 * part, 8)], sems.at[4 * q + part]
-        )
-        for q in range(4)
-        for part in range(4)
-    ]
-    for copy in copies:
-        copy.start()
-    trips = listed(wts, order)
-    vsum[...] = vrow[...] + vcol[...]
-
-    def clear(s, carry):
-        mixed[s] = jnp.zeros((256, 256), jnp.float32)
-        return carry
-
-    lax.fori_loop(0, 16, clear, 0)
-    for copy in copies:
-        copy.wait()
-
-    def product(n):
-        left = jnp.concatenate([pool[q, idx[q, n]] for q in range(4)], axis=1)
-        right = jnp.concatenate([pool[q, idx[q, 96 + n]] for q in range(4)], axis=1)
-        return lax.dot_general(left, right, NT, preferred_element_type=jnp.float32)
-
+def product(idx, pool, n):
+    left = jnp.concatenate([pool[q, idx[q, n]] for q in range(4)], axis=1)
+    right = jnp.concatenate([pool[q, idx[q, 96 + n]] for q in range(4)], axis=1)
+    return lax.dot_general(left, right, NT, preferred_element_type=jnp.float32)
+
+
+def add_coupled(idx, wts, dsum, pool, mixed, vsum, order, trips):
     def coupled(g, carry):
         for u in range(UNROLL):
             entry = order[UNROLL * g + u]
             n = jnp.maximum(entry, 0)
             weight = jnp.where(entry >= 0, wts[64 + n], 0.0)
-            start = -(product(32 + n) * recip(vsum[...] - dsum[32 + n]))
+            at = jnp.where(entry >= 0, n, order[0])
+            start = -(product(idx, pool, 32 + at) * recip(vsum[...] - dsum[32 + at]))
             rounded = start.astype(jnp.bfloat16).astype(jnp.float32)
             mixed[n // 4] += weight * rounded
         return carry
+
+    lax.fori_loop(0, trips, coupled, 0)
+
+
+def early_kernel(idx, wts, dsum, vrow, vcol, *refs):
+    pieces, pool, mixed, vsum, order, sems = refs[:12], *refs[12:]
+    copies = [
+        pltpu.make_async_copy(
+            pieces[3 * q + part], pool.at[q, pl.ds(8 * part, 8)], sems.at[3 * q + part]
+        )
+        for q in range(4)
+        for part in range(3)
+    ]
+    for copy in copies:
+        copy.start()
+    trips = listed(idx, wts, order, True)
+    vsum[...] = vrow[...] + vcol[...]
+
+    def clear(s, carry):
+        mixed[s] = jnp.zeros((256, 256), jnp.float32)
+        return carry
+
+    lax.fori_loop(0, 16, clear, 0)
+    for copy in copies:
+        copy.wait()
+    add_coupled(idx, wts, dsum, pool, mixed, vsum, order, trips)
+
+
+def last_kernel(idx, wts, dsum, vrow, vcol, slot, *refs):
+    pieces, _, _, out, pool, mixed, amp, vsum, order, sems, out_sems = refs[:4], *refs[4:]
+    copies = [
+        pltpu.make_async_copy(pieces[q], pool.at[q, pl.ds(24, 8)], sems.at[q]) for q in range(4)
+    ]
+    for copy in copies:
+        copy.start()
+    trips = listed(idx, wts, order, False)
+    vsum[...] = vrow[...] + vcol[...]
+    for copy in copies:
+        copy.wait()
+    add_coupled(idx, wts, dsum, pool, mixed, vsum, order, trips)
 
     def received(g, carry):
         for u in range(UNROLL):
             s = UNROLL * g + u
-            value = (mixed[s] - product(16 + s)) * recip(vsum[...] - dsum[16 + s])
+            value = (mixed[s] - product(idx, pool, 16 + s)) * recip(vsum[...] - dsum[16 + s])
             amp[s] = value.astype(jnp.bfloat16)
         return carry
 
@@ -83,7 +107,7 @@
     def own(g, carry):
         for u in range(UNROLL):
             p = UNROLL * g + u
-            total = -product(p)
+            total = -product(idx, pool, p)
             for e in range(4):
                 total += wts[4 * p + e] * amp[slot[4 * p + e]].astype(jnp.float32)
             mixed[p] = total * recip(vsum[...] - dsum[p])
@@ -94,7 +118,6 @@
         out_copy(g).wait()
         return carry
 
-    lax.fori_loop(0, trips, coupled, 0)
     lax.fori_loop(0, 16 // UNROLL, received, 0)
     lax.fori_loop(0, 16 // UNROLL, own, 0)
     lax.fori_loop(0, 16 // UNROLL, finish, 0)
@@ -105,26 +128,47 @@
 HBM = pl.BlockSpec(memory_space=pl.ANY)
 
 
-def amplitudes(idx, wts, slot, dsum, virt, pieces):
+POOL = pltpu.VMEM((4, 32, 256, 256), jnp.bfloat16)
+SUMS = pltpu.VMEM((16, 256, 256), jnp.float32)
+
+
+def early_sums(idx, wts, dsum, vrow, vcol, pieces):
     return pl.pallas_call(
-        pair_kernel,
-        in_specs=[SMEM] * 4 + [VMEM] * 2 + [HBM] * 16,
-        out_specs=HBM,
-        out_shape=jax.ShapeDtypeStruct((16, 256, 256), jnp.float32),
+        early_kernel,
+        in_specs=[SMEM] * 3 + [VMEM] * 2 + [HBM] * 12,
+        out_specs=[VMEM] * 2,
+        out_shape=[POOL, SUMS],
         scratch_shapes=[
-            pltpu.VMEM((4, 32, 256, 256), jnp.bfloat16),
-            pltpu.VMEM((16, 256, 256), jnp.float32),
+            pltpu.VMEM((256, 256), jnp.float32),
+            pltpu.SMEM((72,), jnp.int32),
+            pltpu.SemaphoreType.DMA((12,)),
+        ],
+        compiler_params=pltpu.CompilerParams(vmem_limit_bytes=36 * MIB),
+        cost_estimate=pl.CostEstimate(
+            flops=20 * 2 * 256 * 256 * 1024, bytes_accessed=12 * MIB, transcendentals=0
+        ),
+    )(idx, wts, dsum, vrow, vcol, *pieces)
+
+
+def amplitudes(idx, wts, dsum, vrow, vcol, slot, pieces, pool, sums):
+    return pl.pallas_call(
+        last_kernel,
+        in_specs=[SMEM] * 3 + [VMEM] * 2 + [SMEM] + [HBM] * 4 + [VMEM] * 2,
+        out_specs=[HBM] + [VMEM] * 2,
+        out_shape=[jax.ShapeDtypeStruct((16, 256, 256), jnp.float32), POOL, SUMS],
+        input_output_aliases={10: 1, 11: 2},
+        scratch_shapes=[
             pltpu.VMEM((16, 256, 256), jnp.bfloat16),
             pltpu.VMEM((256, 256), jnp.float32),
             pltpu.SMEM((72,), jnp.int32),
-            pltpu.SemaphoreType.DMA((16,)),
+            pltpu.SemaphoreType.DMA((4,)),
             pltpu.SemaphoreType.DMA((4,)),
         ],
-        compiler_params=pltpu.CompilerParams(vmem_limit_bytes=58 * MIB),
+        compiler_params=pltpu.CompilerParams(vmem_limit_bytes=8 * MIB),
         cost_estimate=pl.CostEstimate(
-            flops=96 * 2 * 256 * 256 * 1024, bytes_accessed=20 * MIB, transcendentals=0
+            flops=80 * 2 * 256 * 256 * 1024, bytes_accessed=8 * MIB, transcendentals=0
         ),
-    )(idx, wts, slot, dsum, virt[None, :], virt[:, None], *pieces)
+    )(idx, wts, dsum, vrow, vcol, slot, *pieces, pool, sums)[0]
 
 
 def lookup(table, rows, cols):
@@ -250,8 +294,8 @@
 
     rows = integrals.reshape(64, 16, 512).transpose(1, 0, 2)
     block = lax.all_to_all(rows, "aux", split_axis=0, concat_axis=0, tiled=True)
-    block, metas = lax.optimization_barrier((block, metas))
-    idx, wts, slot, dsum = tables(metas, fock, orb, cpl, cpl_slot)
+    given = (*tables(metas, fock, orb, cpl, cpl_slot), virt_energy[None, :], virt_energy[:, None])
+    block, (idx, wts, slot, dsum, vrow, vcol) = lax.optimization_barrier((block, given))
     fitted = lax.dot_general(
         block.reshape(1024, 512),
         metric,
@@ -265,8 +309,10 @@
     third = [swap(held[q], MASKS[q][2]) for q in range(4)]
     early = [swap(held[q], MASKS[q][3]) for q in range(4)]
     late = [swap(third[q], MASKS[q][3]) for q in range(4)]
-    pieces = [x.reshape(8, 256, 256) for four in zip(held, third, early, late) for x in four]
-    return amplitudes(idx, wts, slot, dsum, virt_energy, pieces)
+    soon = [x.reshape(8, 256, 256) for three in zip(held, third, early) for x in three]
+    pool, sums = early_sums(idx, wts, dsum, vrow, vcol, soon)
+    late = [x.reshape(8, 256, 256) for x in late]
+    return amplitudes(idx, wts, dsum, vrow, vcol, slot, late, pool, sums)
 
 
 def solution(mesh):

time: 180 us -> 172 us (0.956)
  waiting for transfers between devices: 87.1 us -> 79.7 us
  Pallas kernels: 33.1 us -> 31.2 us
    ppermute x24, waiting for transfers between devices: 76.8 us -> 71.9 us  [swap(): return lax.ppermute(block, 'grp', [(g, g ^ mask) for g in range(16)])]
    all_to_all x1, waiting for transfers between devices: 10.3 us -> 7.77 us  [on_device(): block = lax.all_to_all(rows, 'aux', split_axis=0, concat_axis=0, tiled=True)]
    pallas_call x2, Pallas kernels: 5.8 us -> 3.78 us  [join(): pl.pallas_call(join_kernel, in_specs=[HBM] * 8, out_specs=[HBM] * 4, out_...]
    pallas_call x1 -> x2, Pallas kernels: 27.3 us -> 27.4 us  [the longest x1 18.6 us: amplitudes(): pl.pallas_call(last_kernel, in_specs=[SMEM] * 3 + [VMEM] * 2 + [SMEM] + [...]
  transfers between devices with their start and end apart: 25 -> 25, of which waited for: 20 -> 17; matrix products, arithmetic and copies ran while one was open for 5% -> 6% of each run, Pallas kernels for 0% -> 5%
where the time goes in v5:
time: 172 us; the launch traced here: 171 us
  waiting for transfers between devices  79.7 us (46%)
  starting transfers between devices  44.8 us (26%)
  Pallas kernels  31.2 us (18%)
  local copies, waits for them, and re-layouts  6.51 us (4%)
  other arithmetic  5.28 us (3%)
  matrix products  2.73 us (2%)
    ppermute x24, waiting for transfers between devices, swap(): return lax.ppermute(block, 'grp', [(g, g ^ mask) for g in range(16)])  71.9 us
    ppermute x24, starting transfers between devices, swap(): return lax.ppermute(block, 'grp', [(g, g ^ mask) for g in range(16)])  38 us
    pallas_call x1, Pallas kernels, amplitudes(): pl.pallas_call(last_kernel, in_specs=[SMEM] * 3 + [VMEM] * 2 + [SMEM] + [...  18.6 us
    pallas_call x1, Pallas kernels, early_sums(): pl.pallas_call(early_kernel, in_specs=[SMEM] * 3 + [VMEM] * 2 + [HBM] * 1...  8.79 us
    all_to_all x1, waiting for transfers between devices, on_device(): block = lax.all_to_all(rows, 'aux', split_axis=0, concat_axis=0, tiled=True)  7.77 us
    all_to_all x1, starting transfers between devices, on_device(): block = lax.all_to_all(rows, 'aux', split_axis=0, concat_axis=0, tiled=True)  6.84 us
    pallas_call x2, Pallas kernels, join(): pl.pallas_call(join_kernel, in_specs=[HBM] * 8, out_specs=[HBM] * 4, out_...  3.78 us
  transfers between devices with their start and end apart: 25, of which 17 were waited for; matrix products, arithmetic and copies ran while one was open for 6% of the time, Pallas kernels for 5%

profile of v5, /device:TPU:2, one launch (start us, length us, event | category | flops | bytes accessed | tf_op | source)
XLA Modules:
  0.0 170.8 jit_solution(9561269213186452413)
XLA Ops:
  2.5 2.3 %collective-permute-start = (s32[1,176]{1,0:T(1,128)S(1)}, s32[1,176]{1,0:T(1,128)S(1)}, u32[]{:S(2)}, u32[]{:S(2)}) collective-permute-start(s32[1,176]{1,0:T(1,128)S(1)} %pad_add_fusion.5), channel_id=1, source_target_pairs={{0,4},{1,5},{2,6},{3,7},{4,0},{5,1},{6,2},{7,3},{8,12},{9,13},{10,... | collective-permute-start | bytes 2120 | tf_op jit(solution)/shard_map/ppermute | solution.py:239
  7.7 6.8 %all-to-all-start = ((bf16[16,64,512]{2,1,0:T(8,128)(2,1)}), bf16[16,64,512]{2,1,0:T(8,128)(2,1)S(1)}, u32[]{:S(2)}, u32[]{:S(2)}) async-start(bf16[16,64,512]{2,1,0:T(8,128)(2,1)} %copy.76), calls=%async_computation | async-start | bytes 2097152 | tf_op jit(solution)/shard_map/all_to_all | solution.py:296
  16.9 2.2 %collective-permute-start.1 = (s32[2,176]{1,0:T(2,128)S(1)}, s32[2,176]{1,0:T(2,128)S(1)}, u32[]{:S(2)}, u32[]{:S(2)}) collective-permute-start(s32[2,176]{1,0:T(2,128)S(1)} %pad_add_fusion.4), channel_id=1, source_target_pairs={{0,12},{1,13},{2,14},{3,15},{4,8},{5,9},{6,10},{7,11},{8,4},{9,5},... | collective-permute-start | bytes 4232 | tf_op jit(solution)/shard_map/ppermute | solution.py:239
  22.4 1.9 %collective-permute-done.2 = s32[4,176]{1,0:T(4,128)S(1)} collective-permute-done((s32[4,176]{1,0:T(4,128)S(1)}, s32[4,176]{1,0:T(4,128)S(1)}, u32[]{:S(2)}, u32[]{:S(2)}) %collective-permute-start.2) | collective-permute-done | bytes 2848 | tf_op jit(solution)/shard_map/ppermute | solution.py:239
  24.4 3.0 %collective-permute-start.3 = (s32[8,176]{1,0:T(8,128)S(1)}, s32[8,176]{1,0:T(8,128)S(1)}, u32[]{:S(2)}, u32[]{:S(2)}) collective-permute-start(s32[8,176]{1,0:T(8,128)S(1)} %pad_add_fusion.2), channel_id=1, source_target_pairs={{0,3},{1,2},{2,1},{3,0},{4,7},{5,6},{6,5},{7,4},{8,11},{9,10},{10,... | collective-permute-start | bytes 16904 | tf_op jit(solution)/shard_map/ppermute | solution.py:239
  33.5 7.8 %all-to-all-done = bf16[16,64,512]{2,1,0:T(8,128)(2,1)S(1)} async-done(((bf16[16,64,512]{2,1,0:T(8,128)(2,1)}), bf16[16,64,512]{2,1,0:T(8,128)(2,1)S(1)}, u32[]{:S(2)}, u32[]{:S(2)}) %all-to-all-start) | async-done | bytes 1048608 | tf_op jit(solution)/shard_map/all_to_all | solution.py:296
  42.7 3.1 %collective-permute-start.7 = (bf16[1,512,256]{2,1,0:T(8,128)(2,1)S(1)}, bf16[1,512,256]{2,1,0:T(8,128)(2,1)S(1)}, u32[]{:S(2)}, u32[]{:S(2)}) collective-permute-start(bf16[1,512,256]{2,1,0:T(8,128)(2,1)S(1)} %get-tuple-element.49.refs_3_), channel_id=1, source_target_pairs={{0,3},{1,2},{2,1},{3,0},{4,7},{5,6},{6,5},{7,4},{8,11},{9,10},{10,... | collective-permute-start | bytes 786440 | tf_op jit(solution)/shard_map/ppermute | solution.py:239
  45.8 2.2 %collective-permute-start.6 = (bf16[1,512,256]{2,1,0:T(8,128)(2,1)S(1)}, bf16[1,512,256]{2,1,0:T(8,128)(2,1)S(1)}, u32[]{:S(2)}, u32[]{:S(2)}) collective-permute-start(bf16[1,512,256]{2,1,0:T(8,128)(2,1)S(1)} %get-tuple-element.50.refs_2_), channel_id=1, source_target_pairs={{0,12},{1,13},{2,14},{3,15},{4,8},{5,9},{6,10},{7,11},{8,4},{9,5},... | collective-permute-start | bytes 786440 | tf_op jit(solution)/shard_map/ppermute | solution.py:239
  49.5 2.9 %collective-permute-done.7.refs_7_ = bf16[1,512,256]{2,1,0:T(8,128)(2,1)S(1)} collective-permute-done((bf16[1,512,256]{2,1,0:T(8,128)(2,1)S(1)}, bf16[1,512,256]{2,1,0:T(8,128)(2,1)S(1)}, u32[]{:S(2)}, u32[]{:S(2)}) %collective-permute-start.7) | collective-permute-done | bytes 262176 | tf_op jit(solution)/shard_map/ppermute | solution.py:239
  52.4 2.0 %collective-permute-done.6.refs_6_ = bf16[1,512,256]{2,1,0:T(8,128)(2,1)S(1)} collective-permute-done((bf16[1,512,256]{2,1,0:T(8,128)(2,1)S(1)}, bf16[1,512,256]{2,1,0:T(8,128)(2,1)S(1)}, u32[]{:S(2)}, u32[]{:S(2)}) %collective-permute-start.6) | collective-permute-done | bytes 262176 | tf_op jit(solution)/shard_map/ppermute | solution.py:239
  54.4 2.5 %collective-permute-done.5.refs_5_ = bf16[1,512,256]{2,1,0:T(8,128)(2,1)S(1)} collective-permute-done((bf16[1,512,256]{2,1,0:T(8,128)(2,1)S(1)}, bf16[1,512,256]{2,1,0:T(8,128)(2,1)S(1)}, u32[]{:S(2)}, u32[]{:S(2)}) %collective-permute-start.5) | collective-permute-done | bytes 262176 | tf_op jit(solution)/shard_map/ppermute | solution.py:239
  58.8 2.5 %collective-permute-start.10 = (bf16[2,512,256]{2,1,0:T(8,128)(2,1)S(1)}, bf16[2,512,256]{2,1,0:T(8,128)(2,1)S(1)}, u32[]{:S(2)}, u32[]{:S(2)}) collective-permute-start(bf16[2,512,256]{2,1,0:T(8,128)(2,1)S(1)} %get-tuple-element.32.refs_2_), channel_id=1, source_target_pairs={{0,4},{1,5},{2,6},{3,7},{4,0},{5,1},{6,2},{7,3},{8,12},{9,13},{10,... | collective-permute-start | bytes 1572872 | tf_op jit(solution)/shard_map/ppermute | solution.py:239
  62.1 9.6 %collective-permute-done.8.refs_4_ = bf16[2,512,256]{2,1,0:T(8,128)(2,1)S(1)} collective-permute-done((bf16[2,512,256]{2,1,0:T(8,128)(2,1)S(1)}, bf16[2,512,256]{2,1,0:T(8,128)(2,1)S(1)}, u32[]{:S(2)}, u32[]{:S(2)}) %collective-permute-start.8) | collective-permute-done | bytes 524320 | tf_op jit(solution)/shard_map/ppermute | solution.py:239
  74.4 3.4 %shard_map.128 = (bf16[4,512,256]{2,1,0:T(8,128)(2,1)}, bf16[4,512,256]{2,1,0:T(8,128)(2,1)}, bf16[4,512,256]{2,1,0:T(8,128)(2,1)}, bf16[4,512,256]{2,1,0:T(8,128)(2,1)}) custom-call(bf16[2,512,256]{2,1,0:T(8,128)(2,1)} %copy-done.2, bf16[2,512,256]{2,1,0:T(8,128)(2,1)} %copy-done.3, bf16[2,512,256]{2,1,0:T(8,128)(2,1)} %copy-done.4, ...), custom_call_target="tpu_custom_call" | custom-call | bytes 8388608 | tf_op jit(solution)/shard_map/pallas_call | solution.py:271
  77.8 2.5 %collective-permute-start.20 = (bf16[4,512,256]{2,1,0:T(8,128)(2,1)}, bf16[4,512,256]{2,1,0:T(8,128)(2,1)S(1)}, u32[]{:S(2)}, u32[]{:S(2)}) collective-permute-start(bf16[4,512,256]{2,1,0:T(8,128)(2,1)} %get-tuple-element.34), channel_id=1, source_target_pairs={{0,3},{1,2},{2,1},{3,0},{4,7},{5,6},{6,5},{7,4},{8,11},{9,10},{10,... | collective-permute-start | bytes 3145736 | tf_op jit(solution)/shard_map/ppermute | solution.py:239
  85.4 17.9 %collective-permute-done.20 = bf16[4,512,256]{2,1,0:T(8,128)(2,1)S(1)} collective-permute-done((bf16[4,512,256]{2,1,0:T(8,128)(2,1)}, bf16[4,512,256]{2,1,0:T(8,128)(2,1)S(1)}, u32[]{:S(2)}, u32[]{:S(2)}) %collective-permute-start.20) | collective-permute-done | bytes 1048608 | tf_op jit(solution)/shard_map/ppermute | solution.py:239
  103.3 1.9 %collective-permute-start.16 = (bf16[4,512,256]{2,1,0:T(8,128)(2,1)}, bf16[4,512,256]{2,1,0:T(8,128)(2,1)}, u32[]{:S(2)}, u32[]{:S(2)}) collective-permute-start(bf16[4,512,256]{2,1,0:T(8,128)(2,1)} %get-tuple-element.36), channel_id=1, source_target_pairs={{0,3},{1,2},{2,1},{3,0},{4,7},{5,6},{6,5},{7,4},{8,11},{9,10},{10,... | collective-permute-start | bytes 3145736 | tf_op jit(solution)/shard_map/ppermute | solution.py:239
  111.5 14.7 %collective-permute-done.22 = bf16[4,512,256]{2,1,0:T(8,128)(2,1)} collective-permute-done((bf16[4,512,256]{2,1,0:T(8,128)(2,1)}, bf16[4,512,256]{2,1,0:T(8,128)(2,1)}, u32[]{:S(2)}, u32[]{:S(2)}) %collective-permute-start.22) | collective-permute-done | bytes 1048608 | tf_op jit(solution)/shard_map/ppermute | solution.py:239
  127.7 3.1 %collective-permute-done.16 = bf16[4,512,256]{2,1,0:T(8,128)(2,1)} collective-permute-done((bf16[4,512,256]{2,1,0:T(8,128)(2,1)}, bf16[4,512,256]{2,1,0:T(8,128)(2,1)}, u32[]{:S(2)}, u32[]{:S(2)}) %collective-permute-start.16) | collective-permute-done | bytes 1048608 | tf_op jit(solution)/shard_map/ppermute | solution.py:239
  130.9 1.9 %collective-permute-start.19 = (bf16[4,512,256]{2,1,0:T(8,128)(2,1)}, bf16[4,512,256]{2,1,0:T(8,128)(2,1)}, u32[]{:S(2)}, u32[]{:S(2)}) collective-permute-start(bf16[4,512,256]{2,1,0:T(8,128)(2,1)} %collective-permute-done.18), channel_id=1, source_target_pairs={{0,4},{1,5},{2,6},{3,7},{4,0},{5,1},{6,2},{7,3},{8,12},{9,13},{10,... | collective-permute-start | bytes 3145736 | tf_op jit(solution)/shard_map/ppermute | solution.py:239
  133.6 8.8 %shard_map.129 = (bf16[4,32,256,256]{3,2,1,0:T(8,128)(2,1)S(1)}, f32[16,256,256]{2,1,0:T(8,128)S(1)}) custom-call(s32[4,192]{1,0:T(4,128)} %fusion.5.idx, f32[128]{0:T(128)} %pad_maximum_fusion.wts, f32[96]{0:T(128)} %add_bitcast_fusion.dsum, f32[1,256]{1,0:T(1,128)} %bitcast.55, f32[256,1]{1,0:T(8,128)} %copy.89.vcol, bf16[8,256,256]{2,1,0:T(8,128)(2,1)} %bitcast.60, ...), custom_call_target="tpu_custom_call" | custom-call | flops 2684354560 | bytes 12582912 | tf_op jit(solution)/shard_map/pallas_call | solution.py:136
  142.4 7.8 %collective-permute-done.13 = bf16[4,512,256]{2,1,0:T(8,128)(2,1)S(1)} collective-permute-done((bf16[4,512,256]{2,1,0:T(8,128)(2,1)}, bf16[4,512,256]{2,1,0:T(8,128)(2,1)S(1)}, u32[]{:S(2)}, u32[]{:S(2)}) %collective-permute-start.13) | collective-permute-done | bytes 1048608 | tf_op jit(solution)/shard_map/ppermute | solution.py:239
  150.2 1.8 %collective-permute-done.19 = bf16[4,512,256]{2,1,0:T(8,128)(2,1)} collective-permute-done((bf16[4,512,256]{2,1,0:T(8,128)(2,1)}, bf16[4,512,256]{2,1,0:T(8,128)(2,1)}, u32[]{:S(2)}, u32[]{:S(2)}) %collective-permute-start.19) | collective-permute-done | bytes 1048608 | tf_op jit(solution)/shard_map/ppermute | solution.py:239
  152.0 18.6 %shard_map.130 = (f32[16,256,256]{2,1,0:T(8,128)}, bf16[4,32,256,256]{3,2,1,0:T(8,128)(2,1)S(1)}, f32[16,256,256]{2,1,0:T(8,128)S(1)}) custom-call(s32[4,192]{1,0:T(4,128)S(1)} %copy-done.6, f32[128]{0:T(128)S(1)} %copy-done.9, f32[96]{0:T(128)S(1)} %copy-done.10, f32[1,256]{1,0:T(1,128)S(1)} %bitcast.57, ...), custom_call_target="tpu_custom_call", output_to_operand_aliasing={{1}: (10, {}), {2}: (11, {})} | custom-call | flops 10737418240 | bytes 8388608 | tf_op jit(solution)/shard_map/pallas_call | solution.py:154
  (142 shorter events, 39.0 us)
Async XLA Ops:
  2.5 14.3 %collective-permute-start = (s32[1,176]{1,0:T(1,128)S(1)}, s32[1,176]{1,0:T(1,128)S(1)}, u32[]{:S(2)}, u32[]{:S(2)}) collective-permute-start(s32[1,176]{1,0:T(1,128)S(1)} %pad_add_fusion.5), channel_id=1, source_target_pairs={{0,4},{1,5},{2,6},{3,7},{4,0},{5,1},{6,2},{7,3},{8,12},{9,13},{10,... | collective-permute-start | bytes 2120 | tf_op jit(solution)/shard_map/ppermute | solution.py:239
  7.7 33.5 %all-to-all-start = ((bf16[16,64,512]{2,1,0:T(8,128)(2,1)}), bf16[16,64,512]{2,1,0:T(8,128)(2,1)S(1)}, u32[]{:S(2)}, u32[]{:S(2)}) async-start(bf16[16,64,512]{2,1,0:T(8,128)(2,1)} %copy.76), calls=%async_computation | async-start | bytes 2097152 | tf_op jit(solution)/shard_map/all_to_all | solution.py:296
  16.9 3.7 %collective-permute-start.1 = (s32[2,176]{1,0:T(2,128)S(1)}, s32[2,176]{1,0:T(2,128)S(1)}, u32[]{:S(2)}, u32[]{:S(2)}) collective-permute-start(s32[2,176]{1,0:T(2,128)S(1)} %pad_add_fusion.4), channel_id=1, source_target_pairs={{0,12},{1,13},{2,14},{3,15},{4,8},{5,9},{6,10},{7,11},{8,4},{9,5},... | collective-permute-start | bytes 4232 | tf_op jit(solution)/shard_map/ppermute | solution.py:239
  24.4 4.9 %collective-permute-start.3 = (s32[8,176]{1,0:T(8,128)S(1)}, s32[8,176]{1,0:T(8,128)S(1)}, u32[]{:S(2)}, u32[]{:S(2)}) collective-permute-start(s32[8,176]{1,0:T(8,128)S(1)} %pad_add_fusion.2), channel_id=1, source_target_pairs={{0,3},{1,2},{2,1},{3,0},{4,7},{5,6},{6,5},{7,4},{8,11},{9,10},{10,... | collective-permute-start | bytes 16904 | tf_op jit(solution)/shard_map/ppermute | solution.py:239
  42.7 9.7 %collective-permute-start.7 = (bf16[1,512,256]{2,1,0:T(8,128)(2,1)S(1)}, bf16[1,512,256]{2,1,0:T(8,128)(2,1)S(1)}, u32[]{:S(2)}, u32[]{:S(2)}) collective-permute-start(bf16[1,512,256]{2,1,0:T(8,128)(2,1)S(1)} %get-tuple-element.49.refs_3_), channel_id=1, source_target_pairs={{0,3},{1,2},{2,1},{3,0},{4,7},{5,6},{6,5},{7,4},{8,11},{9,10},{10,... | collective-permute-start | bytes 786440 | tf_op jit(solution)/shard_map/ppermute | solution.py:239
  45.8 8.6 %collective-permute-start.6 = (bf16[1,512,256]{2,1,0:T(8,128)(2,1)S(1)}, bf16[1,512,256]{2,1,0:T(8,128)(2,1)S(1)}, u32[]{:S(2)}, u32[]{:S(2)}) collective-permute-start(bf16[1,512,256]{2,1,0:T(8,128)(2,1)S(1)} %get-tuple-element.50.refs_2_), channel_id=1, source_target_pairs={{0,12},{1,13},{2,14},{3,15},{4,8},{5,9},{6,10},{7,11},{8,4},{9,5},... | collective-permute-start | bytes 786440 | tf_op jit(solution)/shard_map/ppermute | solution.py:239
  47.9 9.0 %collective-permute-start.5 = (bf16[1,512,256]{2,1,0:T(8,128)(2,1)S(1)}, bf16[1,512,256]{2,1,0:T(8,128)(2,1)S(1)}, u32[]{:S(2)}, u32[]{:S(2)}) collective-permute-start(bf16[1,512,256]{2,1,0:T(8,128)(2,1)S(1)} %get-tuple-element.51.refs_1_), channel_id=1, source_target_pairs={{0,1},{1,0},{2,3},{3,2},{4,5},{5,4},{6,7},{7,6},{8,9},{9,8},{10,11... | collective-permute-start | bytes 786440 | tf_op jit(solution)/shard_map/ppermute | solution.py:239
  48.1 9.2 %collective-permute-start.4 = (bf16[1,512,256]{2,1,0:T(8,128)(2,1)S(1)}, bf16[1,512,256]{2,1,0:T(8,128)(2,1)S(1)}, u32[]{:S(2)}, u32[]{:S(2)}) collective-permute-start(bf16[1,512,256]{2,1,0:T(8,128)(2,1)S(1)} %get-tuple-element.52.refs_0_), channel_id=1, source_target_pairs={{0,4},{1,5},{2,6},{3,7},{4,0},{5,1},{6,2},{7,3},{8,12},{9,13},{10,... | collective-permute-start | bytes 786440 | tf_op jit(solution)/shard_map/ppermute | solution.py:239
  57.7 14.0 %collective-permute-start.8 = (bf16[2,512,256]{2,1,0:T(8,128)(2,1)S(1)}, bf16[2,512,256]{2,1,0:T(8,128)(2,1)S(1)}, u32[]{:S(2)}, u32[]{:S(2)}) collective-permute-start(bf16[2,512,256]{2,1,0:T(8,128)(2,1)S(1)} %get-tuple-element.30.refs_0_), channel_id=1, source_target_pairs={{0,12},{1,13},{2,14},{3,15},{4,8},{5,9},{6,10},{7,11},{8,4},{9,5},... | collective-permute-start | bytes 1572872 | tf_op jit(solution)/shard_map/ppermute | solution.py:239
  57.8 15.2 %collective-permute-start.9 = (bf16[2,512,256]{2,1,0:T(8,128)(2,1)S(1)}, bf16[2,512,256]{2,1,0:T(8,128)(2,1)S(1)}, u32[]{:S(2)}, u32[]{:S(2)}) collective-permute-start(bf16[2,512,256]{2,1,0:T(8,128)(2,1)S(1)} %get-tuple-element.31.refs_1_), channel_id=1, source_target_pairs={{0,3},{1,2},{2,1},{3,0},{4,7},{5,6},{6,5},{7,4},{8,11},{9,10},{10,... | collective-permute-start | bytes 1572872 | tf_op jit(solution)/shard_map/ppermute | solution.py:239
  58.8 14.2 %collective-permute-start.10 = (bf16[2,512,256]{2,1,0:T(8,128)(2,1)S(1)}, bf16[2,512,256]{2,1,0:T(8,128)(2,1)S(1)}, u32[]{:S(2)}, u32[]{:S(2)}) collective-permute-start(bf16[2,512,256]{2,1,0:T(8,128)(2,1)S(1)} %get-tuple-element.32.refs_2_), channel_id=1, source_target_pairs={{0,4},{1,5},{2,6},{3,7},{4,0},{5,1},{6,2},{7,3},{8,12},{9,13},{10,... | collective-permute-start | bytes 1572872 | tf_op jit(solution)/shard_map/ppermute | solution.py:239
  61.3 13.1 %collective-permute-start.11 = (bf16[2,512,256]{2,1,0:T(8,128)(2,1)S(1)}, bf16[2,512,256]{2,1,0:T(8,128)(2,1)}, u32[]{:S(2)}, u32[]{:S(2)}) collective-permute-start(bf16[2,512,256]{2,1,0:T(8,128)(2,1)S(1)} %get-tuple-element.33.refs_3_), channel_id=1, source_target_pairs={{0,1},{1,0},{2,3},{3,2},{4,5},{5,4},{6,7},{7,6},{8,9},{9,8},{10,11... | collective-permute-start | bytes 1572872 | tf_op jit(solution)/shard_map/ppermute | solution.py:239
  77.8 25.4 %collective-permute-start.20 = (bf16[4,512,256]{2,1,0:T(8,128)(2,1)}, bf16[4,512,256]{2,1,0:T(8,128)(2,1)S(1)}, u32[]{:S(2)}, u32[]{:S(2)}) collective-permute-start(bf16[4,512,256]{2,1,0:T(8,128)(2,1)} %get-tuple-element.34), channel_id=1, source_target_pairs={{0,3},{1,2},{2,1},{3,0},{4,7},{5,6},{6,5},{7,4},{8,11},{9,10},{10,... | collective-permute-start | bytes 3145736 | tf_op jit(solution)/shard_map/ppermute | solution.py:239
  80.3 26.4 %collective-permute-start.12 = (bf16[4,512,256]{2,1,0:T(8,128)(2,1)}, bf16[4,512,256]{2,1,0:T(8,128)(2,1)}, u32[]{:S(2)}, u32[]{:S(2)}) collective-permute-start(bf16[4,512,256]{2,1,0:T(8,128)(2,1)} %get-tuple-element.34), channel_id=1, source_target_pairs={{0,1},{1,0},{2,3},{3,2},{4,5},{5,4},{6,7},{7,6},{8,9},{9,8},{10,11... | collective-permute-start | bytes 3145736 | tf_op jit(solution)/shard_map/ppermute | solution.py:239
  80.8 27.5 %collective-permute-start.21 = (bf16[4,512,256]{2,1,0:T(8,128)(2,1)}, bf16[4,512,256]{2,1,0:T(8,128)(2,1)S(1)}, u32[]{:S(2)}, u32[]{:S(2)}) collective-permute-start(bf16[4,512,256]{2,1,0:T(8,128)(2,1)} %get-tuple-element.35), channel_id=1, source_target_pairs={{0,12},{1,13},{2,14},{3,15},{4,8},{5,9},{6,10},{7,11},{8,4},{9,5},... | collective-permute-start | bytes 3145736 | tf_op jit(solution)/shard_map/ppermute | solution.py:239
  82.2 27.5 %collective-permute-start.14 = (bf16[4,512,256]{2,1,0:T(8,128)(2,1)}, bf16[4,512,256]{2,1,0:T(8,128)(2,1)}, u32[]{:S(2)}, u32[]{:S(2)}) collective-permute-start(bf16[4,512,256]{2,1,0:T(8,128)(2,1)} %get-tuple-element.35), channel_id=1, source_target_pairs={{0,4},{1,5},{2,6},{3,7},{4,0},{5,1},{6,2},{7,3},{8,12},{9,13},{10,... | collective-permute-start | bytes 3145736 | tf_op jit(solution)/shard_map/ppermute | solution.py:239
  83.8 42.5 %collective-permute-start.22 = (bf16[4,512,256]{2,1,0:T(8,128)(2,1)}, bf16[4,512,256]{2,1,0:T(8,128)(2,1)}, u32[]{:S(2)}, u32[]{:S(2)}) collective-permute-start(bf16[4,512,256]{2,1,0:T(8,128)(2,1)} %get-tuple-element.36), channel_id=1, source_target_pairs={{0,1},{1,0},{2,3},{3,2},{4,5},{5,4},{6,7},{7,6},{8,9},{9,8},{10,11... | collective-permute-start | bytes 3145736 | tf_op jit(solution)/shard_map/ppermute | solution.py:239
  103.3 27.6 %collective-permute-start.16 = (bf16[4,512,256]{2,1,0:T(8,128)(2,1)}, bf16[4,512,256]{2,1,0:T(8,128)(2,1)}, u32[]{:S(2)}, u32[]{:S(2)}) collective-permute-start(bf16[4,512,256]{2,1,0:T(8,128)(2,1)} %get-tuple-element.36), channel_id=1, source_target_pairs={{0,3},{1,2},{2,1},{3,0},{4,7},{5,6},{6,5},{7,4},{8,11},{9,10},{10,... | collective-permute-start | bytes 3145736 | tf_op jit(solution)/shard_map/ppermute | solution.py:239
  106.7 24.2 %collective-permute-start.18 = (bf16[4,512,256]{2,1,0:T(8,128)(2,1)}, bf16[4,512,256]{2,1,0:T(8,128)(2,1)}, u32[]{:S(2)}, u32[]{:S(2)}) collective-permute-start(bf16[4,512,256]{2,1,0:T(8,128)(2,1)} %get-tuple-element.37), channel_id=1, source_target_pairs={{0,12},{1,13},{2,14},{3,15},{4,8},{5,9},{6,10},{7,11},{8,4},{9,5},... | collective-permute-start | bytes 3145736 | tf_op jit(solution)/shard_map/ppermute | solution.py:239
  108.2 25.3 %collective-permute-start.23 = (bf16[4,512,256]{2,1,0:T(8,128)(2,1)}, bf16[4,512,256]{2,1,0:T(8,128)(2,1)}, u32[]{:S(2)}, u32[]{:S(2)}) collective-permute-start(bf16[4,512,256]{2,1,0:T(8,128)(2,1)} %get-tuple-element.37), channel_id=1, source_target_pairs={{0,4},{1,5},{2,6},{3,7},{4,0},{5,1},{6,2},{7,3},{8,12},{9,13},{10,... | collective-permute-start | bytes 3145736 | tf_op jit(solution)/shard_map/ppermute | solution.py:239
  109.8 40.4 %collective-permute-start.13 = (bf16[4,512,256]{2,1,0:T(8,128)(2,1)}, bf16[4,512,256]{2,1,0:T(8,128)(2,1)S(1)}, u32[]{:S(2)}, u32[]{:S(2)}) collective-permute-start(bf16[4,512,256]{2,1,0:T(8,128)(2,1)} %collective-permute-done.12), channel_id=1, source_target_pairs={{0,3},{1,2},{2,1},{3,0},{4,7},{5,6},{6,5},{7,4},{8,11},{9,10},{10,... | collective-permute-start | bytes 3145736 | tf_op jit(solution)/shard_map/ppermute | solution.py:239
  126.2 23.9 %collective-permute-start.15 = (bf16[4,512,256]{2,1,0:T(8,128)(2,1)}, bf16[4,512,256]{2,1,0:T(8,128)(2,1)}, u32[]{:S(2)}, u32[]{:S(2)}) collective-permute-start(bf16[4,512,256]{2,1,0:T(8,128)(2,1)} %collective-permute-done.14), channel_id=1, source_target_pairs={{0,12},{1,13},{2,14},{3,15},{4,8},{5,9},{6,10},{7,11},{8,4},{9,5},... | collective-permute-start | bytes 3145736 | tf_op jit(solution)/shard_map/ppermute | solution.py:239
  130.9 19.3 %collective-permute-start.17 = (bf16[4,512,256]{2,1,0:T(8,128)(2,1)}, bf16[4,512,256]{2,1,0:T(8,128)(2,1)}, u32[]{:S(2)}, u32[]{:S(2)}) collective-permute-start(bf16[4,512,256]{2,1,0:T(8,128)(2,1)} %collective-permute-done.16), channel_id=1, source_target_pairs={{0,1},{1,0},{2,3},{3,2},{4,5},{5,4},{6,7},{7,6},{8,9},{9,8},{10,11... | collective-permute-start | bytes 3145736 | tf_op jit(solution)/shard_map/ppermute | solution.py:239
  130.9 21.1 %collective-permute-start.19 = (bf16[4,512,256]{2,1,0:T(8,128)(2,1)}, bf16[4,512,256]{2,1,0:T(8,128)(2,1)}, u32[]{:S(2)}, u32[]{:S(2)}) collective-permute-start(bf16[4,512,256]{2,1,0:T(8,128)(2,1)} %collective-permute-done.18), channel_id=1, source_target_pairs={{0,4},{1,5},{2,6},{3,7},{4,0},{5,1},{6,2},{7,3},{8,12},{9,13},{10,... | collective-permute-start | bytes 3145736 | tf_op jit(solution)/shard_map/ppermute | solution.py:239
  (23 other events, 462.5 us)

commit v6 on v5

--- a/solution.py
+++ b/solution.py
@@ -285,6 +285,10 @@
 def on_device(
     integrals, metric, fock, virt_energy, send_orb, pair_orb, send_pair, cpl_slot, cpl_orb
 ):
+    rows = integrals.reshape(64, 16, 512).transpose(1, 0, 2)
+    rows, pair_orb, cpl_orb, send_pair = lax.optimization_barrier(
+        (rows, pair_orb, cpl_orb, send_pair)
+    )
     orb = pair_orb // 32 * 2 + pair_orb % 2
     cpl = cpl_orb // 32 * 2 + cpl_orb % 2
     metas = jnp.concatenate([orb, cpl.reshape(16, 8)], axis=1).reshape(1, 160)
@@ -292,7 +296,6 @@
     for mask in MASKS[0]:
         metas = jnp.concatenate([metas, swap(metas, mask)], axis=0)
 
-    rows = integrals.reshape(64, 16, 512).transpose(1, 0, 2)
     block = lax.all_to_all(rows, "aux", split_axis=0, concat_axis=0, tiled=True)
     given = (*tables(metas, fock, orb, cpl, cpl_slot), virt_energy[None, :], virt_energy[:, None])
     block, (idx, wts, slot, dsum, vrow, vcol) = lax.optimization_barrier((block, given))

time: 172 us -> 168 us (0.977); the launches traced: 171 us -> 165 us
  waiting for transfers between devices: 79.7 us -> 74.8 us
  other arithmetic: 5.28 us -> 3.1 us
    ppermute x24, waiting for transfers between devices: 71.9 us -> 68.6 us  [swap(): return lax.ppermute(block, 'grp', [(g, g ^ mask) for g in range(16)])]
    pallas_call x1, Pallas kernels: 18.6 us -> 15.5 us  [amplitudes(): pl.pallas_call(last_kernel, in_specs=[SMEM] * 3 + [VMEM] * 2 + [SMEM] + [...]
    pallas_call x1, Pallas kernels: 8.79 us -> 11.9 us  [early_sums(): pl.pallas_call(early_kernel, in_specs=[SMEM] * 3 + [VMEM] * 2 + [HBM] * 1...]
    all_to_all x1, starting transfers between devices: 6.84 us -> 8.57 us  [on_device(): block = lax.all_to_all(rows, 'aux', split_axis=0, concat_axis=0, tiled=True)]
  transfers between devices with their start and end apart: 25 -> 25, of which waited for: 17 -> 19; matrix products, arithmetic and copies ran while one was open for 6% -> 5% of each run, Pallas kernels for 5% -> 7%
where the time goes in v6:
time: 168 us; the launch traced here: 165 us
  waiting for transfers between devices  74.8 us (45%)
  starting transfers between devices  45.4 us (27%)
  Pallas kernels  31.2 us (19%)
  local copies, waits for them, and re-layouts  6.72 us (4%)
  other arithmetic  3.1 us (2%)
  matrix products  2.7 us (2%)
    ppermute x24, waiting for transfers between devices, swap(): return lax.ppermute(block, 'grp', [(g, g ^ mask) for g in range(16)])  68.6 us
    ppermute x24, starting transfers between devices, swap(): return lax.ppermute(block, 'grp', [(g, g ^ mask) for g in range(16)])  36.8 us
    pallas_call x1, Pallas kernels, amplitudes(): pl.pallas_call(last_kernel, in_specs=[SMEM] * 3 + [VMEM] * 2 + [SMEM] + [...  15.5 us
    pallas_call x1, Pallas kernels, early_sums(): pl.pallas_call(early_kernel, in_specs=[SMEM] * 3 + [VMEM] * 2 + [HBM] * 1...  11.9 us
    all_to_all x1, starting transfers between devices, on_device(): block = lax.all_to_all(rows, 'aux', split_axis=0, concat_axis=0, tiled=True)  8.57 us
    all_to_all x1, waiting for transfers between devices, on_device(): block = lax.all_to_all(rows, 'aux', split_axis=0, concat_axis=0, tiled=True)  6.19 us
    pallas_call x2, Pallas kernels, join(): pl.pallas_call(join_kernel, in_specs=[HBM] * 8, out_specs=[HBM] * 4, out_...  3.76 us
  transfers between devices with their start and end apart: 25, of which 19 were waited for; matrix products, arithmetic and copies ran while one was open for 5% of the time, Pallas kernels for 7%

profile of v6, /device:TPU:2, one launch (start us, length us, event | category | flops | bytes accessed | tf_op | source)
XLA Modules:
  0.0 164.6 jit_solution(13089788329980487894)
XLA Ops:
  3.2 8.6 %all-to-all-start = ((bf16[16,64,512]{2,1,0:T(8,128)(2,1)}), bf16[16,64,512]{2,1,0:T(8,128)(2,1)S(1)}, u32[]{:S(2)}, u32[]{:S(2)}) async-start(bf16[16,64,512]{2,1,0:T(8,128)(2,1)} %copy.76), calls=%async_computation | async-start | bytes 2097152 | tf_op jit(solution)/shard_map/all_to_all | solution.py:299
  17.5 1.9 %collective-permute-done.1 = s32[2,176]{1,0:T(2,128)S(1)} collective-permute-done((s32[2,176]{1,0:T(2,128)S(1)}, s32[2,176]{1,0:T(2,128)S(1)}, u32[]{:S(2)}, u32[]{:S(2)}) %collective-permute-start.1) | collective-permute-done | bytes 1440 | tf_op jit(solution)/shard_map/ppermute | solution.py:239
  21.2 1.9 %collective-permute-done.2 = s32[4,176]{1,0:T(4,128)S(1)} collective-permute-done((s32[4,176]{1,0:T(4,128)S(1)}, s32[4,176]{1,0:T(4,128)S(1)}, u32[]{:S(2)}, u32[]{:S(2)}) %collective-permute-start.2) | collective-permute-done | bytes 2848 | tf_op jit(solution)/shard_map/ppermute | solution.py:239
  23.2 3.0 %collective-permute-start.3 = (s32[8,176]{1,0:T(8,128)S(1)}, s32[8,176]{1,0:T(8,128)S(1)}, u32[]{:S(2)}, u32[]{:S(2)}) collective-permute-start(s32[8,176]{1,0:T(8,128)S(1)} %pad_add_fusion.2), channel_id=1, source_target_pairs={{0,3},{1,2},{2,1},{3,0},{4,7},{5,6},{6,5},{7,4},{8,11},{9,10},{10,... | collective-permute-start | bytes 16904 | tf_op jit(solution)/shard_map/ppermute | solution.py:239
  32.2 6.2 %all-to-all-done = bf16[16,64,512]{2,1,0:T(8,128)(2,1)S(1)} async-done(((bf16[16,64,512]{2,1,0:T(8,128)(2,1)}), bf16[16,64,512]{2,1,0:T(8,128)(2,1)S(1)}, u32[]{:S(2)}, u32[]{:S(2)}) %all-to-all-start) | async-done | bytes 1048608 | tf_op jit(solution)/shard_map/all_to_all | solution.py:299
  39.8 3.1 %collective-permute-start.7 = (bf16[1,512,256]{2,1,0:T(8,128)(2,1)S(1)}, bf16[1,512,256]{2,1,0:T(8,128)(2,1)S(1)}, u32[]{:S(2)}, u32[]{:S(2)}) collective-permute-start(bf16[1,512,256]{2,1,0:T(8,128)(2,1)S(1)} %get-tuple-element.57.refs_3_), channel_id=1, source_target_pairs={{0,3},{1,2},{2,1},{3,0},{4,7},{5,6},{6,5},{7,4},{8,11},{9,10},{10,... | collective-permute-start | bytes 786440 | tf_op jit(solution)/shard_map/ppermute | solution.py:239
  44.6 1.8 %collective-permute-start.4 = (bf16[1,512,256]{2,1,0:T(8,128)(2,1)S(1)}, bf16[1,512,256]{2,1,0:T(8,128)(2,1)S(1)}, u32[]{:S(2)}, u32[]{:S(2)}) collective-permute-start(bf16[1,512,256]{2,1,0:T(8,128)(2,1)S(1)} %get-tuple-element.60.refs_0_), channel_id=1, source_target_pairs={{0,4},{1,5},{2,6},{3,7},{4,0},{5,1},{6,2},{7,3},{8,12},{9,13},{10,... | collective-permute-start | bytes 786440 | tf_op jit(solution)/shard_map/ppermute | solution.py:239
  46.4 3.2 %collective-permute-done.7.refs_7_ = bf16[1,512,256]{2,1,0:T(8,128)(2,1)S(1)} collective-permute-done((bf16[1,512,256]{2,1,0:T(8,128)(2,1)S(1)}, bf16[1,512,256]{2,1,0:T(8,128)(2,1)S(1)}, u32[]{:S(2)}, u32[]{:S(2)}) %collective-permute-start.7) | collective-permute-done | bytes 262176 | tf_op jit(solution)/shard_map/ppermute | solution.py:239
  49.6 2.2 %collective-permute-done.6.refs_6_ = bf16[1,512,256]{2,1,0:T(8,128)(2,1)S(1)} collective-permute-done((bf16[1,512,256]{2,1,0:T(8,128)(2,1)S(1)}, bf16[1,512,256]{2,1,0:T(8,128)(2,1)S(1)}, u32[]{:S(2)}, u32[]{:S(2)}) %collective-permute-start.6) | collective-permute-done | bytes 262176 | tf_op jit(solution)/shard_map/ppermute | solution.py:239
  58.3 9.8 %collective-permute-done.8.refs_4_ = bf16[2,512,256]{2,1,0:T(8,128)(2,1)S(1)} collective-permute-done((bf16[2,512,256]{2,1,0:T(8,128)(2,1)S(1)}, bf16[2,512,256]{2,1,0:T(8,128)(2,1)S(1)}, u32[]{:S(2)}, u32[]{:S(2)}) %collective-permute-start.8) | collective-permute-done | bytes 524320 | tf_op jit(solution)/shard_map/ppermute | solution.py:239
  70.7 3.4 %shard_map.128 = (bf16[4,512,256]{2,1,0:T(8,128)(2,1)}, bf16[4,512,256]{2,1,0:T(8,128)(2,1)}, bf16[4,512,256]{2,1,0:T(8,128)(2,1)}, bf16[4,512,256]{2,1,0:T(8,128)(2,1)}) custom-call(bf16[2,512,256]{2,1,0:T(8,128)(2,1)} %copy-done.2, bf16[2,512,256]{2,1,0:T(8,128)(2,1)} %copy-done.3, bf16[2,512,256]{2,1,0:T(8,128)(2,1)} %copy-done.4, ...), custom_call_target="tpu_custom_call" | custom-call | bytes 8388608 | tf_op jit(solution)/shard_map/pallas_call | solution.py:271
  74.0 2.8 %collective-permute-start.20 = (bf16[4,512,256]{2,1,0:T(8,128)(2,1)}, bf16[4,512,256]{2,1,0:T(8,128)(2,1)S(1)}, u32[]{:S(2)}, u32[]{:S(2)}) collective-permute-start(bf16[4,512,256]{2,1,0:T(8,128)(2,1)} %get-tuple-element.42), channel_id=1, source_target_pairs={{0,3},{1,2},{2,1},{3,0},{4,7},{5,6},{6,5},{7,4},{8,11},{9,10},{10,... | collective-permute-start | bytes 3145736 | tf_op jit(solution)/shard_map/ppermute | solution.py:239
  76.9 2.2 %collective-permute-start.21 = (bf16[4,512,256]{2,1,0:T(8,128)(2,1)}, bf16[4,512,256]{2,1,0:T(8,128)(2,1)S(1)}, u32[]{:S(2)}, u32[]{:S(2)}) collective-permute-start(bf16[4,512,256]{2,1,0:T(8,128)(2,1)} %get-tuple-element.43), channel_id=1, source_target_pairs={{0,12},{1,13},{2,14},{3,15},{4,8},{5,9},{6,10},{7,11},{8,4},{9,5},... | collective-permute-start | bytes 3145736 | tf_op jit(solution)/shard_map/ppermute | solution.py:239
  82.2 17.4 %collective-permute-done.20 = bf16[4,512,256]{2,1,0:T(8,128)(2,1)S(1)} collective-permute-done((bf16[4,512,256]{2,1,0:T(8,128)(2,1)}, bf16[4,512,256]{2,1,0:T(8,128)(2,1)S(1)}, u32[]{:S(2)}, u32[]{:S(2)}) %collective-permute-start.20) | collective-permute-done | bytes 1048608 | tf_op jit(solution)/shard_map/ppermute | solution.py:239
  99.6 2.2 %collective-permute-start.16 = (bf16[4,512,256]{2,1,0:T(8,128)(2,1)}, bf16[4,512,256]{2,1,0:T(8,128)(2,1)}, u32[]{:S(2)}, u32[]{:S(2)}) collective-permute-start(bf16[4,512,256]{2,1,0:T(8,128)(2,1)} %get-tuple-element.44), channel_id=1, source_target_pairs={{0,3},{1,2},{2,1},{3,0},{4,7},{5,6},{6,5},{7,4},{8,11},{9,10},{10,... | collective-permute-start | bytes 3145736 | tf_op jit(solution)/shard_map/ppermute | solution.py:239
  103.2 1.8 %collective-permute-start.18 = (bf16[4,512,256]{2,1,0:T(8,128)(2,1)}, bf16[4,512,256]{2,1,0:T(8,128)(2,1)}, u32[]{:S(2)}, u32[]{:S(2)}) collective-permute-start(bf16[4,512,256]{2,1,0:T(8,128)(2,1)} %get-tuple-element.45), channel_id=1, source_target_pairs={{0,12},{1,13},{2,14},{3,15},{4,8},{5,9},{6,10},{7,11},{8,4},{9,5},... | collective-permute-start | bytes 3145736 | tf_op jit(solution)/shard_map/ppermute | solution.py:239
  108.4 14.4 %collective-permute-done.22 = bf16[4,512,256]{2,1,0:T(8,128)(2,1)} collective-permute-done((bf16[4,512,256]{2,1,0:T(8,128)(2,1)}, bf16[4,512,256]{2,1,0:T(8,128)(2,1)}, u32[]{:S(2)}, u32[]{:S(2)}) %collective-permute-start.22) | collective-permute-done | bytes 1048608 | tf_op jit(solution)/shard_map/ppermute | solution.py:239
  122.8 1.8 %collective-permute-start.15 = (bf16[4,512,256]{2,1,0:T(8,128)(2,1)}, bf16[4,512,256]{2,1,0:T(8,128)(2,1)}, u32[]{:S(2)}, u32[]{:S(2)}) collective-permute-start(bf16[4,512,256]{2,1,0:T(8,128)(2,1)} %collective-permute-done.14), channel_id=1, source_target_pairs={{0,12},{1,13},{2,14},{3,15},{4,8},{5,9},{6,10},{7,11},{8,4},{9,5},... | collective-permute-start | bytes 3145736 | tf_op jit(solution)/shard_map/ppermute | solution.py:239
  124.6 2.6 %collective-permute-done.16 = bf16[4,512,256]{2,1,0:T(8,128)(2,1)} collective-permute-done((bf16[4,512,256]{2,1,0:T(8,128)(2,1)}, bf16[4,512,256]{2,1,0:T(8,128)(2,1)}, u32[]{:S(2)}, u32[]{:S(2)}) %collective-permute-start.16) | collective-permute-done | bytes 1048608 | tf_op jit(solution)/shard_map/ppermute | solution.py:239
  127.2 2.1 %collective-permute-start.19 = (bf16[4,512,256]{2,1,0:T(8,128)(2,1)}, bf16[4,512,256]{2,1,0:T(8,128)(2,1)}, u32[]{:S(2)}, u32[]{:S(2)}) collective-permute-start(bf16[4,512,256]{2,1,0:T(8,128)(2,1)} %collective-permute-done.18), channel_id=1, source_target_pairs={{0,4},{1,5},{2,6},{3,7},{4,0},{5,1},{6,2},{7,3},{8,12},{9,13},{10,... | collective-permute-start | bytes 3145736 | tf_op jit(solution)/shard_map/ppermute | solution.py:239
  130.2 11.9 %shard_map.129 = (bf16[4,32,256,256]{3,2,1,0:T(8,128)(2,1)S(1)}, f32[16,256,256]{2,1,0:T(8,128)S(1)}) custom-call(s32[4,192]{1,0:T(4,128)} %fusion.5.idx, f32[128]{0:T(128)} %pad_maximum_fusion.wts, f32[96]{0:T(128)} %add_bitcast_fusion.dsum, f32[1,256]{1,0:T(1,128)} %bitcast.55, f32[256,1]{1,0:T(8,128)} %copy.89.vcol, bf16[8,256,256]{2,1,0:T(8,128)(2,1)} %bitcast.60, ...), custom_call_target="tpu_custom_call" | custom-call | flops 2684354560 | bytes 12582912 | tf_op jit(solution)/shard_map/pallas_call | solution.py:136
  142.1 4.5 %collective-permute-done.13 = bf16[4,512,256]{2,1,0:T(8,128)(2,1)S(1)} collective-permute-done((bf16[4,512,256]{2,1,0:T(8,128)(2,1)}, bf16[4,512,256]{2,1,0:T(8,128)(2,1)S(1)}, u32[]{:S(2)}, u32[]{:S(2)}) %collective-permute-start.13) | collective-permute-done | bytes 1048608 | tf_op jit(solution)/shard_map/ppermute | solution.py:239
  146.8 2.0 %collective-permute-done.19 = bf16[4,512,256]{2,1,0:T(8,128)(2,1)} collective-permute-done((bf16[4,512,256]{2,1,0:T(8,128)(2,1)}, bf16[4,512,256]{2,1,0:T(8,128)(2,1)}, u32[]{:S(2)}, u32[]{:S(2)}) %collective-permute-start.19) | collective-permute-done | bytes 1048608 | tf_op jit(solution)/shard_map/ppermute | solution.py:239
  148.9 15.5 %shard_map.130 = (f32[16,256,256]{2,1,0:T(8,128)}, bf16[4,32,256,256]{3,2,1,0:T(8,128)(2,1)S(1)}, f32[16,256,256]{2,1,0:T(8,128)S(1)}) custom-call(s32[4,192]{1,0:T(4,128)S(1)} %copy-done.6, f32[128]{0:T(128)S(1)} %copy-done.9, f32[96]{0:T(128)S(1)} %copy-done.10, f32[1,256]{1,0:T(1,128)S(1)} %bitcast.57, ...), custom_call_target="tpu_custom_call", output_to_operand_aliasing={{1}: (10, {}), {2}: (11, {})} | custom-call | flops 10737418240 | bytes 8388608 | tf_op jit(solution)/shard_map/pallas_call | solution.py:154
  (146 shorter events, 37.6 us)
Async XLA Ops:
  3.2 35.2 %all-to-all-start = ((bf16[16,64,512]{2,1,0:T(8,128)(2,1)}), bf16[16,64,512]{2,1,0:T(8,128)(2,1)S(1)}, u32[]{:S(2)}, u32[]{:S(2)}) async-start(bf16[16,64,512]{2,1,0:T(8,128)(2,1)} %copy.76), calls=%async_computation | async-start | bytes 2097152 | tf_op jit(solution)/shard_map/all_to_all | solution.py:299
  15.8 3.6 %collective-permute-start.1 = (s32[2,176]{1,0:T(2,128)S(1)}, s32[2,176]{1,0:T(2,128)S(1)}, u32[]{:S(2)}, u32[]{:S(2)}) collective-permute-start(s32[2,176]{1,0:T(2,128)S(1)} %pad_add_fusion.4), channel_id=1, source_target_pairs={{0,12},{1,13},{2,14},{3,15},{4,8},{5,9},{6,10},{7,11},{8,4},{9,5},... | collective-permute-start | bytes 4232 | tf_op jit(solution)/shard_map/ppermute | solution.py:239
  19.5 3.6 %collective-permute-start.2 = (s32[4,176]{1,0:T(4,128)S(1)}, s32[4,176]{1,0:T(4,128)S(1)}, u32[]{:S(2)}, u32[]{:S(2)}) collective-permute-start(s32[4,176]{1,0:T(4,128)S(1)} %pad_add_fusion.3), channel_id=1, source_target_pairs={{0,1},{1,0},{2,3},{3,2},{4,5},{5,4},{6,7},{7,6},{8,9},{9,8},{10,11... | collective-permute-start | bytes 8456 | tf_op jit(solution)/shard_map/ppermute | solution.py:239
  23.2 4.9 %collective-permute-start.3 = (s32[8,176]{1,0:T(8,128)S(1)}, s32[8,176]{1,0:T(8,128)S(1)}, u32[]{:S(2)}, u32[]{:S(2)}) collective-permute-start(s32[8,176]{1,0:T(8,128)S(1)} %pad_add_fusion.2), channel_id=1, source_target_pairs={{0,3},{1,2},{2,1},{3,0},{4,7},{5,6},{6,5},{7,4},{8,11},{9,10},{10,... | collective-permute-start | bytes 16904 | tf_op jit(solution)/shard_map/ppermute | solution.py:239
  39.8 9.7 %collective-permute-start.7 = (bf16[1,512,256]{2,1,0:T(8,128)(2,1)S(1)}, bf16[1,512,256]{2,1,0:T(8,128)(2,1)S(1)}, u32[]{:S(2)}, u32[]{:S(2)}) collective-permute-start(bf16[1,512,256]{2,1,0:T(8,128)(2,1)S(1)} %get-tuple-element.57.refs_3_), channel_id=1, source_target_pairs={{0,3},{1,2},{2,1},{3,0},{4,7},{5,6},{6,5},{7,4},{8,11},{9,10},{10,... | collective-permute-start | bytes 786440 | tf_op jit(solution)/shard_map/ppermute | solution.py:239
  42.9 8.8 %collective-permute-start.6 = (bf16[1,512,256]{2,1,0:T(8,128)(2,1)S(1)}, bf16[1,512,256]{2,1,0:T(8,128)(2,1)S(1)}, u32[]{:S(2)}, u32[]{:S(2)}) collective-permute-start(bf16[1,512,256]{2,1,0:T(8,128)(2,1)S(1)} %get-tuple-element.58.refs_2_), channel_id=1, source_target_pairs={{0,12},{1,13},{2,14},{3,15},{4,8},{5,9},{6,10},{7,11},{8,4},{9,5},... | collective-permute-start | bytes 786440 | tf_op jit(solution)/shard_map/ppermute | solution.py:239
  44.4 9.0 %collective-permute-start.5 = (bf16[1,512,256]{2,1,0:T(8,128)(2,1)S(1)}, bf16[1,512,256]{2,1,0:T(8,128)(2,1)S(1)}, u32[]{:S(2)}, u32[]{:S(2)}) collective-permute-start(bf16[1,512,256]{2,1,0:T(8,128)(2,1)S(1)} %get-tuple-element.59.refs_1_), channel_id=1, source_target_pairs={{0,1},{1,0},{2,3},{3,2},{4,5},{5,4},{6,7},{7,6},{8,9},{9,8},{10,11... | collective-permute-start | bytes 786440 | tf_op jit(solution)/shard_map/ppermute | solution.py:239
  44.6 9.1 %collective-permute-start.4 = (bf16[1,512,256]{2,1,0:T(8,128)(2,1)S(1)}, bf16[1,512,256]{2,1,0:T(8,128)(2,1)S(1)}, u32[]{:S(2)}, u32[]{:S(2)}) collective-permute-start(bf16[1,512,256]{2,1,0:T(8,128)(2,1)S(1)} %get-tuple-element.60.refs_0_), channel_id=1, source_target_pairs={{0,4},{1,5},{2,6},{3,7},{4,0},{5,1},{6,2},{7,3},{8,12},{9,13},{10,... | collective-permute-start | bytes 786440 | tf_op jit(solution)/shard_map/ppermute | solution.py:239
  54.1 14.0 %collective-permute-start.8 = (bf16[2,512,256]{2,1,0:T(8,128)(2,1)S(1)}, bf16[2,512,256]{2,1,0:T(8,128)(2,1)S(1)}, u32[]{:S(2)}, u32[]{:S(2)}) collective-permute-start(bf16[2,512,256]{2,1,0:T(8,128)(2,1)S(1)} %get-tuple-element.38.refs_0_), channel_id=1, source_target_pairs={{0,12},{1,13},{2,14},{3,15},{4,8},{5,9},{6,10},{7,11},{8,4},{9,5},... | collective-permute-start | bytes 1572872 | tf_op jit(solution)/shard_map/ppermute | solution.py:239
  54.8 14.9 %collective-permute-start.9 = (bf16[2,512,256]{2,1,0:T(8,128)(2,1)S(1)}, bf16[2,512,256]{2,1,0:T(8,128)(2,1)S(1)}, u32[]{:S(2)}, u32[]{:S(2)}) collective-permute-start(bf16[2,512,256]{2,1,0:T(8,128)(2,1)S(1)} %get-tuple-element.39.refs_1_), channel_id=1, source_target_pairs={{0,3},{1,2},{2,1},{3,0},{4,7},{5,6},{6,5},{7,4},{8,11},{9,10},{10,... | collective-permute-start | bytes 1572872 | tf_op jit(solution)/shard_map/ppermute | solution.py:239
  55.7 13.9 %collective-permute-start.10 = (bf16[2,512,256]{2,1,0:T(8,128)(2,1)S(1)}, bf16[2,512,256]{2,1,0:T(8,128)(2,1)S(1)}, u32[]{:S(2)}, u32[]{:S(2)}) collective-permute-start(bf16[2,512,256]{2,1,0:T(8,128)(2,1)S(1)} %get-tuple-element.40.refs_2_), channel_id=1, source_target_pairs={{0,4},{1,5},{2,6},{3,7},{4,0},{5,1},{6,2},{7,3},{8,12},{9,13},{10,... | collective-permute-start | bytes 1572872 | tf_op jit(solution)/shard_map/ppermute | solution.py:239
  57.5 13.1 %collective-permute-start.11 = (bf16[2,512,256]{2,1,0:T(8,128)(2,1)S(1)}, bf16[2,512,256]{2,1,0:T(8,128)(2,1)}, u32[]{:S(2)}, u32[]{:S(2)}) collective-permute-start(bf16[2,512,256]{2,1,0:T(8,128)(2,1)S(1)} %get-tuple-element.41.refs_3_), channel_id=1, source_target_pairs={{0,1},{1,0},{2,3},{3,2},{4,5},{5,4},{6,7},{7,6},{8,9},{9,8},{10,11... | collective-permute-start | bytes 1572872 | tf_op jit(solution)/shard_map/ppermute | solution.py:239
  74.0 25.5 %collective-permute-start.20 = (bf16[4,512,256]{2,1,0:T(8,128)(2,1)}, bf16[4,512,256]{2,1,0:T(8,128)(2,1)S(1)}, u32[]{:S(2)}, u32[]{:S(2)}) collective-permute-start(bf16[4,512,256]{2,1,0:T(8,128)(2,1)} %get-tuple-element.42), channel_id=1, source_target_pairs={{0,3},{1,2},{2,1},{3,0},{4,7},{5,6},{6,5},{7,4},{8,11},{9,10},{10,... | collective-permute-start | bytes 3145736 | tf_op jit(solution)/shard_map/ppermute | solution.py:239
  76.8 26.4 %collective-permute-start.12 = (bf16[4,512,256]{2,1,0:T(8,128)(2,1)}, bf16[4,512,256]{2,1,0:T(8,128)(2,1)}, u32[]{:S(2)}, u32[]{:S(2)}) collective-permute-start(bf16[4,512,256]{2,1,0:T(8,128)(2,1)} %get-tuple-element.42), channel_id=1, source_target_pairs={{0,1},{1,0},{2,3},{3,2},{4,5},{5,4},{6,7},{7,6},{8,9},{9,8},{10,11... | collective-permute-start | bytes 3145736 | tf_op jit(solution)/shard_map/ppermute | solution.py:239
  76.9 28.1 %collective-permute-start.21 = (bf16[4,512,256]{2,1,0:T(8,128)(2,1)}, bf16[4,512,256]{2,1,0:T(8,128)(2,1)S(1)}, u32[]{:S(2)}, u32[]{:S(2)}) collective-permute-start(bf16[4,512,256]{2,1,0:T(8,128)(2,1)} %get-tuple-element.43), channel_id=1, source_target_pairs={{0,12},{1,13},{2,14},{3,15},{4,8},{5,9},{6,10},{7,11},{8,4},{9,5},... | collective-permute-start | bytes 3145736 | tf_op jit(solution)/shard_map/ppermute | solution.py:239
  79.1 27.5 %collective-permute-start.14 = (bf16[4,512,256]{2,1,0:T(8,128)(2,1)}, bf16[4,512,256]{2,1,0:T(8,128)(2,1)}, u32[]{:S(2)}, u32[]{:S(2)}) collective-permute-start(bf16[4,512,256]{2,1,0:T(8,128)(2,1)} %get-tuple-element.43), channel_id=1, source_target_pairs={{0,4},{1,5},{2,6},{3,7},{4,0},{5,1},{6,2},{7,3},{8,12},{9,13},{10,... | collective-permute-start | bytes 3145736 | tf_op jit(solution)/shard_map/ppermute | solution.py:239
  80.6 42.2 %collective-permute-start.22 = (bf16[4,512,256]{2,1,0:T(8,128)(2,1)}, bf16[4,512,256]{2,1,0:T(8,128)(2,1)}, u32[]{:S(2)}, u32[]{:S(2)}) collective-permute-start(bf16[4,512,256]{2,1,0:T(8,128)(2,1)} %get-tuple-element.44), channel_id=1, source_target_pairs={{0,1},{1,0},{2,3},{3,2},{4,5},{5,4},{6,7},{7,6},{8,9},{9,8},{10,11... | collective-permute-start | bytes 3145736 | tf_op jit(solution)/shard_map/ppermute | solution.py:239
  99.6 27.6 %collective-permute-start.16 = (bf16[4,512,256]{2,1,0:T(8,128)(2,1)}, bf16[4,512,256]{2,1,0:T(8,128)(2,1)}, u32[]{:S(2)}, u32[]{:S(2)}) collective-permute-start(bf16[4,512,256]{2,1,0:T(8,128)(2,1)} %get-tuple-element.44), channel_id=1, source_target_pairs={{0,3},{1,2},{2,1},{3,0},{4,7},{5,6},{6,5},{7,4},{8,11},{9,10},{10,... | collective-permute-start | bytes 3145736 | tf_op jit(solution)/shard_map/ppermute | solution.py:239
  103.2 24.0 %collective-permute-start.18 = (bf16[4,512,256]{2,1,0:T(8,128)(2,1)}, bf16[4,512,256]{2,1,0:T(8,128)(2,1)}, u32[]{:S(2)}, u32[]{:S(2)}) collective-permute-start(bf16[4,512,256]{2,1,0:T(8,128)(2,1)} %get-tuple-element.45), channel_id=1, source_target_pairs={{0,12},{1,13},{2,14},{3,15},{4,8},{5,9},{6,10},{7,11},{8,4},{9,5},... | collective-permute-start | bytes 3145736 | tf_op jit(solution)/shard_map/ppermute | solution.py:239
  105.1 25.1 %collective-permute-start.23 = (bf16[4,512,256]{2,1,0:T(8,128)(2,1)}, bf16[4,512,256]{2,1,0:T(8,128)(2,1)}, u32[]{:S(2)}, u32[]{:S(2)}) collective-permute-start(bf16[4,512,256]{2,1,0:T(8,128)(2,1)} %get-tuple-element.45), channel_id=1, source_target_pairs={{0,4},{1,5},{2,6},{3,7},{4,0},{5,1},{6,2},{7,3},{8,12},{9,13},{10,... | collective-permute-start | bytes 3145736 | tf_op jit(solution)/shard_map/ppermute | solution.py:239
  106.6 40.0 %collective-permute-start.13 = (bf16[4,512,256]{2,1,0:T(8,128)(2,1)}, bf16[4,512,256]{2,1,0:T(8,128)(2,1)S(1)}, u32[]{:S(2)}, u32[]{:S(2)}) collective-permute-start(bf16[4,512,256]{2,1,0:T(8,128)(2,1)} %collective-permute-done.12), channel_id=1, source_target_pairs={{0,3},{1,2},{2,1},{3,0},{4,7},{5,6},{6,5},{7,4},{8,11},{9,10},{10,... | collective-permute-start | bytes 3145736 | tf_op jit(solution)/shard_map/ppermute | solution.py:239
  122.8 24.0 %collective-permute-start.15 = (bf16[4,512,256]{2,1,0:T(8,128)(2,1)}, bf16[4,512,256]{2,1,0:T(8,128)(2,1)}, u32[]{:S(2)}, u32[]{:S(2)}) collective-permute-start(bf16[4,512,256]{2,1,0:T(8,128)(2,1)} %collective-permute-done.14), channel_id=1, source_target_pairs={{0,12},{1,13},{2,14},{3,15},{4,8},{5,9},{6,10},{7,11},{8,4},{9,5},... | collective-permute-start | bytes 3145736 | tf_op jit(solution)/shard_map/ppermute | solution.py:239
  127.2 19.6 %collective-permute-start.17 = (bf16[4,512,256]{2,1,0:T(8,128)(2,1)}, bf16[4,512,256]{2,1,0:T(8,128)(2,1)}, u32[]{:S(2)}, u32[]{:S(2)}) collective-permute-start(bf16[4,512,256]{2,1,0:T(8,128)(2,1)} %collective-permute-done.16), channel_id=1, source_target_pairs={{0,1},{1,0},{2,3},{3,2},{4,5},{5,4},{6,7},{7,6},{8,9},{9,8},{10,11... | collective-permute-start | bytes 3145736 | tf_op jit(solution)/shard_map/ppermute | solution.py:239
  127.2 21.6 %collective-permute-start.19 = (bf16[4,512,256]{2,1,0:T(8,128)(2,1)}, bf16[4,512,256]{2,1,0:T(8,128)(2,1)}, u32[]{:S(2)}, u32[]{:S(2)}) collective-permute-start(bf16[4,512,256]{2,1,0:T(8,128)(2,1)} %collective-permute-done.18), channel_id=1, source_target_pairs={{0,4},{1,5},{2,6},{3,7},{4,0},{5,1},{6,2},{7,3},{8,12},{9,13},{10,... | collective-permute-start | bytes 3145736 | tf_op jit(solution)/shard_map/ppermute | solution.py:239
  (25 other events, 470.8 us)

commit v7 on v6

--- a/solution.py
+++ b/solution.py
@@ -16,12 +16,12 @@
     return r * (2.0 - x * r)
 
 
-def listed(idx, wts, order, soon):
+def listed(idx, twin, order, soon):
     def entry(n, count):
         last = idx[0, 32 + n]
         for q in range(4):
             last = jnp.maximum(last, jnp.maximum(idx[q, 32 + n], idx[q, 128 + n]))
-        hit = (wts[64 + n] != 0.0) & ((last < 24) == soon)
+        hit = (twin[n] >= -1) & ((last < 24) == soon)
 
         @pl.when(hit)
         def _():
@@ -41,7 +41,7 @@
     return lax.dot_general(left, right, NT, preferred_element_type=jnp.float32)
 
 
-def add_coupled(idx, wts, dsum, pool, mixed, vsum, order, trips):
+def add_coupled(idx, wts, twin, dsum, pool, mixed, vsum, order, trips):
     def coupled(g, carry):
         for u in range(UNROLL):
             entry = order[UNROLL * g + u]
@@ -51,12 +51,15 @@
             start = -(product(idx, pool, 32 + at) * recip(vsum[...] - dsum[32 + at]))
             rounded = start.astype(jnp.bfloat16).astype(jnp.float32)
             mixed[n // 4] += weight * rounded
+            other = jnp.where(entry >= 0, twin[n], -1)
+            m = jnp.maximum(other, 0)
+            mixed[m // 4] += jnp.where(other >= 0, wts[64 + m], 0.0) * rounded
         return carry
 
     lax.fori_loop(0, trips, coupled, 0)
 
 
-def early_kernel(idx, wts, dsum, vrow, vcol, *refs):
+def early_kernel(idx, wts, twin, dsum, vrow, vcol, *refs):
     pieces, pool, mixed, vsum, order, sems = refs[:12], *refs[12:]
     copies = [
         pltpu.make_async_copy(
@@ -67,7 +70,7 @@
     ]
     for copy in copies:
         copy.start()
-    trips = listed(idx, wts, order, True)
+    trips = listed(idx, twin, order, True)
     vsum[...] = vrow[...] + vcol[...]
 
     def clear(s, carry):
@@ -77,21 +80,21 @@
     lax.fori_loop(0, 16, clear, 0)
     for copy in copies:
         copy.wait()
-    add_coupled(idx, wts, dsum, pool, mixed, vsum, order, trips)
-
-
-def last_kernel(idx, wts, dsum, vrow, vcol, slot, *refs):
+    add_coupled(idx, wts, twin, dsum, pool, mixed, vsum, order, trips)
+
+
+def last_kernel(idx, wts, twin, dsum, vrow, vcol, slot, *refs):
     pieces, _, _, out, pool, mixed, amp, vsum, order, sems, out_sems = refs[:4], *refs[4:]
     copies = [
         pltpu.make_async_copy(pieces[q], pool.at[q, pl.ds(24, 8)], sems.at[q]) for q in range(4)
     ]
     for copy in copies:
         copy.start()
-    trips = listed(idx, wts, order, False)
+    trips = listed(idx, twin, order, False)
     vsum[...] = vrow[...] + vcol[...]
     for copy in copies:
         copy.wait()
-    add_coupled(idx, wts, dsum, pool, mixed, vsum, order, trips)
+    add_coupled(idx, wts, twin, dsum, pool, mixed, vsum, order, trips)
 
     def received(g, carry):
         for u in range(UNROLL):
@@ -100,9 +103,8 @@
             amp[s] = value.astype(jnp.bfloat16)
         return carry
 
-    def out_copy(g):
-        rows = pl.ds(UNROLL * g, UNROLL)
-        return pltpu.make_async_copy(mixed.at[rows], out.at[rows], out_sems.at[g])
+    def out_copy(p):
+        return pltpu.make_async_copy(mixed.at[p], out.at[p], out_sems.at[p])
 
     def own(g, carry):
         for u in range(UNROLL):
@@ -111,16 +113,16 @@
             for e in range(4):
                 total += wts[4 * p + e] * amp[slot[4 * p + e]].astype(jnp.float32)
             mixed[p] = total * recip(vsum[...] - dsum[p])
-        out_copy(g).start()
-        return carry
-
-    def finish(g, carry):
-        out_copy(g).wait()
+            out_copy(p).start()
+        return carry
+
+    def finish(p, carry):
+        out_copy(p).wait()
         return carry
 
     lax.fori_loop(0, 16 // UNROLL, received, 0)
     lax.fori_loop(0, 16 // UNROLL, own, 0)
-    lax.fori_loop(0, 16 // UNROLL, finish, 0)
+    lax.fori_loop(0, 16, finish, 0)
 
 
 SMEM = pl.BlockSpec(memory_space=pltpu.SMEM)
@@ -132,10 +134,10 @@
 SUMS = pltpu.VMEM((16, 256, 256), jnp.float32)
 
 
-def early_sums(idx, wts, dsum, vrow, vcol, pieces):
+def early_sums(idx, wts, twin, dsum, vrow, vcol, pieces):
     return pl.pallas_call(
         early_kernel,
-        in_specs=[SMEM] * 3 + [VMEM] * 2 + [HBM] * 12,
+        in_specs=[SMEM] * 4 + [VMEM] * 2 + [HBM] * 12,
         out_specs=[VMEM] * 2,
         out_shape=[POOL, SUMS],
         scratch_shapes=[
@@ -147,28 +149,28 @@
         cost_estimate=pl.CostEstimate(
             flops=20 * 2 * 256 * 256 * 1024, bytes_accessed=12 * MIB, transcendentals=0
         ),
-    )(idx, wts, dsum, vrow, vcol, *pieces)
-
-
-def amplitudes(idx, wts, dsum, vrow, vcol, slot, pieces, pool, sums):
+    )(idx, wts, twin, dsum, vrow, vcol, *pieces)
+
+
+def amplitudes(idx, wts, twin, dsum, vrow, vcol, slot, pieces, pool, sums):
     return pl.pallas_call(
         last_kernel,
-        in_specs=[SMEM] * 3 + [VMEM] * 2 + [SMEM] + [HBM] * 4 + [VMEM] * 2,
+        in_specs=[SMEM] * 4 + [VMEM] * 2 + [SMEM] + [HBM] * 4 + [VMEM] * 2,
         out_specs=[HBM] + [VMEM] * 2,
         out_shape=[jax.ShapeDtypeStruct((16, 256, 256), jnp.float32), POOL, SUMS],
-        input_output_aliases={10: 1, 11: 2},
+        input_output_aliases={11: 1, 12: 2},
         scratch_shapes=[
             pltpu.VMEM((16, 256, 256), jnp.bfloat16),
             pltpu.VMEM((256, 256), jnp.float32),
             pltpu.SMEM((72,), jnp.int32),
             pltpu.SemaphoreType.DMA((4,)),
-            pltpu.SemaphoreType.DMA((4,)),
+            pltpu.SemaphoreType.DMA((16,)),
         ],
         compiler_params=pltpu.CompilerParams(vmem_limit_bytes=8 * MIB),
         cost_estimate=pl.CostEstimate(
             flops=80 * 2 * 256 * 256 * 1024, bytes_accessed=8 * MIB, transcendentals=0
         ),
-    )(idx, wts, dsum, vrow, vcol, slot, *pieces, pool, sums)[0]
+    )(idx, wts, twin, dsum, vrow, vcol, slot, *pieces, pool, sums)[0]
 
 
 def lookup(table, rows, cols):
@@ -203,6 +205,16 @@
     return jnp.sum(jnp.where(hit, ids, 0), axis=-1)
 
 
+def twins(pairs, wts):
+    n = jnp.arange(64, dtype=jnp.int32)
+    code = jnp.where(wts != 0.0, pairs[:, 0] * 32 + pairs[:, 1], -1 - n)
+    same = code[:, None] == code[None, :]
+    rank = jnp.sum((same & (n[None, :] < n[:, None])).astype(jnp.int32), axis=1)
+    after = same & (rank[None, :] == rank[:, None] + 1)
+    second = jnp.max(jnp.where(after, n[None, :], -1), axis=1)
+    return jnp.where((wts != 0.0) & (rank % 2 == 0), second, -2)
+
+
 def tables(metas, fock, orb, cpl, cpl_slot):
     col = lax.axis_index("aux")
     grp = lax.axis_index("grp")
@@ -232,7 +244,7 @@
     offset = (flat // 2) ^ grp
     spot = jnp.stack([found_in(offset, arrival(masks)) for masks in MASKS])
     slot = found_in(cpl_slot.reshape(64) ^ grp, arrival(MASKS[0]))
-    return spot * 2 + flat % 2, wts, slot, dsum
+    return spot * 2 + flat % 2, wts, twins(cpl_q.reshape(64, 2), wts[64:]), slot, dsum
 
 
 def swap(block, mask):
@@ -282,6 +294,53 @@
     )(*held, *got)
 
 
+def stage_kernel(*refs):
+    held, staged = refs[:4], refs[4:8]
+    part, in_sems, out_sems = refs[8:12], refs[12], refs[13]
+    ins = [pltpu.make_async_copy(held[q], part[q], in_sems.at[q]) for q in range(4)]
+    outs = [
+        pltpu.make_async_copy(part[q], staged[q].at[pl.ds(0, 2)], out_sems.at[q]) for q in range(4)
+    ]
+    for copy in ins:
+        copy.start()
+    for copy, out in zip(ins, outs):
+        copy.wait()
+        out.start()
+    for out in outs:
+        out.wait()
+
+
+def fill_kernel(*refs):
+    got, whole = refs[:4], refs[8:12]
+    part, in_sems, out_sems = refs[12:16], refs[16], refs[17]
+    ins = [pltpu.make_async_copy(got[q], part[q], in_sems.at[q]) for q in range(4)]
+    outs = [
+        pltpu.make_async_copy(part[q], whole[q].at[pl.ds(2, 2)], out_sems.at[q]) for q in range(4)
+    ]
+    for copy in ins:
+        copy.start()
+    for copy, out in zip(ins, outs):
+        copy.wait()
+        out.start()
+    for out in outs:
+        out.wait()
+
+
+def half_call(kernel, blocks, staged):
+    shape = (4, *blocks[0].shape[1:])
+    return pl.pallas_call(
+        kernel,
+        in_specs=[HBM] * (4 + len(staged)),
+        out_specs=[HBM] * 4,
+        out_shape=[jax.ShapeDtypeStruct(shape, jnp.bfloat16)] * 4,
+        input_output_aliases={4 + q: q for q in range(len(staged))},
+        scratch_shapes=[pltpu.VMEM(blocks[0].shape, jnp.bfloat16)] * 4
+        + [pltpu.SemaphoreType.DMA((4,)), pltpu.SemaphoreType.DMA((4,))],
+        compiler_params=pltpu.CompilerParams(vmem_limit_bytes=58 * MIB),
+        cost_estimate=pl.CostEstimate(flops=0, bytes_accessed=4 * MIB, transcendentals=0),
+    )(*blocks, *staged)
+
+
 def on_device(
     integrals, metric, fock, virt_energy, send_orb, pair_orb, send_pair, cpl_slot, cpl_orb
 ):
@@ -298,7 +357,7 @@
 
     block = lax.all_to_all(rows, "aux", split_axis=0, concat_axis=0, tiled=True)
     given = (*tables(metas, fock, orb, cpl, cpl_slot), virt_energy[None, :], virt_energy[:, None])
-    block, (idx, wts, slot, dsum, vrow, vcol) = lax.optimization_barrier((block, given))
+    block, (idx, wts, twin, slot, dsum, vrow, vcol) = lax.optimization_barrier((block, given))
     fitted = lax.dot_general(
         block.reshape(1024, 512),
         metric,
@@ -306,16 +365,17 @@
         preferred_element_type=jnp.float32,
     ).astype(jnp.bfloat16)
     held = [fitted[None, :, 256 * q : 256 * q + 256] for q in range(4)]
-    for step in range(2):
-        got = [swap(held[q], MASKS[q][step]) for q in range(4)]
-        held = join(held, got, (16, 58)[step])
+    got = [swap(held[q], MASKS[q][0]) for q in range(4)]
+    held = join(held, got, 16)
+    got = [swap(held[q], MASKS[q][1]) for q in range(4)]
+    held = half_call(fill_kernel, got, half_call(stage_kernel, held, []))
     third = [swap(held[q], MASKS[q][2]) for q in range(4)]
     early = [swap(held[q], MASKS[q][3]) for q in range(4)]
     late = [swap(third[q], MASKS[q][3]) for q in range(4)]
     soon = [x.reshape(8, 256, 256) for three in zip(held, third, early) for x in three]
-    pool, sums = early_sums(idx, wts, dsum, vrow, vcol, soon)
+    pool, sums = early_sums(idx, wts, twin, dsum, vrow, vcol, soon)
     late = [x.reshape(8, 256, 256) for x in late]
-    return amplitudes(idx, wts, dsum, vrow, vcol, slot, late, pool, sums)
+    return amplitudes(idx, wts, twin, dsum, vrow, vcol, slot, late, pool, sums)
 
 
 def solution(mesh):

time: 168 us -> 169 us (level)
  Pallas kernels: 31.2 us -> 33.9 us
  waiting for transfers between devices: 74.8 us -> 72.9 us
    pallas_call x2 -> x4, Pallas kernels: 27.4 us -> 33.5 us  [the longest x1 18.9 us: amplitudes(): pl.pallas_call(last_kernel, in_specs=[SMEM] * 4 + [VMEM] * 2 + [SMEM] + [...]
    pallas_call x2 -> x1, Pallas kernels: 3.76 us -> 0.41 us  [join(): pl.pallas_call(join_kernel, in_specs=[HBM] * 8, out_specs=[HBM] * 4, out_...]
  transfers between devices with their start and end apart: 25 -> 25, of which waited for: 19 -> 19; matrix products, arithmetic and copies ran while one was open for 5% -> 6% of each run, Pallas kernels for 7% -> 7%
where the time goes in v7:
time: 169 us; the launch traced here: 167 us
  waiting for transfers between devices  72.9 us (43%)
  starting transfers between devices  45.4 us (27%)
  Pallas kernels  33.9 us (20%)
  local copies, waits for them, and re-layouts  7.26 us (4%)
  other arithmetic  4.12 us (2%)
  matrix products  2.73 us (2%)
    ppermute x24, waiting for transfers between devices, swap(): return lax.ppermute(block, 'grp', [(g, g ^ mask) for g in range(16)])  68.4 us
    ppermute x24, starting transfers between devices, swap(): return lax.ppermute(block, 'grp', [(g, g ^ mask) for g in range(16)])  36.8 us
    pallas_call x1, Pallas kernels, amplitudes(): pl.pallas_call(last_kernel, in_specs=[SMEM] * 4 + [VMEM] * 2 + [SMEM] + [...  18.9 us
    pallas_call x1, Pallas kernels, early_sums(): pl.pallas_call(early_kernel, in_specs=[SMEM] * 4 + [VMEM] * 2 + [HBM] * 1...  9.71 us
    all_to_all x1, starting transfers between devices, on_device(): block = lax.all_to_all(rows, 'aux', split_axis=0, concat_axis=0, tiled=True)  8.57 us
    pallas_call x2, Pallas kernels, half_call(): pl.pallas_call(kernel, in_specs=[HBM] * (4 + len(staged)), out_specs=[HBM...  4.87 us
    all_to_all x1, waiting for transfers between devices, on_device(): block = lax.all_to_all(rows, 'aux', split_axis=0, concat_axis=0, tiled=True)  4.57 us
  transfers between devices with their start and end apart: 25, of which 19 were waited for; matrix products, arithmetic and copies ran while one was open for 6% of the time, Pallas kernels for 7%

profile of v7, /device:TPU:2, one launch (start us, length us, event | category | flops | bytes accessed | tf_op | source)
XLA Modules:
  0.0 167.0 jit_solution(3897345657510167017)
XLA Ops:
  3.2 8.6 %all-to-all-start = ((bf16[16,64,512]{2,1,0:T(8,128)(2,1)}), bf16[16,64,512]{2,1,0:T(8,128)(2,1)S(1)}, u32[]{:S(2)}, u32[]{:S(2)}) async-start(bf16[16,64,512]{2,1,0:T(8,128)(2,1)} %copy.160), calls=%async_computation | async-start | bytes 2097152 | tf_op jit(solution)/shard_map/all_to_all | solution.py:358
  17.5 1.9 %collective-permute-done.1 = s32[2,176]{1,0:T(2,128)S(1)} collective-permute-done((s32[2,176]{1,0:T(2,128)S(1)}, s32[2,176]{1,0:T(2,128)S(1)}, u32[]{:S(2)}, u32[]{:S(2)}) %collective-permute-start.1) | collective-permute-done | bytes 1440 | tf_op jit(solution)/shard_map/ppermute | solution.py:251
  21.2 1.9 %collective-permute-done.2 = s32[4,176]{1,0:T(4,128)S(1)} collective-permute-done((s32[4,176]{1,0:T(4,128)S(1)}, s32[4,176]{1,0:T(4,128)S(1)}, u32[]{:S(2)}, u32[]{:S(2)}) %collective-permute-start.2) | collective-permute-done | bytes 2848 | tf_op jit(solution)/shard_map/ppermute | solution.py:251
  23.2 3.0 %collective-permute-start.3 = (s32[8,176]{1,0:T(8,128)S(1)}, s32[8,176]{1,0:T(8,128)S(1)}, u32[]{:S(2)}, u32[]{:S(2)}) collective-permute-start(s32[8,176]{1,0:T(8,128)S(1)} %pad_add_fusion.2), channel_id=1, source_target_pairs={{0,3},{1,2},{2,1},{3,0},{4,7},{5,6},{6,5},{7,4},{8,11},{9,10},{10,... | collective-permute-start | bytes 16904 | tf_op jit(solution)/shard_map/ppermute | solution.py:251
  33.9 4.6 %all-to-all-done = bf16[16,64,512]{2,1,0:T(8,128)(2,1)S(1)} async-done(((bf16[16,64,512]{2,1,0:T(8,128)(2,1)}), bf16[16,64,512]{2,1,0:T(8,128)(2,1)S(1)}, u32[]{:S(2)}, u32[]{:S(2)}) %all-to-all-start) | async-done | bytes 1048608 | tf_op jit(solution)/shard_map/all_to_all | solution.py:358
  39.8 3.1 %collective-permute-start.7 = (bf16[1,512,256]{2,1,0:T(8,128)(2,1)S(1)}, bf16[1,512,256]{2,1,0:T(8,128)(2,1)S(1)}, u32[]{:S(2)}, u32[]{:S(2)}) collective-permute-start(bf16[1,512,256]{2,1,0:T(8,128)(2,1)S(1)} %get-tuple-element.69.refs_3_), channel_id=1, source_target_pairs={{0,3},{1,2},{2,1},{3,0},{4,7},{5,6},{6,5},{7,4},{8,11},{9,10},{10,... | collective-permute-start | bytes 786440 | tf_op jit(solution)/shard_map/ppermute | solution.py:251
  44.6 1.8 %collective-permute-start.4 = (bf16[1,512,256]{2,1,0:T(8,128)(2,1)S(1)}, bf16[1,512,256]{2,1,0:T(8,128)(2,1)S(1)}, u32[]{:S(2)}, u32[]{:S(2)}) collective-permute-start(bf16[1,512,256]{2,1,0:T(8,128)(2,1)S(1)} %get-tuple-element.72.refs_0_), channel_id=1, source_target_pairs={{0,4},{1,5},{2,6},{3,7},{4,0},{5,1},{6,2},{7,3},{8,12},{9,13},{10,... | collective-permute-start | bytes 786440 | tf_op jit(solution)/shard_map/ppermute | solution.py:251
  46.4 3.2 %collective-permute-done.7.refs_7_ = bf16[1,512,256]{2,1,0:T(8,128)(2,1)S(1)} collective-permute-done((bf16[1,512,256]{2,1,0:T(8,128)(2,1)S(1)}, bf16[1,512,256]{2,1,0:T(8,128)(2,1)S(1)}, u32[]{:S(2)}, u32[]{:S(2)}) %collective-permute-start.7) | collective-permute-done | bytes 262176 | tf_op jit(solution)/shard_map/ppermute | solution.py:251
  49.6 2.2 %collective-permute-done.6.refs_6_ = bf16[1,512,256]{2,1,0:T(8,128)(2,1)S(1)} collective-permute-done((bf16[1,512,256]{2,1,0:T(8,128)(2,1)S(1)}, bf16[1,512,256]{2,1,0:T(8,128)(2,1)S(1)}, u32[]{:S(2)}, u32[]{:S(2)}) %collective-permute-start.6) | collective-permute-done | bytes 262176 | tf_op jit(solution)/shard_map/ppermute | solution.py:251
  58.4 2.4 %shard_map.128 = (bf16[4,512,256]{2,1,0:T(8,128)(2,1)}, bf16[4,512,256]{2,1,0:T(8,128)(2,1)}, bf16[4,512,256]{2,1,0:T(8,128)(2,1)}, bf16[4,512,256]{2,1,0:T(8,128)(2,1)}) custom-call(bf16[2,512,256]{2,1,0:T(8,128)(2,1)} %copy-done.5, bf16[2,512,256]{2,1,0:T(8,128)(2,1)} %copy-done.4, bf16[2,512,256]{2,1,0:T(8,128)(2,1)} %copy-done.3, ...), custom_call_target="tpu_custom_call" | custom-call | bytes 4194304 | tf_op jit(solution)/shard_map/pallas_call | solution.py:331
  60.8 7.4 %collective-permute-done.8.refs_0_ = bf16[2,512,256]{2,1,0:T(8,128)(2,1)S(1)} collective-permute-done((bf16[2,512,256]{2,1,0:T(8,128)(2,1)S(1)}, bf16[2,512,256]{2,1,0:T(8,128)(2,1)S(1)}, u32[]{:S(2)}, u32[]{:S(2)}) %collective-permute-start.8) | collective-permute-done | bytes 524320 | tf_op jit(solution)/shard_map/ppermute | solution.py:251
  70.6 2.4 %shard_map.129 = (bf16[4,512,256]{2,1,0:T(8,128)(2,1)}, bf16[4,512,256]{2,1,0:T(8,128)(2,1)}, bf16[4,512,256]{2,1,0:T(8,128)(2,1)}, bf16[4,512,256]{2,1,0:T(8,128)(2,1)}) custom-call(bf16[2,512,256]{2,1,0:T(8,128)(2,1)} %copy-done.14, bf16[2,512,256]{2,1,0:T(8,128)(2,1)} %copy-done.15, ...), custom_call_target="tpu_custom_call", output_to_operand_aliasing={{0}: (4, {}), {1}: (5, {}), {2}: (6, {}), {3}: (7, {})} | custom-call | bytes 4194304 | tf_op jit(solution)/shard_map/pallas_call | solution.py:331
  73.1 2.8 %collective-permute-start.20 = (bf16[4,512,256]{2,1,0:T(8,128)(2,1)}, bf16[4,512,256]{2,1,0:T(8,128)(2,1)S(1)}, u32[]{:S(2)}, u32[]{:S(2)}) collective-permute-start(bf16[4,512,256]{2,1,0:T(8,128)(2,1)} %get-tuple-element.52), channel_id=1, source_target_pairs={{0,3},{1,2},{2,1},{3,0},{4,7},{5,6},{6,5},{7,4},{8,11},{9,10},{10,... | collective-permute-start | bytes 3145736 | tf_op jit(solution)/shard_map/ppermute | solution.py:251
  76.0 2.1 %collective-permute-start.21 = (bf16[4,512,256]{2,1,0:T(8,128)(2,1)}, bf16[4,512,256]{2,1,0:T(8,128)(2,1)S(1)}, u32[]{:S(2)}, u32[]{:S(2)}) collective-permute-start(bf16[4,512,256]{2,1,0:T(8,128)(2,1)} %get-tuple-element.53), channel_id=1, source_target_pairs={{0,12},{1,13},{2,14},{3,15},{4,8},{5,9},{6,10},{7,11},{8,4},{9,5},... | collective-permute-start | bytes 3145736 | tf_op jit(solution)/shard_map/ppermute | solution.py:251
  81.3 17.3 %collective-permute-done.20 = bf16[4,512,256]{2,1,0:T(8,128)(2,1)S(1)} collective-permute-done((bf16[4,512,256]{2,1,0:T(8,128)(2,1)}, bf16[4,512,256]{2,1,0:T(8,128)(2,1)S(1)}, u32[]{:S(2)}, u32[]{:S(2)}) %collective-permute-start.20) | collective-permute-done | bytes 1048608 | tf_op jit(solution)/shard_map/ppermute | solution.py:251
  98.6 2.2 %collective-permute-start.16 = (bf16[4,512,256]{2,1,0:T(8,128)(2,1)}, bf16[4,512,256]{2,1,0:T(8,128)(2,1)}, u32[]{:S(2)}, u32[]{:S(2)}) collective-permute-start(bf16[4,512,256]{2,1,0:T(8,128)(2,1)} %get-tuple-element.54), channel_id=1, source_target_pairs={{0,3},{1,2},{2,1},{3,0},{4,7},{5,6},{6,5},{7,4},{8,11},{9,10},{10,... | collective-permute-start | bytes 3145736 | tf_op jit(solution)/shard_map/ppermute | solution.py:251
  102.3 1.8 %collective-permute-start.18 = (bf16[4,512,256]{2,1,0:T(8,128)(2,1)}, bf16[4,512,256]{2,1,0:T(8,128)(2,1)}, u32[]{:S(2)}, u32[]{:S(2)}) collective-permute-start(bf16[4,512,256]{2,1,0:T(8,128)(2,1)} %get-tuple-element.55), channel_id=1, source_target_pairs={{0,12},{1,13},{2,14},{3,15},{4,8},{5,9},{6,10},{7,11},{8,4},{9,5},... | collective-permute-start | bytes 3145736 | tf_op jit(solution)/shard_map/ppermute | solution.py:251
  107.4 14.4 %collective-permute-done.22 = bf16[4,512,256]{2,1,0:T(8,128)(2,1)} collective-permute-done((bf16[4,512,256]{2,1,0:T(8,128)(2,1)}, bf16[4,512,256]{2,1,0:T(8,128)(2,1)}, u32[]{:S(2)}, u32[]{:S(2)}) %collective-permute-start.22) | collective-permute-done | bytes 1048608 | tf_op jit(solution)/shard_map/ppermute | solution.py:251
  123.6 2.6 %collective-permute-done.16 = bf16[4,512,256]{2,1,0:T(8,128)(2,1)} collective-permute-done((bf16[4,512,256]{2,1,0:T(8,128)(2,1)}, bf16[4,512,256]{2,1,0:T(8,128)(2,1)}, u32[]{:S(2)}, u32[]{:S(2)}) %collective-permute-start.16) | collective-permute-done | bytes 1048608 | tf_op jit(solution)/shard_map/ppermute | solution.py:251
  126.3 2.1 %collective-permute-start.19 = (bf16[4,512,256]{2,1,0:T(8,128)(2,1)}, bf16[4,512,256]{2,1,0:T(8,128)(2,1)}, u32[]{:S(2)}, u32[]{:S(2)}) collective-permute-start(bf16[4,512,256]{2,1,0:T(8,128)(2,1)} %collective-permute-done.18), channel_id=1, source_target_pairs={{0,4},{1,5},{2,6},{3,7},{4,0},{5,1},{6,2},{7,3},{8,12},{9,13},{10,... | collective-permute-start | bytes 3145736 | tf_op jit(solution)/shard_map/ppermute | solution.py:251
  129.2 9.7 %shard_map.130 = (bf16[4,32,256,256]{3,2,1,0:T(8,128)(2,1)S(1)}, f32[16,256,256]{2,1,0:T(8,128)S(1)}) custom-call(s32[4,192]{1,0:T(4,128)} %fusion.5.idx, f32[128]{0:T(128)} %pad_maximum_fusion.wts, s32[64]{0:T(128)} %and_select_fusion.2.twin, f32[96]{0:T(128)} %add_bitcast_fusion.dsum, f32[1,256]{1,0:T(1,128)} %bitcast.67, f32[256,1]{1,0:T(8,128)} %copy.177.vcol, ...), custom_call_target="tpu_custom_call" | custom-call | flops 2684354560 | bytes 12582912 | tf_op jit(solution)/shard_map/pallas_call | solution.py:138
  138.9 6.7 %collective-permute-done.13 = bf16[4,512,256]{2,1,0:T(8,128)(2,1)S(1)} collective-permute-done((bf16[4,512,256]{2,1,0:T(8,128)(2,1)}, bf16[4,512,256]{2,1,0:T(8,128)(2,1)S(1)}, u32[]{:S(2)}, u32[]{:S(2)}) %collective-permute-start.13) | collective-permute-done | bytes 1048608 | tf_op jit(solution)/shard_map/ppermute | solution.py:251
  145.9 2.0 %collective-permute-done.19 = bf16[4,512,256]{2,1,0:T(8,128)(2,1)} collective-permute-done((bf16[4,512,256]{2,1,0:T(8,128)(2,1)}, bf16[4,512,256]{2,1,0:T(8,128)(2,1)}, u32[]{:S(2)}, u32[]{:S(2)}) %collective-permute-start.19) | collective-permute-done | bytes 1048608 | tf_op jit(solution)/shard_map/ppermute | solution.py:251
  148.0 18.9 %shard_map.131 = (f32[16,256,256]{2,1,0:T(8,128)}, bf16[4,32,256,256]{3,2,1,0:T(8,128)(2,1)S(1)}, f32[16,256,256]{2,1,0:T(8,128)S(1)}) custom-call(s32[4,192]{1,0:T(4,128)S(1)} %copy-done.6, f32[128]{0:T(128)S(1)} %copy-done.10, s32[64]{0:T(128)S(1)} %copy-done.9, f32[96]{0:T(128)S(1)} %copy-done.11, ...), custom_call_target="tpu_custom_call", output_to_operand_aliasing={{1}: (11, {}), {2}: (12, {})} | custom-call | flops 10737418240 | bytes 8388608 | tf_op jit(solution)/shard_map/pallas_call | solution.py:156
  (161 shorter events, 41.0 us)
Async XLA Ops:
  3.2 35.2 %all-to-all-start = ((bf16[16,64,512]{2,1,0:T(8,128)(2,1)}), bf16[16,64,512]{2,1,0:T(8,128)(2,1)S(1)}, u32[]{:S(2)}, u32[]{:S(2)}) async-start(bf16[16,64,512]{2,1,0:T(8,128)(2,1)} %copy.160), calls=%async_computation | async-start | bytes 2097152 | tf_op jit(solution)/shard_map/all_to_all | solution.py:358
  15.8 3.6 %collective-permute-start.1 = (s32[2,176]{1,0:T(2,128)S(1)}, s32[2,176]{1,0:T(2,128)S(1)}, u32[]{:S(2)}, u32[]{:S(2)}) collective-permute-start(s32[2,176]{1,0:T(2,128)S(1)} %pad_add_fusion.4), channel_id=1, source_target_pairs={{0,12},{1,13},{2,14},{3,15},{4,8},{5,9},{6,10},{7,11},{8,4},{9,5},... | collective-permute-start | bytes 4232 | tf_op jit(solution)/shard_map/ppermute | solution.py:251
  19.5 3.6 %collective-permute-start.2 = (s32[4,176]{1,0:T(4,128)S(1)}, s32[4,176]{1,0:T(4,128)S(1)}, u32[]{:S(2)}, u32[]{:S(2)}) collective-permute-start(s32[4,176]{1,0:T(4,128)S(1)} %pad_add_fusion.3), channel_id=1, source_target_pairs={{0,1},{1,0},{2,3},{3,2},{4,5},{5,4},{6,7},{7,6},{8,9},{9,8},{10,11... | collective-permute-start | bytes 8456 | tf_op jit(solution)/shard_map/ppermute | solution.py:251
  23.2 4.9 %collective-permute-start.3 = (s32[8,176]{1,0:T(8,128)S(1)}, s32[8,176]{1,0:T(8,128)S(1)}, u32[]{:S(2)}, u32[]{:S(2)}) collective-permute-start(s32[8,176]{1,0:T(8,128)S(1)} %pad_add_fusion.2), channel_id=1, source_target_pairs={{0,3},{1,2},{2,1},{3,0},{4,7},{5,6},{6,5},{7,4},{8,11},{9,10},{10,... | collective-permute-start | bytes 16904 | tf_op jit(solution)/shard_map/ppermute | solution.py:251
  39.8 9.7 %collective-permute-start.7 = (bf16[1,512,256]{2,1,0:T(8,128)(2,1)S(1)}, bf16[1,512,256]{2,1,0:T(8,128)(2,1)S(1)}, u32[]{:S(2)}, u32[]{:S(2)}) collective-permute-start(bf16[1,512,256]{2,1,0:T(8,128)(2,1)S(1)} %get-tuple-element.69.refs_3_), channel_id=1, source_target_pairs={{0,3},{1,2},{2,1},{3,0},{4,7},{5,6},{6,5},{7,4},{8,11},{9,10},{10,... | collective-permute-start | bytes 786440 | tf_op jit(solution)/shard_map/ppermute | solution.py:251
  42.9 8.8 %collective-permute-start.6 = (bf16[1,512,256]{2,1,0:T(8,128)(2,1)S(1)}, bf16[1,512,256]{2,1,0:T(8,128)(2,1)S(1)}, u32[]{:S(2)}, u32[]{:S(2)}) collective-permute-start(bf16[1,512,256]{2,1,0:T(8,128)(2,1)S(1)} %get-tuple-element.70.refs_2_), channel_id=1, source_target_pairs={{0,12},{1,13},{2,14},{3,15},{4,8},{5,9},{6,10},{7,11},{8,4},{9,5},... | collective-permute-start | bytes 786440 | tf_op jit(solution)/shard_map/ppermute | solution.py:251
  44.4 9.0 %collective-permute-start.5 = (bf16[1,512,256]{2,1,0:T(8,128)(2,1)S(1)}, bf16[1,512,256]{2,1,0:T(8,128)(2,1)S(1)}, u32[]{:S(2)}, u32[]{:S(2)}) collective-permute-start(bf16[1,512,256]{2,1,0:T(8,128)(2,1)S(1)} %get-tuple-element.71.refs_1_), channel_id=1, source_target_pairs={{0,1},{1,0},{2,3},{3,2},{4,5},{5,4},{6,7},{7,6},{8,9},{9,8},{10,11... | collective-permute-start | bytes 786440 | tf_op jit(solution)/shard_map/ppermute | solution.py:251
  44.6 9.1 %collective-permute-start.4 = (bf16[1,512,256]{2,1,0:T(8,128)(2,1)S(1)}, bf16[1,512,256]{2,1,0:T(8,128)(2,1)S(1)}, u32[]{:S(2)}, u32[]{:S(2)}) collective-permute-start(bf16[1,512,256]{2,1,0:T(8,128)(2,1)S(1)} %get-tuple-element.72.refs_0_), channel_id=1, source_target_pairs={{0,4},{1,5},{2,6},{3,7},{4,0},{5,1},{6,2},{7,3},{8,12},{9,13},{10,... | collective-permute-start | bytes 786440 | tf_op jit(solution)/shard_map/ppermute | solution.py:251
  54.1 14.0 %collective-permute-start.8 = (bf16[2,512,256]{2,1,0:T(8,128)(2,1)S(1)}, bf16[2,512,256]{2,1,0:T(8,128)(2,1)S(1)}, u32[]{:S(2)}, u32[]{:S(2)}) collective-permute-start(bf16[2,512,256]{2,1,0:T(8,128)(2,1)S(1)} %get-tuple-element.44.refs_0_), channel_id=1, source_target_pairs={{0,12},{1,13},{2,14},{3,15},{4,8},{5,9},{6,10},{7,11},{8,4},{9,5},... | collective-permute-start | bytes 1572872 | tf_op jit(solution)/shard_map/ppermute | solution.py:251
  54.8 14.9 %collective-permute-start.9 = (bf16[2,512,256]{2,1,0:T(8,128)(2,1)S(1)}, bf16[2,512,256]{2,1,0:T(8,128)(2,1)S(1)}, u32[]{:S(2)}, u32[]{:S(2)}) collective-permute-start(bf16[2,512,256]{2,1,0:T(8,128)(2,1)S(1)} %get-tuple-element.45.refs_1_), channel_id=1, source_target_pairs={{0,3},{1,2},{2,1},{3,0},{4,7},{5,6},{6,5},{7,4},{8,11},{9,10},{10,... | collective-permute-start | bytes 1572872 | tf_op jit(solution)/shard_map/ppermute | solution.py:251
  55.8 13.9 %collective-permute-start.10 = (bf16[2,512,256]{2,1,0:T(8,128)(2,1)S(1)}, bf16[2,512,256]{2,1,0:T(8,128)(2,1)S(1)}, u32[]{:S(2)}, u32[]{:S(2)}) collective-permute-start(bf16[2,512,256]{2,1,0:T(8,128)(2,1)S(1)} %get-tuple-element.46.refs_2_), channel_id=1, source_target_pairs={{0,4},{1,5},{2,6},{3,7},{4,0},{5,1},{6,2},{7,3},{8,12},{9,13},{10,... | collective-permute-start | bytes 1572872 | tf_op jit(solution)/shard_map/ppermute | solution.py:251
  57.5 13.1 %collective-permute-start.11 = (bf16[2,512,256]{2,1,0:T(8,128)(2,1)S(1)}, bf16[2,512,256]{2,1,0:T(8,128)(2,1)}, u32[]{:S(2)}, u32[]{:S(2)}) collective-permute-start(bf16[2,512,256]{2,1,0:T(8,128)(2,1)S(1)} %get-tuple-element.47.refs_3_), channel_id=1, source_target_pairs={{0,1},{1,0},{2,3},{3,2},{4,5},{5,4},{6,7},{7,6},{8,9},{9,8},{10,11... | collective-permute-start | bytes 1572872 | tf_op jit(solution)/shard_map/ppermute | solution.py:251
  73.1 25.5 %collective-permute-start.20 = (bf16[4,512,256]{2,1,0:T(8,128)(2,1)}, bf16[4,512,256]{2,1,0:T(8,128)(2,1)S(1)}, u32[]{:S(2)}, u32[]{:S(2)}) collective-permute-start(bf16[4,512,256]{2,1,0:T(8,128)(2,1)} %get-tuple-element.52), channel_id=1, source_target_pairs={{0,3},{1,2},{2,1},{3,0},{4,7},{5,6},{6,5},{7,4},{8,11},{9,10},{10,... | collective-permute-start | bytes 3145736 | tf_op jit(solution)/shard_map/ppermute | solution.py:251
  75.9 26.4 %collective-permute-start.12 = (bf16[4,512,256]{2,1,0:T(8,128)(2,1)}, bf16[4,512,256]{2,1,0:T(8,128)(2,1)}, u32[]{:S(2)}, u32[]{:S(2)}) collective-permute-start(bf16[4,512,256]{2,1,0:T(8,128)(2,1)} %get-tuple-element.52), channel_id=1, source_target_pairs={{0,1},{1,0},{2,3},{3,2},{4,5},{5,4},{6,7},{7,6},{8,9},{9,8},{10,11... | collective-permute-start | bytes 3145736 | tf_op jit(solution)/shard_map/ppermute | solution.py:251
  76.0 28.1 %collective-permute-start.21 = (bf16[4,512,256]{2,1,0:T(8,128)(2,1)}, bf16[4,512,256]{2,1,0:T(8,128)(2,1)S(1)}, u32[]{:S(2)}, u32[]{:S(2)}) collective-permute-start(bf16[4,512,256]{2,1,0:T(8,128)(2,1)} %get-tuple-element.53), channel_id=1, source_target_pairs={{0,12},{1,13},{2,14},{3,15},{4,8},{5,9},{6,10},{7,11},{8,4},{9,5},... | collective-permute-start | bytes 3145736 | tf_op jit(solution)/shard_map/ppermute | solution.py:251
  78.2 27.5 %collective-permute-start.14 = (bf16[4,512,256]{2,1,0:T(8,128)(2,1)}, bf16[4,512,256]{2,1,0:T(8,128)(2,1)}, u32[]{:S(2)}, u32[]{:S(2)}) collective-permute-start(bf16[4,512,256]{2,1,0:T(8,128)(2,1)} %get-tuple-element.53), channel_id=1, source_target_pairs={{0,4},{1,5},{2,6},{3,7},{4,0},{5,1},{6,2},{7,3},{8,12},{9,13},{10,... | collective-permute-start | bytes 3145736 | tf_op jit(solution)/shard_map/ppermute | solution.py:251
  79.7 42.1 %collective-permute-start.22 = (bf16[4,512,256]{2,1,0:T(8,128)(2,1)}, bf16[4,512,256]{2,1,0:T(8,128)(2,1)}, u32[]{:S(2)}, u32[]{:S(2)}) collective-permute-start(bf16[4,512,256]{2,1,0:T(8,128)(2,1)} %get-tuple-element.54), channel_id=1, source_target_pairs={{0,1},{1,0},{2,3},{3,2},{4,5},{5,4},{6,7},{7,6},{8,9},{9,8},{10,11... | collective-permute-start | bytes 3145736 | tf_op jit(solution)/shard_map/ppermute | solution.py:251
  98.6 27.6 %collective-permute-start.16 = (bf16[4,512,256]{2,1,0:T(8,128)(2,1)}, bf16[4,512,256]{2,1,0:T(8,128)(2,1)}, u32[]{:S(2)}, u32[]{:S(2)}) collective-permute-start(bf16[4,512,256]{2,1,0:T(8,128)(2,1)} %get-tuple-element.54), channel_id=1, source_target_pairs={{0,3},{1,2},{2,1},{3,0},{4,7},{5,6},{6,5},{7,4},{8,11},{9,10},{10,... | collective-permute-start | bytes 3145736 | tf_op jit(solution)/shard_map/ppermute | solution.py:251
  102.3 23.9 %collective-permute-start.18 = (bf16[4,512,256]{2,1,0:T(8,128)(2,1)}, bf16[4,512,256]{2,1,0:T(8,128)(2,1)}, u32[]{:S(2)}, u32[]{:S(2)}) collective-permute-start(bf16[4,512,256]{2,1,0:T(8,128)(2,1)} %get-tuple-element.55), channel_id=1, source_target_pairs={{0,12},{1,13},{2,14},{3,15},{4,8},{5,9},{6,10},{7,11},{8,4},{9,5},... | collective-permute-start | bytes 3145736 | tf_op jit(solution)/shard_map/ppermute | solution.py:251
  104.1 25.0 %collective-permute-start.23 = (bf16[4,512,256]{2,1,0:T(8,128)(2,1)}, bf16[4,512,256]{2,1,0:T(8,128)(2,1)}, u32[]{:S(2)}, u32[]{:S(2)}) collective-permute-start(bf16[4,512,256]{2,1,0:T(8,128)(2,1)} %get-tuple-element.55), channel_id=1, source_target_pairs={{0,4},{1,5},{2,6},{3,7},{4,0},{5,1},{6,2},{7,3},{8,12},{9,13},{10,... | collective-permute-start | bytes 3145736 | tf_op jit(solution)/shard_map/ppermute | solution.py:251
  105.7 39.9 %collective-permute-start.13 = (bf16[4,512,256]{2,1,0:T(8,128)(2,1)}, bf16[4,512,256]{2,1,0:T(8,128)(2,1)S(1)}, u32[]{:S(2)}, u32[]{:S(2)}) collective-permute-start(bf16[4,512,256]{2,1,0:T(8,128)(2,1)} %collective-permute-done.12), channel_id=1, source_target_pairs={{0,3},{1,2},{2,1},{3,0},{4,7},{5,6},{6,5},{7,4},{8,11},{9,10},{10,... | collective-permute-start | bytes 3145736 | tf_op jit(solution)/shard_map/ppermute | solution.py:251
  121.9 24.0 %collective-permute-start.15 = (bf16[4,512,256]{2,1,0:T(8,128)(2,1)}, bf16[4,512,256]{2,1,0:T(8,128)(2,1)}, u32[]{:S(2)}, u32[]{:S(2)}) collective-permute-start(bf16[4,512,256]{2,1,0:T(8,128)(2,1)} %collective-permute-done.14), channel_id=1, source_target_pairs={{0,12},{1,13},{2,14},{3,15},{4,8},{5,9},{6,10},{7,11},{8,4},{9,5},... | collective-permute-start | bytes 3145736 | tf_op jit(solution)/shard_map/ppermute | solution.py:251
  126.2 19.7 %collective-permute-start.17 = (bf16[4,512,256]{2,1,0:T(8,128)(2,1)}, bf16[4,512,256]{2,1,0:T(8,128)(2,1)}, u32[]{:S(2)}, u32[]{:S(2)}) collective-permute-start(bf16[4,512,256]{2,1,0:T(8,128)(2,1)} %collective-permute-done.16), channel_id=1, source_target_pairs={{0,1},{1,0},{2,3},{3,2},{4,5},{5,4},{6,7},{7,6},{8,9},{9,8},{10,11... | collective-permute-start | bytes 3145736 | tf_op jit(solution)/shard_map/ppermute | solution.py:251
  126.3 21.7 %collective-permute-start.19 = (bf16[4,512,256]{2,1,0:T(8,128)(2,1)}, bf16[4,512,256]{2,1,0:T(8,128)(2,1)}, u32[]{:S(2)}, u32[]{:S(2)}) collective-permute-start(bf16[4,512,256]{2,1,0:T(8,128)(2,1)} %collective-permute-done.18), channel_id=1, source_target_pairs={{0,4},{1,5},{2,6},{3,7},{4,0},{5,1},{6,2},{7,3},{8,12},{9,13},{10,... | collective-permute-start | bytes 3145736 | tf_op jit(solution)/shard_map/ppermute | solution.py:251
  (26 other events, 425.0 us)

commit v8 on v7

--- a/solution.py
+++ b/solution.py
@@ -16,12 +16,9 @@
     return r * (2.0 - x * r)
 
 
-def listed(idx, twin, order, soon):
+def listed(when, kernel, order):
     def entry(n, count):
-        last = idx[0, 32 + n]
-        for q in range(4):
-            last = jnp.maximum(last, jnp.maximum(idx[q, 32 + n], idx[q, 128 + n]))
-        hit = (twin[n] >= -1) & ((last < 24) == soon)
+        hit = when[n] == kernel
 
         @pl.when(hit)
         def _():
@@ -41,7 +38,7 @@
     return lax.dot_general(left, right, NT, preferred_element_type=jnp.float32)
 
 
-def add_coupled(idx, wts, twin, dsum, pool, mixed, vsum, order, trips):
+def add_coupled(idx, wts, dsum, pool, mixed, vsum, order, trips):
     def coupled(g, carry):
         for u in range(UNROLL):
             entry = order[UNROLL * g + u]
@@ -51,15 +48,12 @@
             start = -(product(idx, pool, 32 + at) * recip(vsum[...] - dsum[32 + at]))
             rounded = start.astype(jnp.bfloat16).astype(jnp.float32)
             mixed[n // 4] += weight * rounded
-            other = jnp.where(entry >= 0, twin[n], -1)
-            m = jnp.maximum(other, 0)
-            mixed[m // 4] += jnp.where(other >= 0, wts[64 + m], 0.0) * rounded
         return carry
 
     lax.fori_loop(0, trips, coupled, 0)
 
 
-def early_kernel(idx, wts, twin, dsum, vrow, vcol, *refs):
+def early_kernel(idx, wts, when, dsum, vrow, vcol, *refs):
     pieces, pool, mixed, vsum, order, sems = refs[:12], *refs[12:]
     copies = [
         pltpu.make_async_copy(
@@ -70,7 +64,7 @@
     ]
     for copy in copies:
         copy.start()
-    trips = listed(idx, twin, order, True)
+    trips = listed(when, 1, order)
     vsum[...] = vrow[...] + vcol[...]
 
     def clear(s, carry):
@@ -80,21 +74,21 @@
     lax.fori_loop(0, 16, clear, 0)
     for copy in copies:
         copy.wait()
-    add_coupled(idx, wts, twin, dsum, pool, mixed, vsum, order, trips)
-
-
-def last_kernel(idx, wts, twin, dsum, vrow, vcol, slot, *refs):
+    add_coupled(idx, wts, dsum, pool, mixed, vsum, order, trips)
+
+
+def last_kernel(idx, wts, when, dsum, vrow, vcol, slot, *refs):
     pieces, _, _, out, pool, mixed, amp, vsum, order, sems, out_sems = refs[:4], *refs[4:]
     copies = [
         pltpu.make_async_copy(pieces[q], pool.at[q, pl.ds(24, 8)], sems.at[q]) for q in range(4)
     ]
     for copy in copies:
         copy.start()
-    trips = listed(idx, twin, order, False)
+    trips = listed(when, 2, order)
     vsum[...] = vrow[...] + vcol[...]
     for copy in copies:
         copy.wait()
-    add_coupled(idx, wts, twin, dsum, pool, mixed, vsum, order, trips)
+    add_coupled(idx, wts, dsum, pool, mixed, vsum, order, trips)
 
     def received(g, carry):
         for u in range(UNROLL):
@@ -103,8 +97,9 @@
             amp[s] = value.astype(jnp.bfloat16)
         return carry
 
-    def out_copy(p):
-        return pltpu.make_async_copy(mixed.at[p], out.at[p], out_sems.at[p])
+    def out_copy(g):
+        rows = pl.ds(UNROLL * g, UNROLL)
+        return pltpu.make_async_copy(mixed.at[rows], out.at[rows], out_sems.at[g])
 
     def own(g, carry):
         for u in range(UNROLL):
@@ -113,16 +108,16 @@
             for e in range(4):
                 total += wts[4 * p + e] * amp[slot[4 * p + e]].astype(jnp.float32)
             mixed[p] = total * recip(vsum[...] - dsum[p])
-            out_copy(p).start()
-        return carry
-
-    def finish(p, carry):
-        out_copy(p).wait()
+        out_copy(g).start()
+        return carry
+
+    def finish(g, carry):
+        out_copy(g).wait()
         return carry
 
     lax.fori_loop(0, 16 // UNROLL, received, 0)
     lax.fori_loop(0, 16 // UNROLL, own, 0)
-    lax.fori_loop(0, 16, finish, 0)
+    lax.fori_loop(0, 16 // UNROLL, finish, 0)
 
 
 SMEM = pl.BlockSpec(memory_space=pltpu.SMEM)
@@ -134,7 +129,7 @@
 SUMS = pltpu.VMEM((16, 256, 256), jnp.float32)
 
 
-def early_sums(idx, wts, twin, dsum, vrow, vcol, pieces):
+def early_sums(idx, wts, when, dsum, vrow, vcol, pieces):
     return pl.pallas_call(
         early_kernel,
         in_specs=[SMEM] * 4 + [VMEM] * 2 + [HBM] * 12,
@@ -149,10 +144,10 @@
         cost_estimate=pl.CostEstimate(
             flops=20 * 2 * 256 * 256 * 1024, bytes_accessed=12 * MIB, transcendentals=0
         ),
-    )(idx, wts, twin, dsum, vrow, vcol, *pieces)
-
-
-def amplitudes(idx, wts, twin, dsum, vrow, vcol, slot, pieces, pool, sums):
+    )(idx, wts, when, dsum, vrow, vcol, *pieces)
+
+
+def amplitudes(idx, wts, when, dsum, vrow, vcol, slot, pieces, pool, sums):
     return pl.pallas_call(
         last_kernel,
         in_specs=[SMEM] * 4 + [VMEM] * 2 + [SMEM] + [HBM] * 4 + [VMEM] * 2,
@@ -164,13 +159,13 @@
             pltpu.VMEM((256, 256), jnp.float32),
             pltpu.SMEM((72,), jnp.int32),
             pltpu.SemaphoreType.DMA((4,)),
-            pltpu.SemaphoreType.DMA((16,)),
+            pltpu.SemaphoreType.DMA((4,)),
         ],
         compiler_params=pltpu.CompilerParams(vmem_limit_bytes=8 * MIB),
         cost_estimate=pl.CostEstimate(
             flops=80 * 2 * 256 * 256 * 1024, bytes_accessed=8 * MIB, transcendentals=0
         ),
-    )(idx, wts, twin, dsum, vrow, vcol, slot, *pieces, pool, sums)[0]
+    )(idx, wts, when, dsum, vrow, vcol, slot, *pieces, pool, sums)[0]
 
 
 def lookup(table, rows, cols):
@@ -205,16 +200,6 @@
     return jnp.sum(jnp.where(hit, ids, 0), axis=-1)
 
 
-def twins(pairs, wts):
-    n = jnp.arange(64, dtype=jnp.int32)
-    code = jnp.where(wts != 0.0, pairs[:, 0] * 32 + pairs[:, 1], -1 - n)
-    same = code[:, None] == code[None, :]
-    rank = jnp.sum((same & (n[None, :] < n[:, None])).astype(jnp.int32), axis=1)
-    after = same & (rank[None, :] == rank[:, None] + 1)
-    second = jnp.max(jnp.where(after, n[None, :], -1), axis=1)
-    return jnp.where((wts != 0.0) & (rank % 2 == 0), second, -2)
-
-
 def tables(metas, fock, orb, cpl, cpl_slot):
     col = lax.axis_index("aux")
     grp = lax.axis_index("grp")
@@ -244,7 +229,10 @@
     offset = (flat // 2) ^ grp
     spot = jnp.stack([found_in(offset, arrival(masks)) for masks in MASKS])
     slot = found_in(cpl_slot.reshape(64) ^ grp, arrival(MASKS[0]))
-    return spot * 2 + flat % 2, wts, twins(cpl_q.reshape(64, 2), wts[64:]), slot, dsum
+    last = jnp.max(spot, axis=0)
+    ready = jnp.maximum(last[32:96], last[128:192]) < 12
+    when = jnp.where(wts[64:] != 0.0, jnp.where(ready, 1, 2), 0).astype(jnp.int32)
+    return spot * 2 + flat % 2, wts, when, slot, dsum
 
 
 def swap(block, mask):
@@ -357,7 +345,7 @@
 
     block = lax.all_to_all(rows, "aux", split_axis=0, concat_axis=0, tiled=True)
     given = (*tables(metas, fock, orb, cpl, cpl_slot), virt_energy[None, :], virt_energy[:, None])
-    block, (idx, wts, twin, slot, dsum, vrow, vcol) = lax.optimization_barrier((block, given))
+    block, (idx, wts, when, slot, dsum, vrow, vcol) = lax.optimization_barrier((block, given))
     fitted = lax.dot_general(
         block.reshape(1024, 512),
         metric,
@@ -373,9 +361,9 @@
     early = [swap(held[q], MASKS[q][3]) for q in range(4)]
     late = [swap(third[q], MASKS[q][3]) for q in range(4)]
     soon = [x.reshape(8, 256, 256) for three in zip(held, third, early) for x in three]
-    pool, sums = early_sums(idx, wts, twin, dsum, vrow, vcol, soon)
+    pool, sums = early_sums(idx, wts, when, dsum, vrow, vcol, soon)
     late = [x.reshape(8, 256, 256) for x in late]
-    return amplitudes(idx, wts, twin, dsum, vrow, vcol, slot, late, pool, sums)
+    return amplitudes(idx, wts, when, dsum, vrow, vcol, slot, late, pool, sums)
 
 
 def solution(mesh):

time: 169 us -> 166 us (0.982); the launches traced: 167 us -> 166 us
  Pallas kernels: 33.9 us -> 30.3 us
  waiting for transfers between devices: 72.9 us -> 76.4 us
    pallas_call x1, Pallas kernels: 9.71 us -> 7.13 us  [early_sums(): pl.pallas_call(early_kernel, in_specs=[SMEM] * 4 + [VMEM] * 2 + [HBM] * 1...]
    ppermute x24, waiting for transfers between devices: 68.4 us -> 70.9 us  [swap(): return lax.ppermute(block, 'grp', [(g, g ^ mask) for g in range(16)])]
  transfers between devices with their start and end apart: 25 -> 25, of which waited for: 19 -> 19; matrix products, arithmetic and copies ran while one was open for 6% -> 5% of each run, Pallas kernels for 7% -> 6%
where the time goes in v8:
time: 166 us
  waiting for transfers between devices  76.4 us (46%)
  starting transfers between devices  45.4 us (27%)
  Pallas kernels  30.3 us (18%)
  local copies, waits for them, and re-layouts  6.73 us (4%)
  other arithmetic  3.8 us (2%)
  matrix products  2.73 us (2%)
    ppermute x24, waiting for transfers between devices, swap(): return lax.ppermute(block, 'grp', [(g, g ^ mask) for g in range(16)])  70.9 us
    ppermute x24, starting transfers between devices, swap(): return lax.ppermute(block, 'grp', [(g, g ^ mask) for g in range(16)])  36.8 us
    pallas_call x1, Pallas kernels, amplitudes(): pl.pallas_call(last_kernel, in_specs=[SMEM] * 4 + [VMEM] * 2 + [SMEM] + [...  17.9 us
    all_to_all x1, starting transfers between devices, on_device(): block = lax.all_to_all(rows, 'aux', split_axis=0, concat_axis=0, tiled=True)  8.57 us
    pallas_call x1, Pallas kernels, early_sums(): pl.pallas_call(early_kernel, in_specs=[SMEM] * 4 + [VMEM] * 2 + [HBM] * 1...  7.13 us
    all_to_all x1, waiting for transfers between devices, on_device(): block = lax.all_to_all(rows, 'aux', split_axis=0, concat_axis=0, tiled=True)  5.51 us
    pallas_call x2, Pallas kernels, half_call(): pl.pallas_call(kernel, in_specs=[HBM] * (4 + len(staged)), out_specs=[HBM...  4.87 us
  transfers between devices with their start and end apart: 25, of which 19 were waited for; matrix products, arithmetic and copies ran while one was open for 5% of the time, Pallas kernels for 6%

profile of v8, /device:TPU:2, one launch (start us, length us, event | category | flops | bytes accessed | tf_op | source)
XLA Modules:
  0.0 166.0 jit_solution(9024371576339055941)
XLA Ops:
  3.2 8.6 %all-to-all-start = ((bf16[16,64,512]{2,1,0:T(8,128)(2,1)}), bf16[16,64,512]{2,1,0:T(8,128)(2,1)S(1)}, u32[]{:S(2)}, u32[]{:S(2)}) async-start(bf16[16,64,512]{2,1,0:T(8,128)(2,1)} %copy.80), calls=%async_computation | async-start | bytes 2097152 | tf_op jit(solution)/shard_map/all_to_all | solution.py:346
  17.5 1.9 %collective-permute-done.1 = s32[2,176]{1,0:T(2,128)S(1)} collective-permute-done((s32[2,176]{1,0:T(2,128)S(1)}, s32[2,176]{1,0:T(2,128)S(1)}, u32[]{:S(2)}, u32[]{:S(2)}) %collective-permute-start.1) | collective-permute-done | bytes 1440 | tf_op jit(solution)/shard_map/ppermute | solution.py:239
  21.2 1.9 %collective-permute-done.2 = s32[4,176]{1,0:T(4,128)S(1)} collective-permute-done((s32[4,176]{1,0:T(4,128)S(1)}, s32[4,176]{1,0:T(4,128)S(1)}, u32[]{:S(2)}, u32[]{:S(2)}) %collective-permute-start.2) | collective-permute-done | bytes 2848 | tf_op jit(solution)/shard_map/ppermute | solution.py:239
  23.2 3.0 %collective-permute-start.3 = (s32[8,176]{1,0:T(8,128)S(1)}, s32[8,176]{1,0:T(8,128)S(1)}, u32[]{:S(2)}, u32[]{:S(2)}) collective-permute-start(s32[8,176]{1,0:T(8,128)S(1)} %pad_add_fusion.2), channel_id=1, source_target_pairs={{0,3},{1,2},{2,1},{3,0},{4,7},{5,6},{6,5},{7,4},{8,11},{9,10},{10,... | collective-permute-start | bytes 16904 | tf_op jit(solution)/shard_map/ppermute | solution.py:239
  32.9 5.5 %all-to-all-done = bf16[16,64,512]{2,1,0:T(8,128)(2,1)S(1)} async-done(((bf16[16,64,512]{2,1,0:T(8,128)(2,1)}), bf16[16,64,512]{2,1,0:T(8,128)(2,1)S(1)}, u32[]{:S(2)}, u32[]{:S(2)}) %all-to-all-start) | async-done | bytes 1048608 | tf_op jit(solution)/shard_map/all_to_all | solution.py:346
  39.8 3.1 %collective-permute-start.7 = (bf16[1,512,256]{2,1,0:T(8,128)(2,1)S(1)}, bf16[1,512,256]{2,1,0:T(8,128)(2,1)S(1)}, u32[]{:S(2)}, u32[]{:S(2)}) collective-permute-start(bf16[1,512,256]{2,1,0:T(8,128)(2,1)S(1)} %get-tuple-element.69.refs_3_), channel_id=1, source_target_pairs={{0,3},{1,2},{2,1},{3,0},{4,7},{5,6},{6,5},{7,4},{8,11},{9,10},{10,... | collective-permute-start | bytes 786440 | tf_op jit(solution)/shard_map/ppermute | solution.py:239
  44.6 1.8 %collective-permute-start.4 = (bf16[1,512,256]{2,1,0:T(8,128)(2,1)S(1)}, bf16[1,512,256]{2,1,0:T(8,128)(2,1)S(1)}, u32[]{:S(2)}, u32[]{:S(2)}) collective-permute-start(bf16[1,512,256]{2,1,0:T(8,128)(2,1)S(1)} %get-tuple-element.72.refs_0_), channel_id=1, source_target_pairs={{0,4},{1,5},{2,6},{3,7},{4,0},{5,1},{6,2},{7,3},{8,12},{9,13},{10,... | collective-permute-start | bytes 786440 | tf_op jit(solution)/shard_map/ppermute | solution.py:239
  46.4 3.2 %collective-permute-done.7.refs_7_ = bf16[1,512,256]{2,1,0:T(8,128)(2,1)S(1)} collective-permute-done((bf16[1,512,256]{2,1,0:T(8,128)(2,1)S(1)}, bf16[1,512,256]{2,1,0:T(8,128)(2,1)S(1)}, u32[]{:S(2)}, u32[]{:S(2)}) %collective-permute-start.7) | collective-permute-done | bytes 262176 | tf_op jit(solution)/shard_map/ppermute | solution.py:239
  49.6 2.2 %collective-permute-done.6.refs_6_ = bf16[1,512,256]{2,1,0:T(8,128)(2,1)S(1)} collective-permute-done((bf16[1,512,256]{2,1,0:T(8,128)(2,1)S(1)}, bf16[1,512,256]{2,1,0:T(8,128)(2,1)S(1)}, u32[]{:S(2)}, u32[]{:S(2)}) %collective-permute-start.6) | collective-permute-done | bytes 262176 | tf_op jit(solution)/shard_map/ppermute | solution.py:239
  58.4 2.4 %shard_map.128 = (bf16[4,512,256]{2,1,0:T(8,128)(2,1)}, bf16[4,512,256]{2,1,0:T(8,128)(2,1)}, bf16[4,512,256]{2,1,0:T(8,128)(2,1)}, bf16[4,512,256]{2,1,0:T(8,128)(2,1)}) custom-call(bf16[2,512,256]{2,1,0:T(8,128)(2,1)} %copy-done.5, bf16[2,512,256]{2,1,0:T(8,128)(2,1)} %copy-done.4, bf16[2,512,256]{2,1,0:T(8,128)(2,1)} %copy-done.3, ...), custom_call_target="tpu_custom_call" | custom-call | bytes 4194304 | tf_op jit(solution)/shard_map/pallas_call | solution.py:319
  60.8 7.4 %collective-permute-done.8.refs_0_ = bf16[2,512,256]{2,1,0:T(8,128)(2,1)S(1)} collective-permute-done((bf16[2,512,256]{2,1,0:T(8,128)(2,1)S(1)}, bf16[2,512,256]{2,1,0:T(8,128)(2,1)S(1)}, u32[]{:S(2)}, u32[]{:S(2)}) %collective-permute-start.8) | collective-permute-done | bytes 524320 | tf_op jit(solution)/shard_map/ppermute | solution.py:239
  70.7 2.5 %shard_map.129 = (bf16[4,512,256]{2,1,0:T(8,128)(2,1)}, bf16[4,512,256]{2,1,0:T(8,128)(2,1)}, bf16[4,512,256]{2,1,0:T(8,128)(2,1)}, bf16[4,512,256]{2,1,0:T(8,128)(2,1)}) custom-call(bf16[2,512,256]{2,1,0:T(8,128)(2,1)} %copy-done.14, bf16[2,512,256]{2,1,0:T(8,128)(2,1)} %copy-done.15, ...), custom_call_target="tpu_custom_call", output_to_operand_aliasing={{0}: (4, {}), {1}: (5, {}), {2}: (6, {}), {3}: (7, {})} | custom-call | bytes 4194304 | tf_op jit(solution)/shard_map/pallas_call | solution.py:319
  73.1 2.8 %collective-permute-start.20 = (bf16[4,512,256]{2,1,0:T(8,128)(2,1)}, bf16[4,512,256]{2,1,0:T(8,128)(2,1)S(1)}, u32[]{:S(2)}, u32[]{:S(2)}) collective-permute-start(bf16[4,512,256]{2,1,0:T(8,128)(2,1)} %get-tuple-element.52), channel_id=1, source_target_pairs={{0,3},{1,2},{2,1},{3,0},{4,7},{5,6},{6,5},{7,4},{8,11},{9,10},{10,... | collective-permute-start | bytes 3145736 | tf_op jit(solution)/shard_map/ppermute | solution.py:239
  76.0 2.1 %collective-permute-start.21 = (bf16[4,512,256]{2,1,0:T(8,128)(2,1)}, bf16[4,512,256]{2,1,0:T(8,128)(2,1)S(1)}, u32[]{:S(2)}, u32[]{:S(2)}) collective-permute-start(bf16[4,512,256]{2,1,0:T(8,128)(2,1)} %get-tuple-element.53), channel_id=1, source_target_pairs={{0,12},{1,13},{2,14},{3,15},{4,8},{5,9},{6,10},{7,11},{8,4},{9,5},... | collective-permute-start | bytes 3145736 | tf_op jit(solution)/shard_map/ppermute | solution.py:239
  81.3 17.3 %collective-permute-done.20 = bf16[4,512,256]{2,1,0:T(8,128)(2,1)S(1)} collective-permute-done((bf16[4,512,256]{2,1,0:T(8,128)(2,1)}, bf16[4,512,256]{2,1,0:T(8,128)(2,1)S(1)}, u32[]{:S(2)}, u32[]{:S(2)}) %collective-permute-start.20) | collective-permute-done | bytes 1048608 | tf_op jit(solution)/shard_map/ppermute | solution.py:239
  98.7 2.1 %collective-permute-start.16 = (bf16[4,512,256]{2,1,0:T(8,128)(2,1)}, bf16[4,512,256]{2,1,0:T(8,128)(2,1)}, u32[]{:S(2)}, u32[]{:S(2)}) collective-permute-start(bf16[4,512,256]{2,1,0:T(8,128)(2,1)} %get-tuple-element.54), channel_id=1, source_target_pairs={{0,3},{1,2},{2,1},{3,0},{4,7},{5,6},{6,5},{7,4},{8,11},{9,10},{10,... | collective-permute-start | bytes 3145736 | tf_op jit(solution)/shard_map/ppermute | solution.py:239
  102.3 1.8 %collective-permute-start.18 = (bf16[4,512,256]{2,1,0:T(8,128)(2,1)}, bf16[4,512,256]{2,1,0:T(8,128)(2,1)}, u32[]{:S(2)}, u32[]{:S(2)}) collective-permute-start(bf16[4,512,256]{2,1,0:T(8,128)(2,1)} %get-tuple-element.55), channel_id=1, source_target_pairs={{0,12},{1,13},{2,14},{3,15},{4,8},{5,9},{6,10},{7,11},{8,4},{9,5},... | collective-permute-start | bytes 3145736 | tf_op jit(solution)/shard_map/ppermute | solution.py:239
  107.5 14.4 %collective-permute-done.22 = bf16[4,512,256]{2,1,0:T(8,128)(2,1)} collective-permute-done((bf16[4,512,256]{2,1,0:T(8,128)(2,1)}, bf16[4,512,256]{2,1,0:T(8,128)(2,1)}, u32[]{:S(2)}, u32[]{:S(2)}) %collective-permute-start.22) | collective-permute-done | bytes 1048608 | tf_op jit(solution)/shard_map/ppermute | solution.py:239
  123.7 2.6 %collective-permute-done.16 = bf16[4,512,256]{2,1,0:T(8,128)(2,1)} collective-permute-done((bf16[4,512,256]{2,1,0:T(8,128)(2,1)}, bf16[4,512,256]{2,1,0:T(8,128)(2,1)}, u32[]{:S(2)}, u32[]{:S(2)}) %collective-permute-start.16) | collective-permute-done | bytes 1048608 | tf_op jit(solution)/shard_map/ppermute | solution.py:239
  126.3 2.1 %collective-permute-start.19 = (bf16[4,512,256]{2,1,0:T(8,128)(2,1)}, bf16[4,512,256]{2,1,0:T(8,128)(2,1)}, u32[]{:S(2)}, u32[]{:S(2)}) collective-permute-start(bf16[4,512,256]{2,1,0:T(8,128)(2,1)} %collective-permute-done.18), channel_id=1, source_target_pairs={{0,4},{1,5},{2,6},{3,7},{4,0},{5,1},{6,2},{7,3},{8,12},{9,13},{10,... | collective-permute-start | bytes 3145736 | tf_op jit(solution)/shard_map/ppermute | solution.py:239
  129.3 7.1 %shard_map.130 = (bf16[4,32,256,256]{3,2,1,0:T(8,128)(2,1)S(1)}, f32[16,256,256]{2,1,0:T(8,128)S(1)}) custom-call(s32[4,192]{1,0:T(4,128)} %fusion.5.idx, f32[128]{0:T(128)} %pad_maximum_fusion.wts, s32[64]{0:T(128)} %get-tuple-element.38.when, f32[96]{0:T(128)} %add_bitcast_fusion.dsum, f32[1,256]{1,0:T(1,128)} %bitcast.55, f32[256,1]{1,0:T(8,128)} %copy.93.vcol, ...), custom_call_target="tpu_custom_call" | custom-call | flops 2684354560 | bytes 12582912 | tf_op jit(solution)/shard_map/pallas_call | solution.py:133
  136.4 9.2 %collective-permute-done.13 = bf16[4,512,256]{2,1,0:T(8,128)(2,1)S(1)} collective-permute-done((bf16[4,512,256]{2,1,0:T(8,128)(2,1)}, bf16[4,512,256]{2,1,0:T(8,128)(2,1)S(1)}, u32[]{:S(2)}, u32[]{:S(2)}) %collective-permute-start.13) | collective-permute-done | bytes 1048608 | tf_op jit(solution)/shard_map/ppermute | solution.py:239
  145.9 2.0 %collective-permute-done.19 = bf16[4,512,256]{2,1,0:T(8,128)(2,1)} collective-permute-done((bf16[4,512,256]{2,1,0:T(8,128)(2,1)}, bf16[4,512,256]{2,1,0:T(8,128)(2,1)}, u32[]{:S(2)}, u32[]{:S(2)}) %collective-permute-start.19) | collective-permute-done | bytes 1048608 | tf_op jit(solution)/shard_map/ppermute | solution.py:239
  148.0 17.9 %shard_map.131 = (f32[16,256,256]{2,1,0:T(8,128)}, bf16[4,32,256,256]{3,2,1,0:T(8,128)(2,1)S(1)}, f32[16,256,256]{2,1,0:T(8,128)S(1)}) custom-call(s32[4,192]{1,0:T(4,128)S(1)} %copy-done.6, f32[128]{0:T(128)S(1)} %copy-done.10, s32[64]{0:T(128)S(1)} %copy-done.9, f32[96]{0:T(128)S(1)} %copy-done.11, ...), custom_call_target="tpu_custom_call", output_to_operand_aliasing={{1}: (11, {}), {2}: (12, {})} | custom-call | flops 10737418240 | bytes 8388608 | tf_op jit(solution)/shard_map/pallas_call | solution.py:151
  (150 shorter events, 40.2 us)
Async XLA Ops:
  3.2 35.2 %all-to-all-start = ((bf16[16,64,512]{2,1,0:T(8,128)(2,1)}), bf16[16,64,512]{2,1,0:T(8,128)(2,1)S(1)}, u32[]{:S(2)}, u32[]{:S(2)}) async-start(bf16[16,64,512]{2,1,0:T(8,128)(2,1)} %copy.80), calls=%async_computation | async-start | bytes 2097152 | tf_op jit(solution)/shard_map/all_to_all | solution.py:346
  15.8 3.6 %collective-permute-start.1 = (s32[2,176]{1,0:T(2,128)S(1)}, s32[2,176]{1,0:T(2,128)S(1)}, u32[]{:S(2)}, u32[]{:S(2)}) collective-permute-start(s32[2,176]{1,0:T(2,128)S(1)} %pad_add_fusion.4), channel_id=1, source_target_pairs={{0,12},{1,13},{2,14},{3,15},{4,8},{5,9},{6,10},{7,11},{8,4},{9,5},... | collective-permute-start | bytes 4232 | tf_op jit(solution)/shard_map/ppermute | solution.py:239
  19.5 3.6 %collective-permute-start.2 = (s32[4,176]{1,0:T(4,128)S(1)}, s32[4,176]{1,0:T(4,128)S(1)}, u32[]{:S(2)}, u32[]{:S(2)}) collective-permute-start(s32[4,176]{1,0:T(4,128)S(1)} %pad_add_fusion.3), channel_id=1, source_target_pairs={{0,1},{1,0},{2,3},{3,2},{4,5},{5,4},{6,7},{7,6},{8,9},{9,8},{10,11... | collective-permute-start | bytes 8456 | tf_op jit(solution)/shard_map/ppermute | solution.py:239
  23.2 4.9 %collective-permute-start.3 = (s32[8,176]{1,0:T(8,128)S(1)}, s32[8,176]{1,0:T(8,128)S(1)}, u32[]{:S(2)}, u32[]{:S(2)}) collective-permute-start(s32[8,176]{1,0:T(8,128)S(1)} %pad_add_fusion.2), channel_id=1, source_target_pairs={{0,3},{1,2},{2,1},{3,0},{4,7},{5,6},{6,5},{7,4},{8,11},{9,10},{10,... | collective-permute-start | bytes 16904 | tf_op jit(solution)/shard_map/ppermute | solution.py:239
  39.8 9.7 %collective-permute-start.7 = (bf16[1,512,256]{2,1,0:T(8,128)(2,1)S(1)}, bf16[1,512,256]{2,1,0:T(8,128)(2,1)S(1)}, u32[]{:S(2)}, u32[]{:S(2)}) collective-permute-start(bf16[1,512,256]{2,1,0:T(8,128)(2,1)S(1)} %get-tuple-element.69.refs_3_), channel_id=1, source_target_pairs={{0,3},{1,2},{2,1},{3,0},{4,7},{5,6},{6,5},{7,4},{8,11},{9,10},{10,... | collective-permute-start | bytes 786440 | tf_op jit(solution)/shard_map/ppermute | solution.py:239
  42.9 8.8 %collective-permute-start.6 = (bf16[1,512,256]{2,1,0:T(8,128)(2,1)S(1)}, bf16[1,512,256]{2,1,0:T(8,128)(2,1)S(1)}, u32[]{:S(2)}, u32[]{:S(2)}) collective-permute-start(bf16[1,512,256]{2,1,0:T(8,128)(2,1)S(1)} %get-tuple-element.70.refs_2_), channel_id=1, source_target_pairs={{0,12},{1,13},{2,14},{3,15},{4,8},{5,9},{6,10},{7,11},{8,4},{9,5},... | collective-permute-start | bytes 786440 | tf_op jit(solution)/shard_map/ppermute | solution.py:239
  44.4 9.0 %collective-permute-start.5 = (bf16[1,512,256]{2,1,0:T(8,128)(2,1)S(1)}, bf16[1,512,256]{2,1,0:T(8,128)(2,1)S(1)}, u32[]{:S(2)}, u32[]{:S(2)}) collective-permute-start(bf16[1,512,256]{2,1,0:T(8,128)(2,1)S(1)} %get-tuple-element.71.refs_1_), channel_id=1, source_target_pairs={{0,1},{1,0},{2,3},{3,2},{4,5},{5,4},{6,7},{7,6},{8,9},{9,8},{10,11... | collective-permute-start | bytes 786440 | tf_op jit(solution)/shard_map/ppermute | solution.py:239
  44.6 9.1 %collective-permute-start.4 = (bf16[1,512,256]{2,1,0:T(8,128)(2,1)S(1)}, bf16[1,512,256]{2,1,0:T(8,128)(2,1)S(1)}, u32[]{:S(2)}, u32[]{:S(2)}) collective-permute-start(bf16[1,512,256]{2,1,0:T(8,128)(2,1)S(1)} %get-tuple-element.72.refs_0_), channel_id=1, source_target_pairs={{0,4},{1,5},{2,6},{3,7},{4,0},{5,1},{6,2},{7,3},{8,12},{9,13},{10,... | collective-permute-start | bytes 786440 | tf_op jit(solution)/shard_map/ppermute | solution.py:239
  54.1 14.0 %collective-permute-start.8 = (bf16[2,512,256]{2,1,0:T(8,128)(2,1)S(1)}, bf16[2,512,256]{2,1,0:T(8,128)(2,1)S(1)}, u32[]{:S(2)}, u32[]{:S(2)}) collective-permute-start(bf16[2,512,256]{2,1,0:T(8,128)(2,1)S(1)} %get-tuple-element.44.refs_0_), channel_id=1, source_target_pairs={{0,12},{1,13},{2,14},{3,15},{4,8},{5,9},{6,10},{7,11},{8,4},{9,5},... | collective-permute-start | bytes 1572872 | tf_op jit(solution)/shard_map/ppermute | solution.py:239
  54.8 14.9 %collective-permute-start.9 = (bf16[2,512,256]{2,1,0:T(8,128)(2,1)S(1)}, bf16[2,512,256]{2,1,0:T(8,128)(2,1)S(1)}, u32[]{:S(2)}, u32[]{:S(2)}) collective-permute-start(bf16[2,512,256]{2,1,0:T(8,128)(2,1)S(1)} %get-tuple-element.45.refs_1_), channel_id=1, source_target_pairs={{0,3},{1,2},{2,1},{3,0},{4,7},{5,6},{6,5},{7,4},{8,11},{9,10},{10,... | collective-permute-start | bytes 1572872 | tf_op jit(solution)/shard_map/ppermute | solution.py:239
  55.8 13.9 %collective-permute-start.10 = (bf16[2,512,256]{2,1,0:T(8,128)(2,1)S(1)}, bf16[2,512,256]{2,1,0:T(8,128)(2,1)S(1)}, u32[]{:S(2)}, u32[]{:S(2)}) collective-permute-start(bf16[2,512,256]{2,1,0:T(8,128)(2,1)S(1)} %get-tuple-element.46.refs_2_), channel_id=1, source_target_pairs={{0,4},{1,5},{2,6},{3,7},{4,0},{5,1},{6,2},{7,3},{8,12},{9,13},{10,... | collective-permute-start | bytes 1572872 | tf_op jit(solution)/shard_map/ppermute | solution.py:239
  57.5 13.1 %collective-permute-start.11 = (bf16[2,512,256]{2,1,0:T(8,128)(2,1)S(1)}, bf16[2,512,256]{2,1,0:T(8,128)(2,1)}, u32[]{:S(2)}, u32[]{:S(2)}) collective-permute-start(bf16[2,512,256]{2,1,0:T(8,128)(2,1)S(1)} %get-tuple-element.47.refs_3_), channel_id=1, source_target_pairs={{0,1},{1,0},{2,3},{3,2},{4,5},{5,4},{6,7},{7,6},{8,9},{9,8},{10,11... | collective-permute-start | bytes 1572872 | tf_op jit(solution)/shard_map/ppermute | solution.py:239
  73.1 25.5 %collective-permute-start.20 = (bf16[4,512,256]{2,1,0:T(8,128)(2,1)}, bf16[4,512,256]{2,1,0:T(8,128)(2,1)S(1)}, u32[]{:S(2)}, u32[]{:S(2)}) collective-permute-start(bf16[4,512,256]{2,1,0:T(8,128)(2,1)} %get-tuple-element.52), channel_id=1, source_target_pairs={{0,3},{1,2},{2,1},{3,0},{4,7},{5,6},{6,5},{7,4},{8,11},{9,10},{10,... | collective-permute-start | bytes 3145736 | tf_op jit(solution)/shard_map/ppermute | solution.py:239
  75.9 26.4 %collective-permute-start.12 = (bf16[4,512,256]{2,1,0:T(8,128)(2,1)}, bf16[4,512,256]{2,1,0:T(8,128)(2,1)}, u32[]{:S(2)}, u32[]{:S(2)}) collective-permute-start(bf16[4,512,256]{2,1,0:T(8,128)(2,1)} %get-tuple-element.52), channel_id=1, source_target_pairs={{0,1},{1,0},{2,3},{3,2},{4,5},{5,4},{6,7},{7,6},{8,9},{9,8},{10,11... | collective-permute-start | bytes 3145736 | tf_op jit(solution)/shard_map/ppermute | solution.py:239
  76.0 28.1 %collective-permute-start.21 = (bf16[4,512,256]{2,1,0:T(8,128)(2,1)}, bf16[4,512,256]{2,1,0:T(8,128)(2,1)S(1)}, u32[]{:S(2)}, u32[]{:S(2)}) collective-permute-start(bf16[4,512,256]{2,1,0:T(8,128)(2,1)} %get-tuple-element.53), channel_id=1, source_target_pairs={{0,12},{1,13},{2,14},{3,15},{4,8},{5,9},{6,10},{7,11},{8,4},{9,5},... | collective-permute-start | bytes 3145736 | tf_op jit(solution)/shard_map/ppermute | solution.py:239
  78.2 27.5 %collective-permute-start.14 = (bf16[4,512,256]{2,1,0:T(8,128)(2,1)}, bf16[4,512,256]{2,1,0:T(8,128)(2,1)}, u32[]{:S(2)}, u32[]{:S(2)}) collective-permute-start(bf16[4,512,256]{2,1,0:T(8,128)(2,1)} %get-tuple-element.53), channel_id=1, source_target_pairs={{0,4},{1,5},{2,6},{3,7},{4,0},{5,1},{6,2},{7,3},{8,12},{9,13},{10,... | collective-permute-start | bytes 3145736 | tf_op jit(solution)/shard_map/ppermute | solution.py:239
  79.7 42.1 %collective-permute-start.22 = (bf16[4,512,256]{2,1,0:T(8,128)(2,1)}, bf16[4,512,256]{2,1,0:T(8,128)(2,1)}, u32[]{:S(2)}, u32[]{:S(2)}) collective-permute-start(bf16[4,512,256]{2,1,0:T(8,128)(2,1)} %get-tuple-element.54), channel_id=1, source_target_pairs={{0,1},{1,0},{2,3},{3,2},{4,5},{5,4},{6,7},{7,6},{8,9},{9,8},{10,11... | collective-permute-start | bytes 3145736 | tf_op jit(solution)/shard_map/ppermute | solution.py:239
  98.7 27.6 %collective-permute-start.16 = (bf16[4,512,256]{2,1,0:T(8,128)(2,1)}, bf16[4,512,256]{2,1,0:T(8,128)(2,1)}, u32[]{:S(2)}, u32[]{:S(2)}) collective-permute-start(bf16[4,512,256]{2,1,0:T(8,128)(2,1)} %get-tuple-element.54), channel_id=1, source_target_pairs={{0,3},{1,2},{2,1},{3,0},{4,7},{5,6},{6,5},{7,4},{8,11},{9,10},{10,... | collective-permute-start | bytes 3145736 | tf_op jit(solution)/shard_map/ppermute | solution.py:239
  102.3 24.0 %collective-permute-start.18 = (bf16[4,512,256]{2,1,0:T(8,128)(2,1)}, bf16[4,512,256]{2,1,0:T(8,128)(2,1)}, u32[]{:S(2)}, u32[]{:S(2)}) collective-permute-start(bf16[4,512,256]{2,1,0:T(8,128)(2,1)} %get-tuple-element.55), channel_id=1, source_target_pairs={{0,12},{1,13},{2,14},{3,15},{4,8},{5,9},{6,10},{7,11},{8,4},{9,5},... | collective-permute-start | bytes 3145736 | tf_op jit(solution)/shard_map/ppermute | solution.py:239
  104.1 25.1 %collective-permute-start.23 = (bf16[4,512,256]{2,1,0:T(8,128)(2,1)}, bf16[4,512,256]{2,1,0:T(8,128)(2,1)}, u32[]{:S(2)}, u32[]{:S(2)}) collective-permute-start(bf16[4,512,256]{2,1,0:T(8,128)(2,1)} %get-tuple-element.55), channel_id=1, source_target_pairs={{0,4},{1,5},{2,6},{3,7},{4,0},{5,1},{6,2},{7,3},{8,12},{9,13},{10,... | collective-permute-start | bytes 3145736 | tf_op jit(solution)/shard_map/ppermute | solution.py:239
  105.7 39.9 %collective-permute-start.13 = (bf16[4,512,256]{2,1,0:T(8,128)(2,1)}, bf16[4,512,256]{2,1,0:T(8,128)(2,1)S(1)}, u32[]{:S(2)}, u32[]{:S(2)}) collective-permute-start(bf16[4,512,256]{2,1,0:T(8,128)(2,1)} %collective-permute-done.12), channel_id=1, source_target_pairs={{0,3},{1,2},{2,1},{3,0},{4,7},{5,6},{6,5},{7,4},{8,11},{9,10},{10,... | collective-permute-start | bytes 3145736 | tf_op jit(solution)/shard_map/ppermute | solution.py:239
  121.9 24.0 %collective-permute-start.15 = (bf16[4,512,256]{2,1,0:T(8,128)(2,1)}, bf16[4,512,256]{2,1,0:T(8,128)(2,1)}, u32[]{:S(2)}, u32[]{:S(2)}) collective-permute-start(bf16[4,512,256]{2,1,0:T(8,128)(2,1)} %collective-permute-done.14), channel_id=1, source_target_pairs={{0,12},{1,13},{2,14},{3,15},{4,8},{5,9},{6,10},{7,11},{8,4},{9,5},... | collective-permute-start | bytes 3145736 | tf_op jit(solution)/shard_map/ppermute | solution.py:239
  126.3 19.6 %collective-permute-start.17 = (bf16[4,512,256]{2,1,0:T(8,128)(2,1)}, bf16[4,512,256]{2,1,0:T(8,128)(2,1)}, u32[]{:S(2)}, u32[]{:S(2)}) collective-permute-start(bf16[4,512,256]{2,1,0:T(8,128)(2,1)} %collective-permute-done.16), channel_id=1, source_target_pairs={{0,1},{1,0},{2,3},{3,2},{4,5},{5,4},{6,7},{7,6},{8,9},{9,8},{10,11... | collective-permute-start | bytes 3145736 | tf_op jit(solution)/shard_map/ppermute | solution.py:239
  126.3 21.6 %collective-permute-start.19 = (bf16[4,512,256]{2,1,0:T(8,128)(2,1)}, bf16[4,512,256]{2,1,0:T(8,128)(2,1)}, u32[]{:S(2)}, u32[]{:S(2)}) collective-permute-start(bf16[4,512,256]{2,1,0:T(8,128)(2,1)} %collective-permute-done.18), channel_id=1, source_target_pairs={{0,4},{1,5},{2,6},{3,7},{4,0},{5,1},{6,2},{7,3},{8,12},{9,13},{10,... | collective-permute-start | bytes 3145736 | tf_op jit(solution)/shard_map/ppermute | solution.py:239
  (26 other events, 415.8 us)

commit v9 on v8

--- a/solution.py
+++ b/solution.py
@@ -90,13 +90,6 @@
         copy.wait()
     add_coupled(idx, wts, dsum, pool, mixed, vsum, order, trips)
 
-    def received(g, carry):
-        for u in range(UNROLL):
-            s = UNROLL * g + u
-            value = (mixed[s] - product(idx, pool, 16 + s)) * recip(vsum[...] - dsum[16 + s])
-            amp[s] = value.astype(jnp.bfloat16)
-        return carry
-
     def out_copy(g):
         rows = pl.ds(UNROLL * g, UNROLL)
         return pltpu.make_async_copy(mixed.at[rows], out.at[rows], out_sems.at[g])
@@ -115,7 +108,9 @@
         out_copy(g).wait()
         return carry
 
-    lax.fori_loop(0, 16 // UNROLL, received, 0)
+    for s in range(16):
+        value = (mixed[s] - product(idx, pool, 16 + s)) * recip(vsum[...] - dsum[16 + s])
+        amp[s] = value.astype(jnp.bfloat16)
     lax.fori_loop(0, 16 // UNROLL, own, 0)
     lax.fori_loop(0, 16 // UNROLL, finish, 0)
 

time: 166 us -> 167 us (level); the launches traced: 166 us -> 165 us
  transfers between devices with their start and end apart: 25 -> 25, of which waited for: 19 -> 19; matrix products, arithmetic and copies ran while one was open for 5% -> 5% of each run, Pallas kernels for 6% -> 7%
where the time goes in v9:
time: 167 us; the launch traced here: 165 us
  waiting for transfers between devices  75 us (45%)
  starting transfers between devices  45.4 us (27%)
  Pallas kernels  30.3 us (18%)
  local copies, waits for them, and re-layouts  6.73 us (4%)
  other arithmetic  3.8 us (2%)
  matrix products  2.73 us (2%)
    ppermute x24, waiting for transfers between devices, swap(): return lax.ppermute(block, 'grp', [(g, g ^ mask) for g in range(16)])  69.5 us
    ppermute x24, starting transfers between devices, swap(): return lax.ppermute(block, 'grp', [(g, g ^ mask) for g in range(16)])  36.8 us
    pallas_call x1, Pallas kernels, amplitudes(): pl.pallas_call(last_kernel, in_specs=[SMEM] * 4 + [VMEM] * 2 + [SMEM] + [...  16.4 us
    pallas_call x1, Pallas kernels, early_sums(): pl.pallas_call(early_kernel, in_specs=[SMEM] * 4 + [VMEM] * 2 + [HBM] * 1...  8.59 us
    all_to_all x1, starting transfers between devices, on_device(): block = lax.all_to_all(rows, 'aux', split_axis=0, concat_axis=0, tiled=True)  8.57 us
    all_to_all x1, waiting for transfers between devices, on_device(): block = lax.all_to_all(rows, 'aux', split_axis=0, concat_axis=0, tiled=True)  5.51 us
    pallas_call x2, Pallas kernels, half_call(): pl.pallas_call(kernel, in_specs=[HBM] * (4 + len(staged)), out_specs=[HBM...  4.87 us
  transfers between devices with their start and end apart: 25, of which 19 were waited for; matrix products, arithmetic and copies ran while one was open for 5% of the time, Pallas kernels for 7%

profile of v9, /device:TPU:2, one launch (start us, length us, event | category | flops | bytes accessed | tf_op | source)
XLA Modules:
  0.0 164.6 jit_solution(13996900577828821452)
XLA Ops:
  3.2 8.6 %all-to-all-start = ((bf16[16,64,512]{2,1,0:T(8,128)(2,1)}), bf16[16,64,512]{2,1,0:T(8,128)(2,1)S(1)}, u32[]{:S(2)}, u32[]{:S(2)}) async-start(bf16[16,64,512]{2,1,0:T(8,128)(2,1)} %copy.80), calls=%async_computation | async-start | bytes 2097152 | tf_op jit(solution)/shard_map/all_to_all | solution.py:341
  17.5 1.9 %collective-permute-done.1 = s32[2,176]{1,0:T(2,128)S(1)} collective-permute-done((s32[2,176]{1,0:T(2,128)S(1)}, s32[2,176]{1,0:T(2,128)S(1)}, u32[]{:S(2)}, u32[]{:S(2)}) %collective-permute-start.1) | collective-permute-done | bytes 1440 | tf_op jit(solution)/shard_map/ppermute | solution.py:234
  21.2 1.9 %collective-permute-done.2 = s32[4,176]{1,0:T(4,128)S(1)} collective-permute-done((s32[4,176]{1,0:T(4,128)S(1)}, s32[4,176]{1,0:T(4,128)S(1)}, u32[]{:S(2)}, u32[]{:S(2)}) %collective-permute-start.2) | collective-permute-done | bytes 2848 | tf_op jit(solution)/shard_map/ppermute | solution.py:234
  23.2 3.0 %collective-permute-start.3 = (s32[8,176]{1,0:T(8,128)S(1)}, s32[8,176]{1,0:T(8,128)S(1)}, u32[]{:S(2)}, u32[]{:S(2)}) collective-permute-start(s32[8,176]{1,0:T(8,128)S(1)} %pad_add_fusion.2), channel_id=1, source_target_pairs={{0,3},{1,2},{2,1},{3,0},{4,7},{5,6},{6,5},{7,4},{8,11},{9,10},{10,... | collective-permute-start | bytes 16904 | tf_op jit(solution)/shard_map/ppermute | solution.py:234
  32.9 5.5 %all-to-all-done = bf16[16,64,512]{2,1,0:T(8,128)(2,1)S(1)} async-done(((bf16[16,64,512]{2,1,0:T(8,128)(2,1)}), bf16[16,64,512]{2,1,0:T(8,128)(2,1)S(1)}, u32[]{:S(2)}, u32[]{:S(2)}) %all-to-all-start) | async-done | bytes 1048608 | tf_op jit(solution)/shard_map/all_to_all | solution.py:341
  39.8 3.1 %collective-permute-start.7 = (bf16[1,512,256]{2,1,0:T(8,128)(2,1)S(1)}, bf16[1,512,256]{2,1,0:T(8,128)(2,1)S(1)}, u32[]{:S(2)}, u32[]{:S(2)}) collective-permute-start(bf16[1,512,256]{2,1,0:T(8,128)(2,1)S(1)} %get-tuple-element.69.refs_3_), channel_id=1, source_target_pairs={{0,3},{1,2},{2,1},{3,0},{4,7},{5,6},{6,5},{7,4},{8,11},{9,10},{10,... | collective-permute-start | bytes 786440 | tf_op jit(solution)/shard_map/ppermute | solution.py:234
  44.6 1.8 %collective-permute-start.4 = (bf16[1,512,256]{2,1,0:T(8,128)(2,1)S(1)}, bf16[1,512,256]{2,1,0:T(8,128)(2,1)S(1)}, u32[]{:S(2)}, u32[]{:S(2)}) collective-permute-start(bf16[1,512,256]{2,1,0:T(8,128)(2,1)S(1)} %get-tuple-element.72.refs_0_), channel_id=1, source_target_pairs={{0,4},{1,5},{2,6},{3,7},{4,0},{5,1},{6,2},{7,3},{8,12},{9,13},{10,... | collective-permute-start | bytes 786440 | tf_op jit(solution)/shard_map/ppermute | solution.py:234
  46.4 3.2 %collective-permute-done.7.refs_7_ = bf16[1,512,256]{2,1,0:T(8,128)(2,1)S(1)} collective-permute-done((bf16[1,512,256]{2,1,0:T(8,128)(2,1)S(1)}, bf16[1,512,256]{2,1,0:T(8,128)(2,1)S(1)}, u32[]{:S(2)}, u32[]{:S(2)}) %collective-permute-start.7) | collective-permute-done | bytes 262176 | tf_op jit(solution)/shard_map/ppermute | solution.py:234
  49.6 2.2 %collective-permute-done.6.refs_6_ = bf16[1,512,256]{2,1,0:T(8,128)(2,1)S(1)} collective-permute-done((bf16[1,512,256]{2,1,0:T(8,128)(2,1)S(1)}, bf16[1,512,256]{2,1,0:T(8,128)(2,1)S(1)}, u32[]{:S(2)}, u32[]{:S(2)}) %collective-permute-start.6) | collective-permute-done | bytes 262176 | tf_op jit(solution)/shard_map/ppermute | solution.py:234
  58.4 2.4 %shard_map.128 = (bf16[4,512,256]{2,1,0:T(8,128)(2,1)}, bf16[4,512,256]{2,1,0:T(8,128)(2,1)}, bf16[4,512,256]{2,1,0:T(8,128)(2,1)}, bf16[4,512,256]{2,1,0:T(8,128)(2,1)}) custom-call(bf16[2,512,256]{2,1,0:T(8,128)(2,1)} %copy-done.5, bf16[2,512,256]{2,1,0:T(8,128)(2,1)} %copy-done.4, bf16[2,512,256]{2,1,0:T(8,128)(2,1)} %copy-done.3, ...), custom_call_target="tpu_custom_call" | custom-call | bytes 4194304 | tf_op jit(solution)/shard_map/pallas_call | solution.py:314
  60.8 7.4 %collective-permute-done.8.refs_0_ = bf16[2,512,256]{2,1,0:T(8,128)(2,1)S(1)} collective-permute-done((bf16[2,512,256]{2,1,0:T(8,128)(2,1)S(1)}, bf16[2,512,256]{2,1,0:T(8,128)(2,1)S(1)}, u32[]{:S(2)}, u32[]{:S(2)}) %collective-permute-start.8) | collective-permute-done | bytes 524320 | tf_op jit(solution)/shard_map/ppermute | solution.py:234
  70.7 2.5 %shard_map.129 = (bf16[4,512,256]{2,1,0:T(8,128)(2,1)}, bf16[4,512,256]{2,1,0:T(8,128)(2,1)}, bf16[4,512,256]{2,1,0:T(8,128)(2,1)}, bf16[4,512,256]{2,1,0:T(8,128)(2,1)}) custom-call(bf16[2,512,256]{2,1,0:T(8,128)(2,1)} %copy-done.14, bf16[2,512,256]{2,1,0:T(8,128)(2,1)} %copy-done.15, ...), custom_call_target="tpu_custom_call", output_to_operand_aliasing={{0}: (4, {}), {1}: (5, {}), {2}: (6, {}), {3}: (7, {})} | custom-call | bytes 4194304 | tf_op jit(solution)/shard_map/pallas_call | solution.py:314
  73.1 2.8 %collective-permute-start.20 = (bf16[4,512,256]{2,1,0:T(8,128)(2,1)}, bf16[4,512,256]{2,1,0:T(8,128)(2,1)S(1)}, u32[]{:S(2)}, u32[]{:S(2)}) collective-permute-start(bf16[4,512,256]{2,1,0:T(8,128)(2,1)} %get-tuple-element.52), channel_id=1, source_target_pairs={{0,3},{1,2},{2,1},{3,0},{4,7},{5,6},{6,5},{7,4},{8,11},{9,10},{10,... | collective-permute-start | bytes 3145736 | tf_op jit(solution)/shard_map/ppermute | solution.py:234
  76.0 2.1 %collective-permute-start.21 = (bf16[4,512,256]{2,1,0:T(8,128)(2,1)}, bf16[4,512,256]{2,1,0:T(8,128)(2,1)S(1)}, u32[]{:S(2)}, u32[]{:S(2)}) collective-permute-start(bf16[4,512,256]{2,1,0:T(8,128)(2,1)} %get-tuple-element.53), channel_id=1, source_target_pairs={{0,12},{1,13},{2,14},{3,15},{4,8},{5,9},{6,10},{7,11},{8,4},{9,5},... | collective-permute-start | bytes 3145736 | tf_op jit(solution)/shard_map/ppermute | solution.py:234
  81.3 17.3 %collective-permute-done.20 = bf16[4,512,256]{2,1,0:T(8,128)(2,1)S(1)} collective-permute-done((bf16[4,512,256]{2,1,0:T(8,128)(2,1)}, bf16[4,512,256]{2,1,0:T(8,128)(2,1)S(1)}, u32[]{:S(2)}, u32[]{:S(2)}) %collective-permute-start.20) | collective-permute-done | bytes 1048608 | tf_op jit(solution)/shard_map/ppermute | solution.py:234
  98.7 2.1 %collective-permute-start.16 = (bf16[4,512,256]{2,1,0:T(8,128)(2,1)}, bf16[4,512,256]{2,1,0:T(8,128)(2,1)}, u32[]{:S(2)}, u32[]{:S(2)}) collective-permute-start(bf16[4,512,256]{2,1,0:T(8,128)(2,1)} %get-tuple-element.54), channel_id=1, source_target_pairs={{0,3},{1,2},{2,1},{3,0},{4,7},{5,6},{6,5},{7,4},{8,11},{9,10},{10,... | collective-permute-start | bytes 3145736 | tf_op jit(solution)/shard_map/ppermute | solution.py:234
  102.3 1.8 %collective-permute-start.18 = (bf16[4,512,256]{2,1,0:T(8,128)(2,1)}, bf16[4,512,256]{2,1,0:T(8,128)(2,1)}, u32[]{:S(2)}, u32[]{:S(2)}) collective-permute-start(bf16[4,512,256]{2,1,0:T(8,128)(2,1)} %get-tuple-element.55), channel_id=1, source_target_pairs={{0,12},{1,13},{2,14},{3,15},{4,8},{5,9},{6,10},{7,11},{8,4},{9,5},... | collective-permute-start | bytes 3145736 | tf_op jit(solution)/shard_map/ppermute | solution.py:234
  107.5 14.4 %collective-permute-done.22 = bf16[4,512,256]{2,1,0:T(8,128)(2,1)} collective-permute-done((bf16[4,512,256]{2,1,0:T(8,128)(2,1)}, bf16[4,512,256]{2,1,0:T(8,128)(2,1)}, u32[]{:S(2)}, u32[]{:S(2)}) %collective-permute-start.22) | collective-permute-done | bytes 1048608 | tf_op jit(solution)/shard_map/ppermute | solution.py:234
  123.7 2.6 %collective-permute-done.16 = bf16[4,512,256]{2,1,0:T(8,128)(2,1)} collective-permute-done((bf16[4,512,256]{2,1,0:T(8,128)(2,1)}, bf16[4,512,256]{2,1,0:T(8,128)(2,1)}, u32[]{:S(2)}, u32[]{:S(2)}) %collective-permute-start.16) | collective-permute-done | bytes 1048608 | tf_op jit(solution)/shard_map/ppermute | solution.py:234
  126.3 2.1 %collective-permute-start.19 = (bf16[4,512,256]{2,1,0:T(8,128)(2,1)}, bf16[4,512,256]{2,1,0:T(8,128)(2,1)}, u32[]{:S(2)}, u32[]{:S(2)}) collective-permute-start(bf16[4,512,256]{2,1,0:T(8,128)(2,1)} %collective-permute-done.18), channel_id=1, source_target_pairs={{0,4},{1,5},{2,6},{3,7},{4,0},{5,1},{6,2},{7,3},{8,12},{9,13},{10,... | collective-permute-start | bytes 3145736 | tf_op jit(solution)/shard_map/ppermute | solution.py:234
  129.3 8.6 %shard_map.130 = (bf16[4,32,256,256]{3,2,1,0:T(8,128)(2,1)S(1)}, f32[16,256,256]{2,1,0:T(8,128)S(1)}) custom-call(s32[4,192]{1,0:T(4,128)} %fusion.5.idx, f32[128]{0:T(128)} %pad_maximum_fusion.wts, s32[64]{0:T(128)} %get-tuple-element.38.when, f32[96]{0:T(128)} %add_bitcast_fusion.dsum, f32[1,256]{1,0:T(1,128)} %bitcast.55, f32[256,1]{1,0:T(8,128)} %copy.93.vcol, ...), custom_call_target="tpu_custom_call" | custom-call | flops 2684354560 | bytes 12582912 | tf_op jit(solution)/shard_map/pallas_call | solution.py:128
  137.9 7.8 %collective-permute-done.13 = bf16[4,512,256]{2,1,0:T(8,128)(2,1)S(1)} collective-permute-done((bf16[4,512,256]{2,1,0:T(8,128)(2,1)}, bf16[4,512,256]{2,1,0:T(8,128)(2,1)S(1)}, u32[]{:S(2)}, u32[]{:S(2)}) %collective-permute-start.13) | collective-permute-done | bytes 1048608 | tf_op jit(solution)/shard_map/ppermute | solution.py:234
  145.9 2.0 %collective-permute-done.19 = bf16[4,512,256]{2,1,0:T(8,128)(2,1)} collective-permute-done((bf16[4,512,256]{2,1,0:T(8,128)(2,1)}, bf16[4,512,256]{2,1,0:T(8,128)(2,1)}, u32[]{:S(2)}, u32[]{:S(2)}) %collective-permute-start.19) | collective-permute-done | bytes 1048608 | tf_op jit(solution)/shard_map/ppermute | solution.py:234
  148.0 16.4 %shard_map.131 = (f32[16,256,256]{2,1,0:T(8,128)}, bf16[4,32,256,256]{3,2,1,0:T(8,128)(2,1)S(1)}, f32[16,256,256]{2,1,0:T(8,128)S(1)}) custom-call(s32[4,192]{1,0:T(4,128)S(1)} %copy-done.6, f32[128]{0:T(128)S(1)} %copy-done.10, s32[64]{0:T(128)S(1)} %copy-done.9, f32[96]{0:T(128)S(1)} %copy-done.11, ...), custom_call_target="tpu_custom_call", output_to_operand_aliasing={{1}: (11, {}), {2}: (12, {})} | custom-call | flops 10737418240 | bytes 8388608 | tf_op jit(solution)/shard_map/pallas_call | solution.py:146
  (150 shorter events, 40.2 us)
Async XLA Ops:
  3.2 35.2 %all-to-all-start = ((bf16[16,64,512]{2,1,0:T(8,128)(2,1)}), bf16[16,64,512]{2,1,0:T(8,128)(2,1)S(1)}, u32[]{:S(2)}, u32[]{:S(2)}) async-start(bf16[16,64,512]{2,1,0:T(8,128)(2,1)} %copy.80), calls=%async_computation | async-start | bytes 2097152 | tf_op jit(solution)/shard_map/all_to_all | solution.py:341
  15.8 3.6 %collective-permute-start.1 = (s32[2,176]{1,0:T(2,128)S(1)}, s32[2,176]{1,0:T(2,128)S(1)}, u32[]{:S(2)}, u32[]{:S(2)}) collective-permute-start(s32[2,176]{1,0:T(2,128)S(1)} %pad_add_fusion.4), channel_id=1, source_target_pairs={{0,12},{1,13},{2,14},{3,15},{4,8},{5,9},{6,10},{7,11},{8,4},{9,5},... | collective-permute-start | bytes 4232 | tf_op jit(solution)/shard_map/ppermute | solution.py:234
  19.5 3.6 %collective-permute-start.2 = (s32[4,176]{1,0:T(4,128)S(1)}, s32[4,176]{1,0:T(4,128)S(1)}, u32[]{:S(2)}, u32[]{:S(2)}) collective-permute-start(s32[4,176]{1,0:T(4,128)S(1)} %pad_add_fusion.3), channel_id=1, source_target_pairs={{0,1},{1,0},{2,3},{3,2},{4,5},{5,4},{6,7},{7,6},{8,9},{9,8},{10,11... | collective-permute-start | bytes 8456 | tf_op jit(solution)/shard_map/ppermute | solution.py:234
  23.2 4.9 %collective-permute-start.3 = (s32[8,176]{1,0:T(8,128)S(1)}, s32[8,176]{1,0:T(8,128)S(1)}, u32[]{:S(2)}, u32[]{:S(2)}) collective-permute-start(s32[8,176]{1,0:T(8,128)S(1)} %pad_add_fusion.2), channel_id=1, source_target_pairs={{0,3},{1,2},{2,1},{3,0},{4,7},{5,6},{6,5},{7,4},{8,11},{9,10},{10,... | collective-permute-start | bytes 16904 | tf_op jit(solution)/shard_map/ppermute | solution.py:234
  39.8 9.7 %collective-permute-start.7 = (bf16[1,512,256]{2,1,0:T(8,128)(2,1)S(1)}, bf16[1,512,256]{2,1,0:T(8,128)(2,1)S(1)}, u32[]{:S(2)}, u32[]{:S(2)}) collective-permute-start(bf16[1,512,256]{2,1,0:T(8,128)(2,1)S(1)} %get-tuple-element.69.refs_3_), channel_id=1, source_target_pairs={{0,3},{1,2},{2,1},{3,0},{4,7},{5,6},{6,5},{7,4},{8,11},{9,10},{10,... | collective-permute-start | bytes 786440 | tf_op jit(solution)/shard_map/ppermute | solution.py:234
  42.9 8.8 %collective-permute-start.6 = (bf16[1,512,256]{2,1,0:T(8,128)(2,1)S(1)}, bf16[1,512,256]{2,1,0:T(8,128)(2,1)S(1)}, u32[]{:S(2)}, u32[]{:S(2)}) collective-permute-start(bf16[1,512,256]{2,1,0:T(8,128)(2,1)S(1)} %get-tuple-element.70.refs_2_), channel_id=1, source_target_pairs={{0,12},{1,13},{2,14},{3,15},{4,8},{5,9},{6,10},{7,11},{8,4},{9,5},... | collective-permute-start | bytes 786440 | tf_op jit(solution)/shard_map/ppermute | solution.py:234
  44.4 9.0 %collective-permute-start.5 = (bf16[1,512,256]{2,1,0:T(8,128)(2,1)S(1)}, bf16[1,512,256]{2,1,0:T(8,128)(2,1)S(1)}, u32[]{:S(2)}, u32[]{:S(2)}) collective-permute-start(bf16[1,512,256]{2,1,0:T(8,128)(2,1)S(1)} %get-tuple-element.71.refs_1_), channel_id=1, source_target_pairs={{0,1},{1,0},{2,3},{3,2},{4,5},{5,4},{6,7},{7,6},{8,9},{9,8},{10,11... | collective-permute-start | bytes 786440 | tf_op jit(solution)/shard_map/ppermute | solution.py:234
  44.6 9.1 %collective-permute-start.4 = (bf16[1,512,256]{2,1,0:T(8,128)(2,1)S(1)}, bf16[1,512,256]{2,1,0:T(8,128)(2,1)S(1)}, u32[]{:S(2)}, u32[]{:S(2)}) collective-permute-start(bf16[1,512,256]{2,1,0:T(8,128)(2,1)S(1)} %get-tuple-element.72.refs_0_), channel_id=1, source_target_pairs={{0,4},{1,5},{2,6},{3,7},{4,0},{5,1},{6,2},{7,3},{8,12},{9,13},{10,... | collective-permute-start | bytes 786440 | tf_op jit(solution)/shard_map/ppermute | solution.py:234
  54.1 14.0 %collective-permute-start.8 = (bf16[2,512,256]{2,1,0:T(8,128)(2,1)S(1)}, bf16[2,512,256]{2,1,0:T(8,128)(2,1)S(1)}, u32[]{:S(2)}, u32[]{:S(2)}) collective-permute-start(bf16[2,512,256]{2,1,0:T(8,128)(2,1)S(1)} %get-tuple-element.44.refs_0_), channel_id=1, source_target_pairs={{0,12},{1,13},{2,14},{3,15},{4,8},{5,9},{6,10},{7,11},{8,4},{9,5},... | collective-permute-start | bytes 1572872 | tf_op jit(solution)/shard_map/ppermute | solution.py:234
  54.8 14.9 %collective-permute-start.9 = (bf16[2,512,256]{2,1,0:T(8,128)(2,1)S(1)}, bf16[2,512,256]{2,1,0:T(8,128)(2,1)S(1)}, u32[]{:S(2)}, u32[]{:S(2)}) collective-permute-start(bf16[2,512,256]{2,1,0:T(8,128)(2,1)S(1)} %get-tuple-element.45.refs_1_), channel_id=1, source_target_pairs={{0,3},{1,2},{2,1},{3,0},{4,7},{5,6},{6,5},{7,4},{8,11},{9,10},{10,... | collective-permute-start | bytes 1572872 | tf_op jit(solution)/shard_map/ppermute | solution.py:234
  55.8 13.9 %collective-permute-start.10 = (bf16[2,512,256]{2,1,0:T(8,128)(2,1)S(1)}, bf16[2,512,256]{2,1,0:T(8,128)(2,1)S(1)}, u32[]{:S(2)}, u32[]{:S(2)}) collective-permute-start(bf16[2,512,256]{2,1,0:T(8,128)(2,1)S(1)} %get-tuple-element.46.refs_2_), channel_id=1, source_target_pairs={{0,4},{1,5},{2,6},{3,7},{4,0},{5,1},{6,2},{7,3},{8,12},{9,13},{10,... | collective-permute-start | bytes 1572872 | tf_op jit(solution)/shard_map/ppermute | solution.py:234
  57.5 13.1 %collective-permute-start.11 = (bf16[2,512,256]{2,1,0:T(8,128)(2,1)S(1)}, bf16[2,512,256]{2,1,0:T(8,128)(2,1)}, u32[]{:S(2)}, u32[]{:S(2)}) collective-permute-start(bf16[2,512,256]{2,1,0:T(8,128)(2,1)S(1)} %get-tuple-element.47.refs_3_), channel_id=1, source_target_pairs={{0,1},{1,0},{2,3},{3,2},{4,5},{5,4},{6,7},{7,6},{8,9},{9,8},{10,11... | collective-permute-start | bytes 1572872 | tf_op jit(solution)/shard_map/ppermute | solution.py:234
  73.1 25.5 %collective-permute-start.20 = (bf16[4,512,256]{2,1,0:T(8,128)(2,1)}, bf16[4,512,256]{2,1,0:T(8,128)(2,1)S(1)}, u32[]{:S(2)}, u32[]{:S(2)}) collective-permute-start(bf16[4,512,256]{2,1,0:T(8,128)(2,1)} %get-tuple-element.52), channel_id=1, source_target_pairs={{0,3},{1,2},{2,1},{3,0},{4,7},{5,6},{6,5},{7,4},{8,11},{9,10},{10,... | collective-permute-start | bytes 3145736 | tf_op jit(solution)/shard_map/ppermute | solution.py:234
  75.9 26.4 %collective-permute-start.12 = (bf16[4,512,256]{2,1,0:T(8,128)(2,1)}, bf16[4,512,256]{2,1,0:T(8,128)(2,1)}, u32[]{:S(2)}, u32[]{:S(2)}) collective-permute-start(bf16[4,512,256]{2,1,0:T(8,128)(2,1)} %get-tuple-element.52), channel_id=1, source_target_pairs={{0,1},{1,0},{2,3},{3,2},{4,5},{5,4},{6,7},{7,6},{8,9},{9,8},{10,11... | collective-permute-start | bytes 3145736 | tf_op jit(solution)/shard_map/ppermute | solution.py:234
  76.0 28.1 %collective-permute-start.21 = (bf16[4,512,256]{2,1,0:T(8,128)(2,1)}, bf16[4,512,256]{2,1,0:T(8,128)(2,1)S(1)}, u32[]{:S(2)}, u32[]{:S(2)}) collective-permute-start(bf16[4,512,256]{2,1,0:T(8,128)(2,1)} %get-tuple-element.53), channel_id=1, source_target_pairs={{0,12},{1,13},{2,14},{3,15},{4,8},{5,9},{6,10},{7,11},{8,4},{9,5},... | collective-permute-start | bytes 3145736 | tf_op jit(solution)/shard_map/ppermute | solution.py:234
  78.2 27.5 %collective-permute-start.14 = (bf16[4,512,256]{2,1,0:T(8,128)(2,1)}, bf16[4,512,256]{2,1,0:T(8,128)(2,1)}, u32[]{:S(2)}, u32[]{:S(2)}) collective-permute-start(bf16[4,512,256]{2,1,0:T(8,128)(2,1)} %get-tuple-element.53), channel_id=1, source_target_pairs={{0,4},{1,5},{2,6},{3,7},{4,0},{5,1},{6,2},{7,3},{8,12},{9,13},{10,... | collective-permute-start | bytes 3145736 | tf_op jit(solution)/shard_map/ppermute | solution.py:234
  79.7 42.1 %collective-permute-start.22 = (bf16[4,512,256]{2,1,0:T(8,128)(2,1)}, bf16[4,512,256]{2,1,0:T(8,128)(2,1)}, u32[]{:S(2)}, u32[]{:S(2)}) collective-permute-start(bf16[4,512,256]{2,1,0:T(8,128)(2,1)} %get-tuple-element.54), channel_id=1, source_target_pairs={{0,1},{1,0},{2,3},{3,2},{4,5},{5,4},{6,7},{7,6},{8,9},{9,8},{10,11... | collective-permute-start | bytes 3145736 | tf_op jit(solution)/shard_map/ppermute | solution.py:234
  98.7 27.6 %collective-permute-start.16 = (bf16[4,512,256]{2,1,0:T(8,128)(2,1)}, bf16[4,512,256]{2,1,0:T(8,128)(2,1)}, u32[]{:S(2)}, u32[]{:S(2)}) collective-permute-start(bf16[4,512,256]{2,1,0:T(8,128)(2,1)} %get-tuple-element.54), channel_id=1, source_target_pairs={{0,3},{1,2},{2,1},{3,0},{4,7},{5,6},{6,5},{7,4},{8,11},{9,10},{10,... | collective-permute-start | bytes 3145736 | tf_op jit(solution)/shard_map/ppermute | solution.py:234
  102.3 24.0 %collective-permute-start.18 = (bf16[4,512,256]{2,1,0:T(8,128)(2,1)}, bf16[4,512,256]{2,1,0:T(8,128)(2,1)}, u32[]{:S(2)}, u32[]{:S(2)}) collective-permute-start(bf16[4,512,256]{2,1,0:T(8,128)(2,1)} %get-tuple-element.55), channel_id=1, source_target_pairs={{0,12},{1,13},{2,14},{3,15},{4,8},{5,9},{6,10},{7,11},{8,4},{9,5},... | collective-permute-start | bytes 3145736 | tf_op jit(solution)/shard_map/ppermute | solution.py:234
  104.1 25.1 %collective-permute-start.23 = (bf16[4,512,256]{2,1,0:T(8,128)(2,1)}, bf16[4,512,256]{2,1,0:T(8,128)(2,1)}, u32[]{:S(2)}, u32[]{:S(2)}) collective-permute-start(bf16[4,512,256]{2,1,0:T(8,128)(2,1)} %get-tuple-element.55), channel_id=1, source_target_pairs={{0,4},{1,5},{2,6},{3,7},{4,0},{5,1},{6,2},{7,3},{8,12},{9,13},{10,... | collective-permute-start | bytes 3145736 | tf_op jit(solution)/shard_map/ppermute | solution.py:234
  105.7 39.9 %collective-permute-start.13 = (bf16[4,512,256]{2,1,0:T(8,128)(2,1)}, bf16[4,512,256]{2,1,0:T(8,128)(2,1)S(1)}, u32[]{:S(2)}, u32[]{:S(2)}) collective-permute-start(bf16[4,512,256]{2,1,0:T(8,128)(2,1)} %collective-permute-done.12), channel_id=1, source_target_pairs={{0,3},{1,2},{2,1},{3,0},{4,7},{5,6},{6,5},{7,4},{8,11},{9,10},{10,... | collective-permute-start | bytes 3145736 | tf_op jit(solution)/shard_map/ppermute | solution.py:234
  121.9 24.0 %collective-permute-start.15 = (bf16[4,512,256]{2,1,0:T(8,128)(2,1)}, bf16[4,512,256]{2,1,0:T(8,128)(2,1)}, u32[]{:S(2)}, u32[]{:S(2)}) collective-permute-start(bf16[4,512,256]{2,1,0:T(8,128)(2,1)} %collective-permute-done.14), channel_id=1, source_target_pairs={{0,12},{1,13},{2,14},{3,15},{4,8},{5,9},{6,10},{7,11},{8,4},{9,5},... | collective-permute-start | bytes 3145736 | tf_op jit(solution)/shard_map/ppermute | solution.py:234
  126.3 19.6 %collective-permute-start.17 = (bf16[4,512,256]{2,1,0:T(8,128)(2,1)}, bf16[4,512,256]{2,1,0:T(8,128)(2,1)}, u32[]{:S(2)}, u32[]{:S(2)}) collective-permute-start(bf16[4,512,256]{2,1,0:T(8,128)(2,1)} %collective-permute-done.16), channel_id=1, source_target_pairs={{0,1},{1,0},{2,3},{3,2},{4,5},{5,4},{6,7},{7,6},{8,9},{9,8},{10,11... | collective-permute-start | bytes 3145736 | tf_op jit(solution)/shard_map/ppermute | solution.py:234
  126.3 21.6 %collective-permute-start.19 = (bf16[4,512,256]{2,1,0:T(8,128)(2,1)}, bf16[4,512,256]{2,1,0:T(8,128)(2,1)}, u32[]{:S(2)}, u32[]{:S(2)}) collective-permute-start(bf16[4,512,256]{2,1,0:T(8,128)(2,1)} %collective-permute-done.18), channel_id=1, source_target_pairs={{0,4},{1,5},{2,6},{3,7},{4,0},{5,1},{6,2},{7,3},{8,12},{9,13},{10,... | collective-permute-start | bytes 3145736 | tf_op jit(solution)/shard_map/ppermute | solution.py:234
  (26 other events, 415.8 us)
